TPU v7x, 128 devices: a whole 4x4x4 slice. The times are simulated.
128 devices in a mesh: section: 2 (over z_hi), rep: 4 (over x), shard: 16 (over y, z_lo, core).
Axes of the slice: x: 4, y: 4, z: 4 (z_hi: 2, z_lo: 2; z = z_hi * 2 + z_lo), core: 2. Of those that a mesh axis runs over, the one named last changes fastest.
Arguments:
- inputs: bfloat16 [2, 4, 1024, 1024], P(None, 'rep', 'shard'), may hold values from -6 to 6
- cotangent: bfloat16 [2, 4, 1024, 1024], P(None, 'rep', 'shard'), may hold values from -6 to 6
- norm_in: bfloat16 [2, 1024], P('section', 'shard'), may hold values from 0.5 to 1.5
- w_in: bfloat16 [2, 1024, 3352], P('section', 'shard'), may hold values from -0.1875 to 0.1875
- conv_w: bfloat16 [2, 4, 1792], P('section', None, 'shard'), may hold values from -0.5 to 0.5
- conv_b: bfloat16 [2, 1792], P('section', 'shard'), may hold values from -0.29882812 to 0.29882812
- dt_bias: float32 [2, 24], P('section'), may hold values from -6 to -2
- a_log: float32 [2, 24], P('section'), may hold values from -1 to 2
- skip_gain: float32 [2, 24], P('section'), may hold values from 0.5 to 1.5
- norm_ssm: bfloat16 [2, 1536], P('section', 'shard'), may hold values from 0.5 to 1.5
- w_out: bfloat16 [2, 1536, 1024], P('section', 'shard'), may hold values from -0.15625 to 0.15625
- query_weight: bfloat16 [2, 1024, 512], P('section', 'shard'), may hold values from -0.1875 to 0.1875
- key_weight: bfloat16 [2, 1024, 128], P('section', 'shard'), may hold values from -0.1875 to 0.1875
- value_weight: bfloat16 [2, 1024, 128], P('section', 'shard'), may hold values from -0.1875 to 0.1875
- output_weight: bfloat16 [2, 512, 1024], P('section', 'shard'), may hold values from -0.75 to 0.75
- norm_mid: bfloat16 [2, 1024], P('section', 'shard'), may hold values from 0.5 to 1.5
- w_gate: bfloat16 [2, 1024, 2048], P('section', 'shard'), may hold values from -0.1875 to 0.1875
- w_up: bfloat16 [2, 1024, 2048], P('section', 'shard'), may hold values from -0.1875 to 0.1875
- w_down: bfloat16 [2, 2048, 1024], P('section', 'shard'), may hold values from -0.125 to 0.125
Outputs:
- section_out: bfloat16 [2, 2, 4, 1024, 1024], P('section', None, 'rep', 'shard')
- input_grad: float32 [2, 2, 4, 1024, 1024], P('section', None, 'rep', 'shard')
- grad_norm_in: float32 [2, 1024], P('section', 'shard')
- grad_w_in: float32 [2, 1024, 3352], P('section', 'shard')
- grad_conv_w: float32 [2, 4, 1792], P('section', None, 'shard')
- grad_conv_b: float32 [2, 1792], P('section', 'shard')
- grad_dt_bias: float32 [2, 24], P('section')
- grad_a_log: float32 [2, 24], P('section')
- grad_skip: float32 [2, 24], P('section')
- grad_norm_ssm: float32 [2, 1536], P('section', 'shard')
- grad_w_out: float32 [2, 1536, 1024], P('section', 'shard')
- grad_w_q: float32 [2, 1024, 512], P('section', 'shard')
- grad_w_k: float32 [2, 1024, 128], P('section', 'shard')
- grad_w_v: float32 [2, 1024, 128], P('section', 'shard')
- grad_w_o: float32 [2, 512, 1024], P('section', 'shard')
- grad_norm_mid: float32 [2, 1024], P('section', 'shard')
- grad_w_gate: float32 [2, 1024, 2048], P('section', 'shard')
- grad_w_up: float32 [2, 1024, 2048], P('section', 'shard')
- grad_w_down: float32 [2, 2048, 1024], P('section', 'shard')
All inputs are finite; a program needn't handle non-finite values.
Results may differ from a plain program's by a relative error of at most 0.03.
Values may be sent and summed in bfloat16 or wider, within the bound.
No kernel may reach another device: no remote copies, remote signals or barrier semaphores. Data moves between devices by JAX's collectives and lax.ppermute only.
A program may use at most 256 MiB of HBM per device.

v0:
```python
import jax
import jax.numpy as jnp
from jax import lax
from jax.sharding import PartitionSpec as P

MODEL_WIDTH = 1024
NH = 24
HD = 64
NS = 128
QUERY_HEADS = 8
KEY_VALUE_HEADS = 2
ATTN_HEAD_SIZE = 64
CONV = 4
MB = 2


EPSILON = 1e-05


def passed_along(block, axis, distance):
    devices = range(lax.axis_size(axis))
    route = [(i - distance, i) for i in devices if i - distance in devices]
    return lax.ppermute(block, axis, route)


def prefix(x, axis, join, neutral):
    place = lax.axis_index(axis)
    gathered = jax.tree.map(
        lambda a, kind: lax.all_gather(a.astype(kind), axis), x, (jnp.bfloat16, jnp.bfloat16)
    )
    state = jax.tree.map(lambda a, e: jnp.zeros_like(a) + jnp.asarray(e, a.dtype), x, neutral)

    def one(step, state):
        return join(
            state,
            jax.tree.map(
                lambda a, own: lax.dynamic_index_in_dim(a, step, 0, False).astype(own.dtype),
                gathered,
                x,
            ),
        )

    return lax.fori_loop(0, place, one, state)


def prefix_2(x, axis, join, neutral):
    count = lax.axis_size(axis)
    place = lax.axis_index(axis)
    ahead = count - 1 - place
    gathered = jax.tree.map(
        lambda a, kind: lax.all_gather(a.astype(kind), axis),
        x,
        jax.tree.map(lambda a: jnp.bfloat16 if a.dtype == jnp.float32 else a.dtype, x),
    )
    state = jax.tree.map(lambda a, e: jnp.zeros_like(a) + jnp.asarray(e, a.dtype), x, neutral)

    def one(step, state):
        source = count - 1 - step
        return join(
            state,
            jax.tree.map(
                lambda a, own: lax.dynamic_index_in_dim(a, source, 0, False).astype(own.dtype),
                gathered,
                x,
            ),
        )

    return lax.fori_loop(0, ahead, one, state)


def dot_plain(former, latter):
    return jnp.dot(former, latter, preferred_element_type=jnp.float32)


def dot_rows(former, latter):
    return lax.dot_general(
        former, latter, (((0,), (0,)), ((), ())), preferred_element_type=jnp.float32
    )


def product_backward(former, latter):
    return lax.dot_general(
        former, latter, (((1,), (1,)), ((), ())), preferred_element_type=jnp.float32
    )


def rms_scale(values, norm_gain):
    return (
        values * lax.rsqrt(jnp.mean(values * values, axis=-1, keepdims=True) + EPSILON) * norm_gain
    )


def swiglu(gate_val, up_val):
    return jax.nn.silu(gate_val) * up_val


def combine_state(earlier, later):
    return (earlier[0] * later[0], later[0][:, None, None] * earlier[1] + later[1])


def choose(flag, former, latter):
    return jax.tree.map(
        lambda first_leaf, second_leaf: jnp.where(flag, first_leaf, second_leaf), former, latter
    )


def mixer_inputs(extended, dt_raw, conv_weight, conv_bias, dt_shift, log_rate):
    sequence_length = extended.shape[0] - (CONV - 1)
    inner_width = NH * HD
    convolved = conv_bias[None, :] + sum(
        (
            conv_weight[shift_index][None, :]
            * extended[shift_index : shift_index + sequence_length]
            for shift_index in range(CONV)
        )
    )
    activated = jax.nn.silu(convolved)
    states_in = activated[:, :inner_width].reshape(sequence_length, NH, HD)
    input_map = activated[:, inner_width : inner_width + NS]
    output_map = activated[:, inner_width + NS :]
    step_size = jax.nn.softplus(dt_raw + dt_shift[None, :])
    log_decay = -step_size * jnp.exp(log_rate)[None, :]
    return (states_in, input_map, output_map, step_size, log_decay)


def mixer_state(extended, dt_raw, conv_weight, conv_bias, dt_shift, log_rate):
    states_in, input_map, output_map, step_size, log_decay = mixer_inputs(
        extended, dt_raw, conv_weight, conv_bias, dt_shift, log_rate
    )
    cumulative = jnp.cumsum(log_decay, axis=0)
    weights_tail = jnp.exp(cumulative[-1][None, :] - cumulative) * step_size
    state_end = jnp.einsum(
        "sh,shd,sn->hdn", weights_tail, states_in, input_map, precision=lax.Precision.HIGHEST
    )
    return (state_end, jnp.exp(cumulative[-1]))


def mixer_output(
    extended,
    gate_raw,
    dt_raw,
    conv_weight,
    conv_bias,
    dt_shift,
    log_rate,
    skip_gain,
    norm_gain,
    start_state,
):
    states_in, input_map, output_map, step_size, log_decay = mixer_inputs(
        extended, dt_raw, conv_weight, conv_bias, dt_shift, log_rate
    )
    sequence_length = states_in.shape[0]
    cumulative = jnp.cumsum(log_decay, axis=0)
    from_start = (
        jnp.einsum("tn,hdn->thd", output_map, start_state, precision=lax.Precision.HIGHEST)
        * jnp.exp(cumulative)[:, :, None]
    )
    rows_index = lax.broadcasted_iota(jnp.int32, (sequence_length, sequence_length), 0)
    cols_index = lax.broadcasted_iota(jnp.int32, (sequence_length, sequence_length), 1)
    causal = (cols_index <= rows_index)[:, :, None]
    spread = jnp.where(causal, cumulative[:, None, :] - cumulative[None, :, :], 0.0)
    within = jnp.where(causal, jnp.exp(spread), 0.0)
    coupling = jnp.dot(output_map, input_map.T, precision=lax.Precision.HIGHEST)
    mixing = within * coupling[:, :, None] * step_size[None, :, :]
    local_part = jnp.einsum("tsh,shd->thd", mixing, states_in, precision=lax.Precision.HIGHEST)
    mixed_out = from_start + local_part + skip_gain[None, :, None] * states_in
    gated = mixed_out.reshape(sequence_length, NH * HD) * jax.nn.silu(gate_raw)
    return rms_scale(gated, norm_gain)


def attend(query_half_precision, gathered_keys, gathered_values, offset):
    sequence_length = query_half_precision.shape[0]
    key_total_count = gathered_keys.shape[0]
    query_groups = QUERY_HEADS // KEY_VALUE_HEADS
    query_head_count = query_half_precision.reshape(
        sequence_length, KEY_VALUE_HEADS, query_groups, ATTN_HEAD_SIZE
    )
    key_head_count = gathered_keys.reshape(key_total_count, KEY_VALUE_HEADS, ATTN_HEAD_SIZE)
    value_head_count = gathered_values.reshape(key_total_count, KEY_VALUE_HEADS, ATTN_HEAD_SIZE)
    scores = jnp.einsum(
        "qkgd,skd->kgqs", query_head_count, key_head_count, preferred_element_type=jnp.float32
    ) * ATTN_HEAD_SIZE ** (-0.5)
    query_pos = offset + lax.broadcasted_iota(jnp.int32, (sequence_length, key_total_count), 0)
    key_pos = lax.broadcasted_iota(jnp.int32, (sequence_length, key_total_count), 1)
    visible = key_pos <= query_pos
    soft_out = jax.nn.softmax(jnp.where(visible, scores, -1e30), axis=-1)
    soft_bf = soft_out.astype(jnp.bfloat16)
    output = jnp.einsum(
        "kgqs,skd->qkgd", soft_bf, value_head_count, preferred_element_type=jnp.float32
    )
    attended_bf = output.reshape(sequence_length, QUERY_HEADS * ATTN_HEAD_SIZE).astype(jnp.bfloat16)
    return (attended_bf, soft_out, soft_bf, query_head_count, key_head_count, value_head_count)


def layer_forward(hidden_in, weights, head_params, offset):
    (
        norm_in,
        w_in,
        conv_w,
        conv_b,
        norm_ssm,
        w_out,
        query_weight,
        key_weight,
        value_weight,
        output_weight,
        norm_mid,
        w_gate,
        w_up,
        w_down,
    ) = weights
    dt_shift, log_rate, skip_gain = head_params
    inner_width = NH * HD
    conv_width = inner_width + 2 * NS
    normed_bf = rms_scale(hidden_in, norm_in.astype(jnp.float32)).astype(jnp.bfloat16)
    project = dot_plain(normed_bf, w_in)
    gate_raw = project[:, :inner_width]
    conv_in = project[:, inner_width : inner_width + conv_width]
    dt_raw = project[:, inner_width + conv_width :]
    rim_rows = passed_along(conv_in[conv_in.shape[0] - (CONV - 1) :], "shard", 1)
    extended = jnp.concatenate([rim_rows, conv_in], axis=0)
    conv_weight = conv_w.astype(jnp.float32)
    conv_bias = conv_b.astype(jnp.float32)
    state_end, decay_all = mixer_state(extended, dt_raw, conv_weight, conv_bias, dt_shift, log_rate)
    scanned = prefix(
        (decay_all, state_end),
        "shard",
        combine_state,
        (jnp.ones_like(decay_all), jnp.zeros_like(state_end)),
    )
    start_state = scanned[1]
    mixer_val = mixer_output(
        extended,
        gate_raw,
        dt_raw,
        conv_weight,
        conv_bias,
        dt_shift,
        log_rate,
        skip_gain,
        norm_ssm.astype(jnp.float32),
        start_state,
    )
    mamba_val = dot_plain(mixer_val.astype(jnp.bfloat16), w_out)
    key_bf = dot_plain(normed_bf, key_weight).astype(jnp.bfloat16)
    value_bf = dot_plain(normed_bf, value_weight).astype(jnp.bfloat16)
    gathered_keys, gathered_values = (
        lax.all_gather(key_bf, "shard", axis=0, tiled=True),
        lax.all_gather(value_bf, "shard", axis=0, tiled=True),
    )
    query_half_precision = dot_plain(normed_bf, query_weight).astype(jnp.bfloat16)
    attended = attend(query_half_precision, gathered_keys, gathered_values, offset)
    hidden = hidden_in + mamba_val + dot_plain(attended[0], output_weight)
    normed_mid = rms_scale(hidden, norm_mid.astype(jnp.float32)).astype(jnp.bfloat16)
    swish_out = swiglu(dot_plain(normed_mid, w_gate), dot_plain(normed_mid, w_up)).astype(
        jnp.bfloat16
    )
    result = hidden + dot_plain(swish_out, w_down)
    return (result, (hidden_in, rim_rows, start_state, gathered_keys, gathered_values))


def layer_backward(grad_out, kept, weights, head_params, offset):
    hidden_in, rim_rows, start_state, gathered_keys, gathered_values = kept
    (
        norm_in,
        w_in,
        conv_w,
        conv_b,
        norm_ssm,
        w_out,
        query_weight,
        key_weight,
        value_weight,
        output_weight,
        norm_mid,
        w_gate,
        w_up,
        w_down,
    ) = weights
    dt_shift, log_rate, skip_gain = head_params
    sequence_length = hidden_in.shape[0]
    key_total_count = gathered_keys.shape[0]
    query_groups = QUERY_HEADS // KEY_VALUE_HEADS
    inner_width = NH * HD
    conv_width = inner_width + 2 * NS
    rim_width = CONV - 1
    normed_val, in_pull = jax.vjp(rms_scale, hidden_in, norm_in.astype(jnp.float32))
    normed_bf = normed_val.astype(jnp.bfloat16)
    project = dot_plain(normed_bf, w_in)
    gate_raw = project[:, :inner_width]
    conv_in = project[:, inner_width : inner_width + conv_width]
    dt_raw = project[:, inner_width + conv_width :]
    extended = jnp.concatenate([rim_rows, conv_in], axis=0)
    conv_weight = conv_w.astype(jnp.float32)
    conv_bias = conv_b.astype(jnp.float32)
    mixer_val, mixer_pull = jax.vjp(
        mixer_output,
        extended,
        gate_raw,
        dt_raw,
        conv_weight,
        conv_bias,
        dt_shift,
        log_rate,
        skip_gain,
        norm_ssm.astype(jnp.float32),
        start_state,
    )
    mixer_bf = mixer_val.astype(jnp.bfloat16)
    mamba_val = dot_plain(mixer_bf, w_out)
    query_half_precision = dot_plain(normed_bf, query_weight).astype(jnp.bfloat16)
    attended_bf, soft_out, soft_bf, query_head_count, key_head_count, value_head_count = attend(
        query_half_precision, gathered_keys, gathered_values, offset
    )
    hidden = hidden_in + mamba_val + dot_plain(attended_bf, output_weight)
    normed_mid, mid_pull = jax.vjp(rms_scale, hidden, norm_mid.astype(jnp.float32))
    normed_mid_bf = normed_mid.astype(jnp.bfloat16)
    swish_val, swish_pull = jax.vjp(
        swiglu, dot_plain(normed_mid_bf, w_gate), dot_plain(normed_mid_bf, w_up)
    )
    swish_bf = swish_val.astype(jnp.bfloat16)
    grad_out_bf = grad_out.astype(jnp.bfloat16)
    grad_gate, grad_up = swish_pull(product_backward(grad_out_bf, w_down))
    grad_gate_bf = grad_gate.astype(jnp.bfloat16)
    grad_up_bf = grad_up.astype(jnp.bfloat16)
    grad_hidden_norm, grad_gain_mid = mid_pull(
        product_backward(grad_gate_bf, w_gate) + product_backward(grad_up_bf, w_up)
    )
    grad_hidden = grad_out + grad_hidden_norm
    hidden_gradient_half = grad_hidden.astype(jnp.bfloat16)
    grad_attended = (
        product_backward(hidden_gradient_half, output_weight)
        .astype(jnp.bfloat16)
        .reshape(sequence_length, KEY_VALUE_HEADS, query_groups, ATTN_HEAD_SIZE)
    )
    grad_soft = jnp.einsum(
        "qkgd,skd->kgqs", grad_attended, value_head_count, preferred_element_type=jnp.float32
    )
    value_gradient = jnp.einsum(
        "kgqs,qkgd->skd", soft_bf, grad_attended, preferred_element_type=jnp.float32
    )
    row_total = jnp.sum(soft_out * grad_soft, axis=-1, keepdims=True)
    grad_scores = (soft_out * (grad_soft - row_total)).astype(jnp.bfloat16)
    grad_query = jnp.einsum(
        "kgqs,skd->qkgd", grad_scores, key_head_count, preferred_element_type=jnp.float32
    ) * ATTN_HEAD_SIZE ** (-0.5)
    grad_query_bf = grad_query.reshape(sequence_length, QUERY_HEADS * ATTN_HEAD_SIZE).astype(
        jnp.bfloat16
    )
    key_gradient = jnp.einsum(
        "kgqs,qkgd->skd", grad_scores, query_head_count, preferred_element_type=jnp.float32
    ) * ATTN_HEAD_SIZE ** (-0.5)
    grad_key_own, grad_value_own = (
        lax.psum_scatter(
            key_gradient.reshape(key_total_count, KEY_VALUE_HEADS * ATTN_HEAD_SIZE).astype(
                jnp.bfloat16
            ),
            "shard",
            scatter_dimension=0,
            tiled=True,
        ).astype(jnp.float32),
        lax.psum_scatter(
            value_gradient.reshape(key_total_count, KEY_VALUE_HEADS * ATTN_HEAD_SIZE).astype(
                jnp.bfloat16
            ),
            "shard",
            scatter_dimension=0,
            tiled=True,
        ).astype(jnp.float32),
    )
    grad_key_bf = grad_key_own.astype(jnp.bfloat16)
    grad_value_bf = grad_value_own.astype(jnp.bfloat16)
    mixer_grads = mixer_pull(product_backward(hidden_gradient_half, w_out))
    (state_end, decay_all), state_pull = jax.vjp(
        mixer_state, extended, dt_raw, conv_weight, conv_bias, dt_shift, log_rate
    )
    scanned = prefix_2(
        (decay_all, mixer_grads[9]),
        "shard",
        combine_state,
        (jnp.ones_like(decay_all), jnp.zeros_like(state_end)),
    )
    grad_carry = scanned[1]
    grad_decay = jnp.sum(grad_carry * start_state, axis=(1, 2))
    state_grads = state_pull((grad_carry, grad_decay))
    grad_extended = mixer_grads[0] + state_grads[0]
    returned = passed_along(grad_extended[:rim_width], "shard", -1)
    grad_conv_in = grad_extended[rim_width:] + jnp.concatenate(
        [jnp.zeros((sequence_length - rim_width, conv_width), jnp.float32), returned], axis=0
    )
    grad_dt_raw = mixer_grads[2] + state_grads[1]
    grad_project_bf = jnp.concatenate([mixer_grads[1], grad_conv_in, grad_dt_raw], axis=1).astype(
        jnp.bfloat16
    )
    grad_normed = (
        product_backward(grad_project_bf, w_in)
        + product_backward(grad_query_bf, query_weight)
        + product_backward(grad_key_bf, key_weight)
        + product_backward(grad_value_bf, value_weight)
    )
    grad_input_norm, grad_gain_in = in_pull(grad_normed)
    grad_input = grad_hidden + grad_input_norm
    stash = (
        normed_bf,
        grad_project_bf,
        grad_query_bf,
        grad_key_bf,
        grad_value_bf,
        mixer_bf,
        attended_bf,
        hidden_gradient_half,
        normed_mid_bf,
        grad_gate_bf,
        grad_up_bf,
        swish_bf,
        grad_out_bf,
    )
    small_grads = (
        grad_gain_in,
        mixer_grads[3] + state_grads[2],
        mixer_grads[4] + state_grads[3],
        mixer_grads[8],
        grad_gain_mid,
        mixer_grads[5] + state_grads[4],
        mixer_grads[6] + state_grads[5],
        mixer_grads[7],
    )
    return (grad_input, stash, small_grads)


def body(
    inputs,
    cotangent,
    norm_in,
    w_in,
    conv_w,
    conv_b,
    dt_bias,
    a_log,
    skip_gain,
    norm_ssm,
    w_out,
    query_weight,
    key_weight,
    value_weight,
    output_weight,
    norm_mid,
    w_gate,
    w_up,
    w_down,
):
    sequence_length = inputs.shape[2]
    offset = lax.axis_index("shard") * sequence_length
    section_first = lax.axis_index("section") == 0
    head_params = (dt_bias[0], a_log[0], skip_gain[0])
    weights = (
        lax.all_gather(norm_in[0], "shard", axis=0, tiled=True),
        lax.all_gather(w_in[0], "shard", axis=0, tiled=True),
        lax.all_gather(conv_w[0], "shard", axis=1, tiled=True),
        lax.all_gather(conv_b[0], "shard", axis=0, tiled=True),
        lax.all_gather(norm_ssm[0], "shard", axis=0, tiled=True),
        lax.all_gather(w_out[0], "shard", axis=0, tiled=True),
        lax.all_gather(query_weight[0], "shard", axis=0, tiled=True),
        lax.all_gather(key_weight[0], "shard", axis=0, tiled=True),
        lax.all_gather(value_weight[0], "shard", axis=0, tiled=True),
        lax.all_gather(output_weight[0], "shard", axis=0, tiled=True),
        lax.all_gather(norm_mid[0], "shard", axis=0, tiled=True),
        lax.all_gather(w_gate[0], "shard", axis=0, tiled=True),
        lax.all_gather(w_up[0], "shard", axis=0, tiled=True),
        lax.all_gather(w_down[0], "shard", axis=0, tiled=True),
    )
    received = jnp.zeros((sequence_length, MODEL_WIDTH), jnp.bfloat16)
    out_ticks = []
    kept_ticks = []
    for clock_tick in range(MB + 1):
        layer_in = jnp.where(section_first, inputs[min(clock_tick, MB - 1), 0], received).astype(
            jnp.float32
        )
        result, kept = layer_forward(layer_in, weights, head_params, offset)
        result_bf = result.astype(jnp.bfloat16)
        received = passed_along(result_bf, "section", 1)
        out_ticks.append(result_bf)
        kept_ticks.append(kept)
    section_rows = [
        choose(section_first, out_ticks[batch_index], out_ticks[batch_index + 1])
        for batch_index in range(MB)
    ]
    kept_batches = [
        choose(section_first, kept_ticks[batch_index], kept_ticks[batch_index + 1])
        for batch_index in range(MB)
    ]
    weights_back = (
        lax.all_gather(norm_in[0], "shard", axis=0, tiled=True),
        lax.all_gather(w_in[0], "shard", axis=0, tiled=True),
        lax.all_gather(conv_w[0], "shard", axis=1, tiled=True),
        lax.all_gather(conv_b[0], "shard", axis=0, tiled=True),
        lax.all_gather(norm_ssm[0], "shard", axis=0, tiled=True),
        lax.all_gather(w_out[0], "shard", axis=0, tiled=True),
        lax.all_gather(query_weight[0], "shard", axis=0, tiled=True),
        lax.all_gather(key_weight[0], "shard", axis=0, tiled=True),
        lax.all_gather(value_weight[0], "shard", axis=0, tiled=True),
        lax.all_gather(output_weight[0], "shard", axis=0, tiled=True),
        lax.all_gather(norm_mid[0], "shard", axis=0, tiled=True),
        lax.all_gather(w_gate[0], "shard", axis=0, tiled=True),
        lax.all_gather(w_up[0], "shard", axis=0, tiled=True),
        lax.all_gather(w_down[0], "shard", axis=0, tiled=True),
    )
    returned = jnp.zeros((sequence_length, MODEL_WIDTH), jnp.bfloat16)
    grad_ticks = []
    stash_ticks = []
    small_ticks = []
    for clock_tick in range(MB + 1):
        kept = choose(
            section_first,
            kept_batches[max(clock_tick - 1, 0)],
            kept_batches[min(clock_tick, MB - 1)],
        )
        grad_out = jnp.where(section_first, returned, cotangent[min(clock_tick, MB - 1), 0]).astype(
            jnp.float32
        )
        grad_input, stash, small_grads = layer_backward(
            grad_out, kept, weights_back, head_params, offset
        )
        returned = passed_along(grad_input.astype(jnp.bfloat16), "section", -1)
        grad_ticks.append(grad_input)
        stash_ticks.append(stash)
        small_ticks.append(small_grads)
    grad_rows = [
        choose(section_first, grad_ticks[batch_index + 1], grad_ticks[batch_index])
        for batch_index in range(MB)
    ]
    stash_batches = [
        choose(section_first, stash_ticks[batch_index + 1], stash_ticks[batch_index])
        for batch_index in range(MB)
    ]
    small_total = choose(section_first, small_ticks[1], small_ticks[0])
    batch_index = 1
    small_total = jax.tree.map(
        jnp.add,
        small_total,
        choose(section_first, small_ticks[batch_index + 1], small_ticks[batch_index]),
    )
    stacked = jax.tree.map(lambda *members: jnp.concatenate(members, axis=0), *stash_batches)
    (
        normed_all,
        grad_project_all,
        grad_query_all,
        grad_key_all,
        grad_value_all,
        mixer_all,
        attended_all,
        grad_hidden_all,
        normed_mid_all,
        grad_gate_all,
        grad_up_all,
        swish_all,
        grad_out_all,
    ) = stacked
    (
        grad_gain_in,
        grad_conv_weight,
        grad_conv_bias,
        grad_gain_ssm,
        grad_gain_mid,
        grad_dt_shift,
        grad_log_rate,
        grad_skip_gain,
    ) = small_total
    scattered = (
        lax.psum_scatter(
            grad_gain_in.astype(jnp.bfloat16), "shard", scatter_dimension=0, tiled=True
        ).astype(jnp.float32),
        lax.psum_scatter(
            dot_rows(normed_all, grad_project_all).astype(jnp.bfloat16),
            "shard",
            scatter_dimension=0,
            tiled=True,
        ).astype(jnp.float32),
        lax.psum_scatter(
            grad_conv_weight.astype(jnp.bfloat16), "shard", scatter_dimension=1, tiled=True
        ).astype(jnp.float32),
        lax.psum_scatter(
            grad_conv_bias.astype(jnp.bfloat16), "shard", scatter_dimension=0, tiled=True
        ).astype(jnp.float32),
        lax.psum_scatter(
            grad_gain_ssm.astype(jnp.bfloat16), "shard", scatter_dimension=0, tiled=True
        ).astype(jnp.float32),
        lax.psum_scatter(
            dot_rows(mixer_all, grad_hidden_all).astype(jnp.bfloat16),
            "shard",
            scatter_dimension=0,
            tiled=True,
        ).astype(jnp.float32),
        lax.psum_scatter(
            dot_rows(normed_all, grad_query_all).astype(jnp.bfloat16),
            "shard",
            scatter_dimension=0,
            tiled=True,
        ).astype(jnp.float32),
        lax.psum_scatter(
            dot_rows(normed_all, grad_key_all).astype(jnp.bfloat16),
            "shard",
            scatter_dimension=0,
            tiled=True,
        ).astype(jnp.float32),
        lax.psum_scatter(
            dot_rows(normed_all, grad_value_all).astype(jnp.bfloat16),
            "shard",
            scatter_dimension=0,
            tiled=True,
        ).astype(jnp.float32),
        lax.psum_scatter(
            dot_rows(attended_all, grad_hidden_all).astype(jnp.bfloat16),
            "shard",
            scatter_dimension=0,
            tiled=True,
        ).astype(jnp.float32),
        lax.psum_scatter(
            grad_gain_mid.astype(jnp.bfloat16), "shard", scatter_dimension=0, tiled=True
        ).astype(jnp.float32),
        lax.psum_scatter(
            dot_rows(normed_mid_all, grad_gate_all).astype(jnp.bfloat16),
            "shard",
            scatter_dimension=0,
            tiled=True,
        ).astype(jnp.float32),
        lax.psum_scatter(
            dot_rows(normed_mid_all, grad_up_all).astype(jnp.bfloat16),
            "shard",
            scatter_dimension=0,
            tiled=True,
        ).astype(jnp.float32),
        lax.psum_scatter(
            dot_rows(swish_all, grad_out_all).astype(jnp.bfloat16),
            "shard",
            scatter_dimension=0,
            tiled=True,
        ).astype(jnp.float32),
    )
    summed = (
        lax.psum(scattered[0].astype(jnp.bfloat16), "rep").astype(jnp.float32),
        lax.psum(scattered[1].astype(jnp.bfloat16), "rep").astype(jnp.float32),
        lax.psum(scattered[2].astype(jnp.bfloat16), "rep").astype(jnp.float32),
        lax.psum(scattered[3].astype(jnp.bfloat16), "rep").astype(jnp.float32),
        lax.psum(scattered[4].astype(jnp.bfloat16), "rep").astype(jnp.float32),
        lax.psum(scattered[5].astype(jnp.bfloat16), "rep").astype(jnp.float32),
        lax.psum(scattered[6].astype(jnp.bfloat16), "rep").astype(jnp.float32),
        lax.psum(scattered[7].astype(jnp.bfloat16), "rep").astype(jnp.float32),
        lax.psum(scattered[8].astype(jnp.bfloat16), "rep").astype(jnp.float32),
        lax.psum(scattered[9].astype(jnp.bfloat16), "rep").astype(jnp.float32),
        lax.psum(scattered[10].astype(jnp.bfloat16), "rep").astype(jnp.float32),
        lax.psum(scattered[11].astype(jnp.bfloat16), "rep").astype(jnp.float32),
        lax.psum(scattered[12].astype(jnp.bfloat16), "rep").astype(jnp.float32),
        lax.psum(scattered[13].astype(jnp.bfloat16), "rep").astype(jnp.float32),
    )
    head_grads = lax.psum((grad_dt_shift, grad_log_rate, grad_skip_gain), ("rep", "shard"))
    section_out = jnp.stack(section_rows)[None, :, None]
    input_grad = jnp.stack(grad_rows)[None, :, None]
    return (
        section_out,
        input_grad,
        summed[0][None],
        summed[1][None],
        summed[2][None],
        summed[3][None],
        head_grads[0][None],
        head_grads[1][None],
        head_grads[2][None],
        summed[4][None],
        summed[5][None],
        summed[6][None],
        summed[7][None],
        summed[8][None],
        summed[9][None],
        summed[10][None],
        summed[11][None],
        summed[12][None],
        summed[13][None],
    )


def solution(mesh):
    return jax.shard_map(
        body,
        mesh=mesh,
        in_specs=(
            P(None, "rep", "shard", None),
            P(None, "rep", "shard", None),
            P("section", "shard"),
            P("section", "shard", None),
            P("section", None, "shard"),
            P("section", "shard"),
            P("section", None),
            P("section", None),
            P("section", None),
            P("section", "shard"),
            P("section", "shard", None),
            P("section", "shard", None),
            P("section", "shard", None),
            P("section", "shard", None),
            P("section", "shard", None),
            P("section", "shard"),
            P("section", "shard", None),
            P("section", "shard", None),
            P("section", "shard", None),
        ),
        out_specs=(
            P("section", None, "rep", "shard", None),
            P("section", None, "rep", "shard", None),
            P("section", "shard"),
            P("section", "shard", None),
            P("section", None, "shard"),
            P("section", "shard"),
            P("section", None),
            P("section", None),
            P("section", None),
            P("section", "shard"),
            P("section", "shard", None),
            P("section", "shard", None),
            P("section", "shard", None),
            P("section", "shard", None),
            P("section", "shard", None),
            P("section", "shard"),
            P("section", "shard", None),
            P("section", "shard", None),
            P("section", "shard", None),
        ),
        check_vma=False,
    )
```

profile of v0, /device:TPU:0, one launch (start us, length us, event | category | flops | bytes accessed | tf_op | source)
XLA Modules:
  0.0 2040.3 jit_solution(7676901987491877386)
XLA Ops:
  11.4 23.3 %all-gather.1 = bf16[1,4,1792]{1,0,2:T(2,128)(2,1)S(1)} all-gather(bf16[1,4,112]{1,0,2:T(2,128)(2,1)S(1)} %copy.558), channel_id=3, replica_groups=mesh['section'=2,'rep'=4,'shard'=16] {'shard'}, dimensions={2}, use_global_device_ids=true | all-gather | bytes 15232 | tf_op jit(solution)/shard_map/all_gather | solution.py:460
  35.7 37.1 %slice_reduce_fusion.3 = (f32[1792]{0:T(1024)S(1)}, f32[1792]{0:T(1024)S(1)}, f32[1792]{0:T(1024)S(1)}, f32[1792]{0:T(1024)S(1)}) fusion(f32[1,4,1792]{1,0,2:T(1,128)S(1)} %convert_element_type.811), kind=kLoop, calls=%fused_computation.320 | loop fusion | bytes 57344 | tf_op jit(solution)/shard_map/slice | solution.py:112
  76.5 55.2 %all-reduce.82 = (bf16[1024]{0:T(1024)(128)(2,1)S(1)}, bf16[1536]{0:T(1024)(128)(2,1)S(1)}, bf16[1792]{0:T(1024)(128)(2,1)S(1)}, bf16[1024]{0:T(1024)(128)(2,1)}) all-reduce(bf16[1024]{0:T(1024)(128)(2,1)S(1)} %dynamic-update-slice.1, ...), channel_id=4, replica_groups=mesh['section'=2,'rep'=4,'shard'=16] {'shard'}, use_global_device_ids=true, to_apply=%add.73 | all-reduce | flops 5376 | bytes 21504
  161.9 18.9 all_gather.144
  267.9 35.9 %all-gather.54.cloned.1.call-done = bf16[1,2048,1024]{2,1,0:T(8,128)(2,1)} async-done(((bf16[1,128,1024]{2,1,0:T(8,128)(2,1)}), bf16[1,2048,1024]{2,1,0:T(8,128)(2,1)}) %all-gather.54.cloned.1.call-update) | async-done | bytes 4194320 | tf_op jit(solution)/shard_map/all_gather | solution.py:471
  303.9 39.2 %all-gather.52.cloned.1.call-done = bf16[1,1024,2048]{2,1,0:T(8,128)(2,1)} async-done(((bf16[1,64,2048]{2,1,0:T(8,128)(2,1)}), bf16[1,1024,2048]{2,1,0:T(8,128)(2,1)}) %all-gather.52.cloned.1.call-update) | async-done | bytes 4194320 | tf_op jit(solution)/shard_map/all_gather | solution.py:470
  373.6 20.4 all_gather.156
  554.6 42.5 %all-gather.23 = bf16[16,1,24]{2,1,0:T(2,128)(2,1)S(1)} all-gather(bf16[1,1,24]{2,1,0:T(2,128)(2,1)} %convert_bitcast_fusion.2), channel_id=1, replica_groups=mesh['section'=2,'rep'=4,'shard'=16] {'shard'}, dimensions={0}, use_global_device_ids=true | all-gather | bytes 816 | tf_op jit(solution)/shard_map/all_gather | solution.py:51
  614.1 28.6 %while.81 = (s32[]{:T(128)}, f32[24,64,128]{2,1,0:T(8,128)S(1)}, s32[]{:T(128)}, bf16[16,24]{1,0:T(8,128)(2,1)}, bf16[16,24,64,128]{3,2,1,0:T(8,128)(2,1)}, /*index=5*/s32[]{:T(128)}, s32[]{:T(128)}, s32[]{:T(128)}, s32[]{:T(128)}) while((s32[]{:T(128)}, f32[24,64,128]{2,1,0:T(8,128)S(1)}, s32[]{:T(128)}, bf16[16,24]{1,0:T(8,128)(2,1)}, ...), condition=%wide.region_34.36_spmd, body=%wide.region_33.35_spmd.sunk | while | flops 589854 | bytes 1966475 | solution.py:68
  670.0 58.7 %reduce-scatter.51.cloned.1.call-done = bf16[64,128]{1,0:T(8,128)(2,1)} async-done(((bf16[1024,128]{1,0:T(8,128)(2,1)}), bf16[64,128]{1,0:T(8,128)(2,1)}) %reduce-scatter.51.cloned.1.call-update) | async-done | bytes 16400
  785.0 18.2 all_gather.161
  911.0 41.8 %all-gather.24 = bf16[16,1,24]{2,1,0:T(2,128)(2,1)S(1)} all-gather(bf16[1,1,24]{2,1,0:T(2,128)(2,1)S(1)} %convert_bitcast_fusion.1), channel_id=1, replica_groups=mesh['section'=2,'rep'=4,'shard'=16] {'shard'}, dimensions={0}, use_global_device_ids=true | all-gather | bytes 816 | tf_op jit(solution)/shard_map/all_gather | solution.py:51
  999.0 44.4 %while.82 = (s32[]{:T(128)}, f32[24,64,128]{2,1,0:T(8,128)}, s32[]{:T(128)}, bf16[16,24]{1,0:T(8,128)(2,1)}, bf16[16,24,64,128]{3,2,1,0:T(8,128)(2,1)}, /*index=5*/s32[]{:T(128)}, s32[]{:T(128)}, s32[]{:T(128)}, s32[]{:T(128)}) while((s32[]{:T(128)}, f32[24,64,128]{2,1,0:T(8,128)}, s32[]{:T(128)}, bf16[16,24]{1,0:T(8,128)(2,1)}, ...), condition=%wide.region_57.59_spmd, body=%wide.region_56.58_spmd.sunk | while | flops 589854 | bytes 1966475 | solution.py:68
  1083.1 20.9 %reduce-scatter.55.cloned.1.call-done = bf16[64,128]{1,0:T(8,128)(2,1)} async-done(((bf16[1024,128]{1,0:T(8,128)(2,1)}), bf16[64,128]{1,0:T(8,128)(2,1)}) %reduce-scatter.55.cloned.1.call-update) | async-done | bytes 16400
  1225.7 44.3 %while.83 = (s32[]{:T(128)}, f32[24,64,128]{2,1,0:T(8,128)}, s32[]{:T(128)}, bf16[16,24]{1,0:T(8,128)(2,1)}, bf16[16,24,64,128]{3,2,1,0:T(8,128)(2,1)}, /*index=5*/s32[]{:T(128)}, s32[]{:T(128)}, s32[]{:T(128)}, s32[]{:T(128)}) while((s32[]{:T(128)}, f32[24,64,128]{2,1,0:T(8,128)}, s32[]{:T(128)}, bf16[16,24]{1,0:T(8,128)(2,1)}, ...), condition=%wide.region_80.82_spmd, body=%wide.region_79.81_spmd.sunk | while | flops 589854 | bytes 1966475 | solution.py:68
  1381.1 141.5 %all-reduce.80 = (f32[1,24]{1,0:T(1,128)}, f32[1,24]{1,0:T(1,128)}, f32[1,24]{1,0:T(1,128)}) all-reduce(f32[1,24]{1,0:T(1,128)S(1)} %fusion.692, f32[1,24]{1,0:T(1,128)S(1)} %fusion.694, f32[1,24]{1,0:T(1,128)S(1)} %fusion.696), channel_id=1, replica_groups=mesh['section'=2,'rep'=4,'shard'=16] {'rep','shard'}, use_global_device_ids=true, to_apply=%region_140.142 | all-reduce | flops 72 | bytes 576 | tf_op jit(solution)/shard_map/psum | solution.py:657
  1528.8 31.6 %reduce-scatter.43.cloned.1.call-done = bf16[64,2048]{1,0:T(8,128)(2,1)} async-done(((bf16[1024,2048]{1,0:T(8,128)(2,1)}), bf16[64,2048]{1,0:T(8,128)(2,1)}) %reduce-scatter.43.cloned.1.call-update) | async-done | bytes 262160 | tf_op jit(solution)/shard_map/reduce_scatter | solution.py:622
  1560.4 68.4 %reduce-scatter.45.cloned.1.call-done = bf16[64,2048]{1,0:T(8,128)(2,1)} async-done(((bf16[1024,2048]{1,0:T(8,128)(2,1)}), bf16[64,2048]{1,0:T(8,128)(2,1)}) %reduce-scatter.45.cloned.1.call-update) | async-done | bytes 262160 | tf_op jit(solution)/shard_map/reduce_scatter | solution.py:628
  1628.8 68.5 %reduce-scatter.47.cloned.1.call-done = bf16[128,1024]{1,0:T(8,128)(2,1)} async-done(((bf16[2048,1024]{1,0:T(8,128)(2,1)}), bf16[128,1024]{1,0:T(8,128)(2,1)}) %reduce-scatter.47.cloned.1.call-update) | async-done | bytes 262160 | tf_op jit(solution)/shard_map/reduce_scatter | solution.py:634
  1697.3 84.3 %reduce-scatter.31.cloned.1.call-done = bf16[64,3352]{1,0:T(8,128)(2,1)} async-done(((bf16[1024,3352]{1,0:T(8,128)(2,1)}), bf16[64,3352]{1,0:T(8,128)(2,1)}) %reduce-scatter.31.cloned.1.call-update) | async-done | bytes 429072 | tf_op jit(solution)/shard_map/reduce_scatter | solution.py:574
  1782.3 54.8 %all-reduce.81 = (bf16[1024]{0:T(1024)(128)(2,1)S(1)}, bf16[1792]{0:T(1024)(128)(2,1)S(1)}, bf16[1536]{0:T(1024)(128)(2,1)S(1)}, bf16[1024]{0:T(1024)(128)(2,1)S(1)}) all-reduce(bf16[1024]{0:T(1024)(128)(2,1)S(1)} %add_convert_fusion.7, ...), channel_id=28, replica_groups=mesh['section'=2,'rep'=4,'shard'=16] {'shard'}, use_global_device_ids=true, to_apply=%region_96.98.clone | all-reduce | flops 5376 | bytes 21504
  1847.5 60.7 %reduce-scatter.37.cloned.1.call-done = bf16[64,128]{1,0:T(8,128)(2,1)} async-done(((bf16[1024,128]{1,0:T(8,128)(2,1)}), bf16[64,128]{1,0:T(8,128)(2,1)}) %reduce-scatter.37.cloned.1.call-update) | async-done | bytes 16400 | tf_op jit(solution)/shard_map/reduce_scatter | solution.py:601
  1908.2 62.1 %reduce-scatter.39.cloned.1.call-done = bf16[64,128]{1,0:T(8,128)(2,1)} async-done(((bf16[1024,128]{1,0:T(8,128)(2,1)}), bf16[64,128]{1,0:T(8,128)(2,1)}) %reduce-scatter.39.cloned.1.call-update) | async-done | bytes 16400 | tf_op jit(solution)/shard_map/reduce_scatter | solution.py:607
  1992.3 30.4 %all-reduce.87.cloned.1.call-done = (bf16[1,64,3352]{2,1,0:T(8,128)(2,1)}, bf16[1,96,1024]{2,1,0:T(8,128)(2,1)}, bf16[1,64,512]{2,1,0:T(8,128)(2,1)}, bf16[1,32,...) async-done(((bf16[1,64,3352]{2,1,0:T(8,128)(2,1)}, bf16[1,96,1024]{2,1,0:T(8,128)(2,1)}, ...) | async-done | bytes 1543184 | tf_op jit(solution)/shard_map/psum | solution.py:643
  (1549 shorter events, 1000.1 us)
Async XLA Ops:
  7.9 212.6 %all-gather.46.cloned.1.call-start = ((), (), s32[]{:S(2)}) async-start(), calls=%async_computation.28 | async-start | bytes 1114112 | tf_op jit(solution)/shard_map/all_gather | solution.py:464
  8.7 221.2 %all-gather.48.cloned.1.call-start = ((), (), s32[]{:S(2)}) async-start(), calls=%async_computation.29 | async-start | bytes 1114112 | tf_op jit(solution)/shard_map/all_gather | solution.py:467
  9.4 245.4 %all-gather.42.cloned.1.call-start = ((), (), s32[]{:S(2)}) async-start(), calls=%async_computation.26 | async-start | bytes 6684672 | tf_op jit(solution)/shard_map/all_gather | solution.py:29
  143.4 199.6 %all-gather.52.cloned.1.call-start = ((), (), s32[]{:S(2)}) async-start(), calls=%async_computation.31 | async-start | bytes 4456448 | tf_op jit(solution)/shard_map/all_gather | solution.py:470
  144.2 300.7 %all-gather.56.cloned.1.call-start = ((), (), s32[]{:S(2)}) async-start(), calls=%async_computation.33 | async-start | bytes 6684672 | tf_op jit(solution)/shard_map/all_gather | solution.py:29
  367.5 246.5 %all-gather.60.cloned.1.call-start = ((), (), s32[]{:S(2)}) async-start(), calls=%async_computation.35 | async-start | bytes 6684672 | tf_op jit(solution)/shard_map/all_gather | solution.py:51
  553.2 175.4 %reduce-scatter.51.cloned.1.call-start = ((), (), s32[]{:S(2)}) async-start(), calls=%async_computation.39 | async-start | bytes 278528
  608.5 243.8 %all-gather.58.cloned.1.call-start = ((), (), s32[]{:S(2)}) async-start(), calls=%async_computation.34 | async-start | bytes 6684672 | tf_op jit(solution)/shard_map/all_gather | solution.py:29
  758.8 239.1 %all-gather.62.cloned.1.call-start = ((), (), s32[]{:S(2)}) async-start(), calls=%async_computation.36 | async-start | bytes 6684672 | tf_op jit(solution)/shard_map/all_gather | solution.py:51
  910.3 170.8 %reduce-scatter.53.cloned.1.call-start = ((), (), s32[]{:S(2)}) async-start(), calls=%async_computation.40 | async-start | bytes 278528
  997.9 226.9 %all-gather.64.cloned.1.call-start = ((), (), s32[]{:S(2)}) async-start(), calls=%async_computation.37 | async-start | bytes 6684672 | tf_op jit(solution)/shard_map/all_gather | solution.py:51
  1136.7 237.4 %reduce-scatter.57.cloned.1.call-start = ((), (), s32[]{:S(2)}) async-start(), calls=%async_computation.42 | async-start | bytes 278528
  1147.4 231.5 %reduce-scatter.59.cloned.1.call-start = ((), (), s32[]{:S(2)}) async-start(), calls=%async_computation.43 | async-start | bytes 278528
  1152.0 376.7 %reduce-scatter.35.cloned.1.call-start = ((), (), s32[]{:S(2)}) async-start(), calls=%async_computation.18 | async-start | bytes 1114112 | tf_op jit(solution)/shard_map/reduce_scatter | solution.py:595
  1158.1 370.6 %reduce-scatter.41.cloned.1.call-start = ((), (), s32[]{:S(2)}) async-start(), calls=%async_computation.21 | async-start | bytes 1114112 | tf_op jit(solution)/shard_map/reduce_scatter | solution.py:613
  1161.7 367.0 %reduce-scatter.33.cloned.1.call-start = ((), (), s32[]{:S(2)}) async-start(), calls=%async_computation.17 | async-start | bytes 3342336 | tf_op jit(solution)/shard_map/reduce_scatter | solution.py:589
  1166.9 393.5 %reduce-scatter.43.cloned.1.call-start = ((), (), s32[]{:S(2)}) async-start(), calls=%async_computation.22 | async-start | bytes 4456448 | tf_op jit(solution)/shard_map/reduce_scatter | solution.py:622
  1171.4 457.4 %reduce-scatter.45.cloned.1.call-start = ((), (), s32[]{:S(2)}) async-start(), calls=%async_computation.23 | async-start | bytes 4456448 | tf_op jit(solution)/shard_map/reduce_scatter | solution.py:628
  1175.9 521.5 %reduce-scatter.47.cloned.1.call-start = ((), (), s32[]{:S(2)}) async-start(), calls=%async_computation.24 | async-start | bytes 4456448 | tf_op jit(solution)/shard_map/reduce_scatter | solution.py:634
  1180.3 601.4 %reduce-scatter.31.cloned.1.call-start = ((), (), s32[]{:S(2)}) async-start(), calls=%async_computation.16 | async-start | bytes 7520256 | tf_op jit(solution)/shard_map/reduce_scatter | solution.py:574
  1308.7 538.0 %reduce-scatter.61.cloned.1.call-start = ((), (), s32[]{:S(2)}) async-start(), calls=%async_computation.44 | async-start | bytes 487424
  1377.2 531.1 %reduce-scatter.37.cloned.1.call-start = ((), (), s32[]{:S(2)}) async-start(), calls=%async_computation.19 | async-start | bytes 278528 | tf_op jit(solution)/shard_map/reduce_scatter | solution.py:601
  1378.2 592.1 %reduce-scatter.39.cloned.1.call-start = ((), (), s32[]{:S(2)}) async-start(), calls=%async_computation.20 | async-start | bytes 278528 | tf_op jit(solution)/shard_map/reduce_scatter | solution.py:607
  1380.9 641.9 %all-reduce.87.cloned.1.call-start = ((), (), s32[]{:S(2)}) async-start(), calls=%async_computation.45 | async-start | bytes 3112960 | tf_op jit(solution)/shard_map/psum | solution.py:643
  (435 other events, 9237.6 us)
Sparse Core Ops, SparseCore 0:
  9.7 53.0 all-gather.39
  141.7 45.3 all-gather.41
  367.6 50.2 all-gather.55
  535.9 68.2 all-gather.59
  606.6 61.0 reduce-scatter.48
  670.0 58.6 reduce-scatter.50
  758.9 44.2 all-gather.57
  910.4 68.8 all-gather.61
  981.6 61.0 reduce-scatter.52
  1045.0 58.8 reduce-scatter.54
  1136.8 39.0 all-gather.63
  1178.1 61.1 reduce-scatter.56
  1241.7 58.6 reduce-scatter.58
  1302.6 60.0 reduce-scatter.34
  1365.2 60.0 reduce-scatter.40
  1427.8 64.3 reduce-scatter.32
  1494.5 65.7 reduce-scatter.42
  1562.6 66.1 reduce-scatter.44
  1631.2 66.0 reduce-scatter.46
  1699.6 82.0 reduce-scatter.30
  1784.6 62.0 reduce-scatter.60
  1849.6 58.5 reduce-scatter.36
  1911.3 58.9 reduce-scatter.38
  1973.0 49.6 all-reduce.86
  (6 shorter events, 214.3 us)
where the time goes:
time: 2060 us; the launch traced here: 2040 us
  blocking collectives  592 us (29%)
  waiting for transfers between devices  581 us (28%)
  matrix products  335 us (16%)
  other arithmetic  259 us (13%)
  local copies, waits for them, and re-layouts  223 us (11%)
  between operations  24.7 us (1%)
  starting transfers between devices  24.1 us (1%)
    psum x1, blocking collectives, body(): lax.psum((grad_dt_shift, grad_log_rate, grad_skip_gain), ('rep', 'shard'))  142 us
    unnamed x2, blocking collectives  110 us
    all_gather x3, blocking collectives, prefix_2(): lax.all_gather(a.astype(kind), axis)  101 us
    unnamed x37, waiting for transfers between devices  92.7 us
    dot_general x42, matrix products, dot_plain(): return jnp.dot(former, latter, preferred_element_type=jnp.float32)  86.4 us
    add x45, other arithmetic, combine_state(): later[0][:, None, None] * earlier[1] + later[1]  86.1 us
    reduce_scatter x1, waiting for transfers between devices, body(): lax.psum_scatter(dot_rows(normed_all, grad_project_all).astype(jnp.bfloat...  84.3 us
    reduce_scatter x1, waiting for transfers between devices, body(): lax.psum_scatter(dot_rows(swish_all, grad_out_all).astype(jnp.bfloat16),...  68.5 us
  transfers between devices with their start and end apart: 40, of which 15 were waited for; matrix products, arithmetic and copies ran while one was open for 29% of the time, Pallas kernels for 0%

commit v1 on v0

v1 whole, which is shorter than its diff:
```python
import jax
import jax.numpy as jnp
from jax import lax
from jax.experimental import pallas as pl
from jax.experimental.pallas import tpu as pltpu
from jax.sharding import PartitionSpec as P

MODEL_WIDTH = 1024
NH = 24
HD = 64
NS = 128
QUERY_HEADS = 8
KEY_VALUE_HEADS = 2
ATTN_HEAD_SIZE = 64
FF = 2048
CONV = 4
MB = 2

EPSILON = 1e-05

SHARDS = 16
CORES = 2
CHIPS = SHARDS // CORES
INNER = NH * HD
NARROW = INNER // SHARDS
LANES = 128
HALF_HEAD = ATTN_HEAD_SIZE // 2
IN_COLS = 4 * LANES
WIDE_COLS = 2 * LANES
CONVED = 3 * LANES
CHUNK = 128
BLOCK = 64
FF_CORE = FF // SHARDS
RATIO = ATTN_HEAD_SIZE ** (-0.5)

BF = jnp.bfloat16
F32 = jnp.float32


def dot_plain(former, latter):
    return jnp.dot(former, latter, preferred_element_type=F32)


def dot_rows(former, latter):
    return lax.dot_general(former, latter, (((0,), (0,)), ((), ())), preferred_element_type=F32)


def dot_back(former, latter):
    return lax.dot_general(former, latter, (((1,), (1,)), ((), ())), preferred_element_type=F32)


def exact(former, latter, dims):
    return lax.dot_general(
        former,
        latter,
        ((dims[:1], dims[1:]), ((), ())),
        precision=lax.Precision.HIGHEST,
        preferred_element_type=F32,
    )


def swap_cores(x):
    return lax.ppermute(x, "shard", [(i, i ^ 1) for i in range(SHARDS)])


def swap_sections(x):
    return lax.ppermute(x, "section", [(0, 1), (1, 0)])


def same_core():
    return [list(range(core, SHARDS, CORES)) for core in range(CORES)]


def spread(rows):
    count, width = rows.shape
    copies = jnp.broadcast_to(rows[None], (CHIPS, count, width)).reshape(CHIPS * count, width)
    return lax.all_to_all(copies, "shard", 0, 0, axis_index_groups=same_core(), tiled=True)


def collect(partial):
    rows = partial.shape[0] // CHIPS
    met = lax.all_to_all(
        partial.astype(BF), "shard", 0, 0, axis_index_groups=same_core(), tiled=True
    )
    return jnp.sum(met.reshape(CHIPS, rows, partial.shape[1]).astype(F32), axis=0)


def two_parts(x):
    high = x.astype(BF)
    return high, (x - high.astype(F32)).astype(BF)


def by_place(core, own, other, axis):
    return jnp.where(
        core == 0,
        jnp.concatenate([own, other], axis=axis),
        jnp.concatenate([other, own], axis=axis),
    )


def normalize(x):
    scale = lax.rsqrt(jnp.mean(x * x, axis=-1, keepdims=True) + EPSILON)
    return x * scale, scale


def normalize_back(unit, scale, grad):
    return scale * (grad - unit * jnp.mean(grad * unit, axis=-1, keepdims=True))


def whole_vmem(count):
    return [pl.BlockSpec(memory_space=pltpu.VMEM)] * count


def scalar_first(count):
    return [pl.BlockSpec(memory_space=pltpu.SMEM)] + whole_vmem(count)


def params():
    return pltpu.CompilerParams(vmem_limit_bytes=48 * 2**20)


def softplus(v):
    return jnp.maximum(v, 0.0) + jnp.log1p(jnp.exp(-jnp.abs(v)))


def chunk_rows(core, own_ref, recv_ref, k):
    at = pl.ds(pl.multiple_of(k * BLOCK, BLOCK), BLOCK)
    own = jnp.concatenate([own_ref[at, 0:LANES], own_ref[at, 3 * LANES : 5 * LANES]], axis=1)
    own = own.astype(F32)
    recv = recv_ref[at, 0:CONVED].astype(F32)
    return jnp.where(core == 0, own, recv), jnp.where(core == 0, recv, own)


def chunk_parts(ext, conv_ref, cols_ref, sel_ref):
    conv = conv_ref[CONV : CONV + 1, :]
    for j in range(CONV):
        start = 8 - (CONV - 1) + j
        conv = conv + conv_ref[j : j + 1, :] * ext[start : start + CHUNK, :]
    sig = 1.0 / (1.0 + jnp.exp(-conv))
    activated = conv * sig
    states_in = activated[:, 0:LANES]
    input_map = activated[:, LANES : 2 * LANES]
    output_map = activated[:, 2 * LANES :]
    raw = dot_plain(ext[8 : 8 + CHUNK, 0:LANES].astype(BF), sel_ref[...]) + cols_ref[0:1, :]
    step = softplus(raw)
    log_decay = -step * cols_ref[1:2, :]
    rows = lax.broadcasted_iota(jnp.int32, (CHUNK, CHUNK), 0)
    cols = lax.broadcasted_iota(jnp.int32, (CHUNK, CHUNK), 1)
    causal = cols <= rows
    lower = jnp.where(causal, 1.0, 0.0)
    cumulative = exact(lower, log_decay, (1, 0))
    turned = exact(log_decay, lower, (0, 1))
    weighted = states_in * step
    coupling = dot_back(output_map.astype(BF), input_map.astype(BF))
    within = []
    for lane in (0, NARROW - 1):
        gap = cumulative[:, lane : lane + 1] - turned[lane : lane + 1, :]
        within.append(jnp.where(causal, jnp.exp(jnp.where(causal, gap, 0.0)), 0.0))
    last = cumulative[CHUNK - 1 : CHUNK, :]
    tail = jnp.exp(last - cumulative)
    decay = jnp.exp(turned[:, CHUNK - 1 : CHUNK])
    return (
        conv,
        sig,
        states_in,
        input_map.astype(BF),
        output_map.astype(BF),
        raw,
        step,
        log_decay,
        lower,
        cumulative,
        weighted,
        coupling,
        within,
        last,
        tail,
        decay,
    )


def mixer_kernel(
    core_ref, own_ref, recv_ref, conv_ref, cols_ref, sel_ref, mine_ref, theirs_ref, starts_ref, ext
):
    core = core_ref[0]
    ext[0:8, :] = jnp.zeros((8, CONVED), F32)

    def chunk(k, state):
        first, second = chunk_rows(core, own_ref, recv_ref, k)
        ext[8 : 8 + BLOCK, :] = first
        ext[8 + BLOCK : 8 + CHUNK, :] = second
        (
            conv,
            sig,
            states_in,
            input_map,
            output_map,
            raw,
            step,
            log_decay,
            lower,
            cumulative,
            weighted,
            coupling,
            within,
            last,
            tail,
            decay,
        ) = chunk_parts(ext, conv_ref, cols_ref, sel_ref)
        starts_ref[k] = state
        mixed = dot_back(output_map, state.astype(BF)) * jnp.exp(cumulative)
        mixed = mixed + cols_ref[2:3, :] * states_in
        for head in range(2):
            mixed = mixed + dot_plain(
                (within[head] * coupling).astype(BF),
                (weighted * cols_ref[3 + head : 4 + head, :]).astype(BF),
            )
        state = decay * state + dot_rows((weighted * tail).astype(BF), input_map)
        at = pl.ds(pl.multiple_of(k * BLOCK, BLOCK), BLOCK)
        low, high = mixed[:BLOCK, :], mixed[BLOCK:, :]
        mine_ref[at, :] = jnp.where(core == 0, low, high).astype(BF)
        theirs_ref[at, :] = jnp.where(core == 0, high, low).astype(BF)
        ext[0:8, :] = ext[CHUNK : CHUNK + 8, :]
        return state

    lax.fori_loop(0, CHIPS, chunk, jnp.zeros((LANES, NS), F32))


def mixer(core, own, recv, layer):
    rows = own.shape[0]
    return pl.pallas_call(
        mixer_kernel,
        out_shape=(
            jax.ShapeDtypeStruct((rows, LANES), BF),
            jax.ShapeDtypeStruct((rows, LANES), BF),
            jax.ShapeDtypeStruct((CHIPS, LANES, NS), F32),
        ),
        in_specs=scalar_first(5),
        out_specs=tuple(whole_vmem(3)),
        scratch_shapes=[pltpu.VMEM((CHUNK + 8, CONVED), F32)],
        compiler_params=params(),
        cost_estimate=pl.CostEstimate(
            flops=8 * 10**9, bytes_accessed=2 * 10**6, transcendentals=10**6
        ),
    )(core, own, recv, layer["conv"], layer["cols"], layer["sel"])


def mixer_back_kernel(
    core_ref,
    own_ref,
    recv_ref,
    conv_ref,
    cols_ref,
    sel_ref,
    starts_ref,
    grad_own_ref,
    grad_recv_ref,
    mine_ref,
    theirs_ref,
    conv_grad_ref,
    cols_grad_ref,
    ext,
    later,
):
    core = core_ref[0]
    later[...] = jnp.zeros((CHUNK + 8, CONVED), F32)
    conv_grad_ref[...] = jnp.zeros((8, CONVED), F32)
    cols_grad_ref[...] = jnp.zeros((8, LANES), F32)
    ones = jnp.ones((CHUNK, LANES), BF)
    lanes = lax.broadcasted_iota(jnp.int32, (CHUNK, LANES), 1)

    def chunk(turn, grad_state):
        k = CHIPS - 1 - turn
        first, second = chunk_rows(core, own_ref, recv_ref, k)
        ext[8 : 8 + BLOCK, :] = first
        ext[8 + BLOCK : 8 + CHUNK, :] = second
        before = jnp.maximum(k - 1, 0)
        at_end = pl.ds(pl.multiple_of(before * BLOCK + BLOCK - 16, 16), 16)
        own_end = jnp.concatenate(
            [own_ref[at_end, 0:LANES], own_ref[at_end, 3 * LANES : 5 * LANES]], axis=1
        ).astype(F32)
        recv_end = recv_ref[at_end, 0:CONVED].astype(F32)
        end = jnp.where(core == 0, recv_end, own_end)[8:16, :]
        ext[0:8, :] = jnp.where(k > 0, end, 0.0)
        (
            conv,
            sig,
            states_in,
            input_map,
            output_map,
            raw,
            step,
            log_decay,
            lower,
            cumulative,
            weighted,
            coupling,
            within,
            last,
            tail,
            decay,
        ) = chunk_parts(ext, conv_ref, cols_ref, sel_ref)
        start = starts_ref[k]
        start_low = start.astype(BF)
        at = pl.ds(pl.multiple_of(k * BLOCK, BLOCK), BLOCK)
        grad_mine = grad_own_ref[at, :].astype(F32)
        grad_theirs = grad_recv_ref[at, :].astype(F32)
        grad = jnp.concatenate(
            [
                jnp.where(core == 0, grad_mine, grad_theirs),
                jnp.where(core == 0, grad_theirs, grad_mine),
            ],
            axis=0,
        )
        grad_states = cols_ref[2:3, :] * grad
        grad_skip = jnp.sum(grad * states_in, axis=0, keepdims=True)
        grown = grad * jnp.exp(cumulative)
        grown_low = grown.astype(BF)
        grad_out_map = dot_plain(grown_low, start_low)
        grad_start = dot_rows(grown_low, output_map)
        grad_cum = grown * dot_back(output_map, start_low)
        grad_coupling = jnp.zeros((CHUNK, CHUNK), F32)
        grad_weighted = jnp.zeros((CHUNK, LANES), F32)
        for head in range(2):
            member = cols_ref[3 + head : 4 + head, :]
            grad_head = (grad * member).astype(BF)
            grad_mixing = dot_back(grad_head, weighted.astype(BF))
            mixing = within[head] * coupling
            grad_weighted = grad_weighted + dot_rows(mixing.astype(BF), grad_head)
            grad_coupling = grad_coupling + grad_mixing * within[head]
            pairs = (grad_mixing * mixing).astype(BF)
            change = dot_plain(pairs, ones) - dot_rows(pairs, ones)
            grad_cum = grad_cum + jnp.where(lanes == head * (NARROW - 1), change, 0.0)
        coupling_low = grad_coupling.astype(BF)
        grad_out_map = grad_out_map + dot_plain(coupling_low, input_map)
        grad_in_map = dot_rows(coupling_low, output_map)
        state_low = grad_state.astype(BF)
        tailed = weighted * tail
        grad_in_map = grad_in_map + dot_plain(tailed.astype(BF), state_low)
        reach = dot_back(input_map, state_low)
        grad_weighted = grad_weighted + reach * tail
        moved = reach * tailed
        grad_cum = grad_cum - moved
        kept = exact(jnp.ones((8, NS), F32), grad_state * start, (1, 1))[0:1, :]
        grad_last = jnp.sum(moved, axis=0, keepdims=True) + kept * jnp.exp(last)
        grad_log = exact(lower, grad_cum, (0, 0)) + grad_last
        grad_step = grad_weighted * states_in - cols_ref[1:2, :] * grad_log
        grad_states = grad_states + grad_weighted * step
        grad_raw = grad_step / (1.0 + jnp.exp(-raw))
        cols_grad_ref[0:1, :] += jnp.sum(grad_raw, axis=0, keepdims=True)
        cols_grad_ref[1:2, :] += jnp.sum(grad_log * log_decay, axis=0, keepdims=True)
        cols_grad_ref[2:3, :] += grad_skip
        grad_dt = exact(grad_raw, sel_ref[...].astype(F32), (1, 1))
        slope = sig * (1.0 + conv * (1.0 - sig))
        grad_conv = jnp.concatenate([grad_states, grad_in_map, grad_out_map], axis=1) * slope
        later[CHUNK : CHUNK + 8, :] = later[0:8, :]
        later[0:CHUNK, :] = grad_conv
        conv_grad_ref[CONV : CONV + 1, :] += jnp.sum(grad_conv, axis=0, keepdims=True)
        grad_in = jnp.zeros((CHUNK, CONVED), F32)
        for j in range(CONV):
            low = 8 - (CONV - 1) + j
            conv_grad_ref[j : j + 1, :] += jnp.sum(
                grad_conv * ext[low : low + CHUNK, :], axis=0, keepdims=True
            )
            ahead = CONV - 1 - j
            grad_in = grad_in + conv_ref[j : j + 1, :] * later[ahead : ahead + CHUNK, :]
        grad_in = jnp.concatenate([grad_in[:, 0:LANES] + grad_dt, grad_in[:, LANES:]], axis=1)
        low, high = grad_in[:BLOCK, :], grad_in[BLOCK:, :]
        mine_ref[at, :] = jnp.where(core == 0, low, high)
        theirs_ref[at, :] = jnp.where(core == 0, high, low).astype(BF)
        return decay * grad_state + grad_start

    lax.fori_loop(0, CHIPS, chunk, jnp.zeros((LANES, NS), F32))


def mixer_back(core, own, recv, layer, starts, grad_own, grad_recv):
    rows = own.shape[0]
    return pl.pallas_call(
        mixer_back_kernel,
        out_shape=(
            jax.ShapeDtypeStruct((rows, CONVED), F32),
            jax.ShapeDtypeStruct((rows, CONVED), BF),
            jax.ShapeDtypeStruct((8, CONVED), F32),
            jax.ShapeDtypeStruct((8, LANES), F32),
        ),
        in_specs=scalar_first(8),
        out_specs=tuple(whole_vmem(4)),
        scratch_shapes=[pltpu.VMEM((CHUNK + 8, CONVED), F32)] * 2,
        compiler_params=params(),
        cost_estimate=pl.CostEstimate(
            flops=16 * 10**9, bytes_accessed=4 * 10**6, transcendentals=10**6
        ),
    )(core, own, recv, layer["conv"], layer["cols"], layer["sel"], starts, grad_own, grad_recv)


def seen(core, part, rows, columns):
    row = lax.broadcasted_iota(jnp.int32, (rows, columns), 0) + part * rows
    col = lax.broadcasted_iota(jnp.int32, (rows, columns), 1)
    half = columns // 2
    query_at = (row // BLOCK * 2 + core) * BLOCK + row % BLOCK
    other = col // half
    key = col - other * half
    key_at = (key // BLOCK * 2 + jnp.where(other == 0, core, 1 - core)) * BLOCK + key % BLOCK
    return key_at <= query_at


def keys_values(own_ref, recv_ref):
    both = jnp.concatenate([own_ref[:, 5 * LANES :], recv_ref[:, CONVED:]], axis=0)
    return both[:, :ATTN_HEAD_SIZE], both[:, ATTN_HEAD_SIZE:]


def attend_kernel(core_ref, own_ref, recv_ref, out_ref, stat_ref):
    core = core_ref[0]
    keys, values = keys_values(own_ref, recv_ref)
    for part in range(own_ref.shape[0] // CHUNK):
        at = slice(part * CHUNK, (part + 1) * CHUNK)
        query = own_ref[at, LANES : LANES + ATTN_HEAD_SIZE]
        scores = dot_back(query, keys) * RATIO
        scores = jnp.where(seen(core, part, *scores.shape), scores, -1e30)
        top = jnp.max(scores, axis=1, keepdims=True)
        grown = jnp.exp(scores - top)
        total = jnp.sum(grown, axis=1, keepdims=True)
        soft = grown / total
        out_ref[at, :] = dot_plain(soft.astype(BF), values).astype(BF)
        stat_ref[at, :] = jnp.broadcast_to(top + jnp.log(total), (CHUNK, LANES))


def attend(core, own, recv):
    rows = own.shape[0]
    return pl.pallas_call(
        attend_kernel,
        out_shape=(
            jax.ShapeDtypeStruct((rows, ATTN_HEAD_SIZE), BF),
            jax.ShapeDtypeStruct((rows, LANES), F32),
        ),
        in_specs=scalar_first(2),
        out_specs=tuple(whole_vmem(2)),
        compiler_params=params(),
        cost_estimate=pl.CostEstimate(
            flops=3 * 10**9, bytes_accessed=2 * 10**6, transcendentals=10**6
        ),
    )(core, own, recv)


def attend_back_kernel(
    core_ref, own_ref, recv_ref, stat_ref, grad_ref, query_ref, mine_ref, theirs_ref, total
):
    core = core_ref[0]
    keys, values = keys_values(own_ref, recv_ref)
    total[...] = jnp.zeros(total.shape, F32)
    half = own_ref.shape[0]
    for part in range(half // CHUNK):
        at = slice(part * CHUNK, (part + 1) * CHUNK)
        query = own_ref[at, LANES : LANES + ATTN_HEAD_SIZE]
        grad = grad_ref[at, :]
        scores = dot_back(query, keys) * RATIO
        visible = seen(core, part, *scores.shape)
        soft = jnp.where(visible, jnp.exp(scores - stat_ref[at, 0:1]), 0.0)
        grad_soft = dot_back(grad, values)
        row_total = jnp.sum(soft * grad_soft, axis=1, keepdims=True)
        grad_scores = (soft * (grad_soft - row_total)).astype(BF)
        query_grad = dot_plain(grad_scores, keys) * RATIO
        query_ref[at, :] = jnp.concatenate([query_grad, jnp.zeros_like(query_grad)], axis=1)
        key_grad = dot_rows(grad_scores, query) * RATIO
        value_grad = dot_rows(soft.astype(BF), grad)
        total[...] += jnp.concatenate([key_grad, value_grad], axis=1)
    mine_ref[...] = total[:half, :]
    theirs_ref[...] = total[half:, :].astype(BF)


def attend_back(core, own, recv, stat, grad):
    rows = own.shape[0]
    return pl.pallas_call(
        attend_back_kernel,
        out_shape=(
            jax.ShapeDtypeStruct((rows, LANES), F32),
            jax.ShapeDtypeStruct((rows, LANES), F32),
            jax.ShapeDtypeStruct((rows, LANES), BF),
        ),
        in_specs=scalar_first(4),
        out_specs=tuple(whole_vmem(3)),
        scratch_shapes=[pltpu.VMEM((2 * rows, LANES), F32)],
        compiler_params=params(),
        cost_estimate=pl.CostEstimate(
            flops=6 * 10**9, bytes_accessed=2 * 10**6, transcendentals=10**6
        ),
    )(core, own, recv, stat, grad)


def forward_mixer(x, layer, core):
    unit, scale = normalize(x)
    own_unit = spread(unit.astype(BF))
    weights = layer["in"]
    own = dot_plain(own_unit, weights[:, 2 * LANES :]).astype(BF)
    recv = swap_cores(own[:, 2 * LANES :])
    gate_raw = dot_plain(own_unit, weights[:, : 2 * LANES])
    attended, stat = attend(core, own, recv)
    attention = collect(dot_plain(attended, layer["out"]))
    mine, theirs, starts = mixer(core, own, recv, layer)
    mixed = jnp.concatenate([mine, swap_cores(theirs)], axis=1).astype(F32)
    gated = mixed * jax.nn.silu(gate_raw)
    squares = jnp.sum(gated * gated, axis=-1, keepdims=True)
    gained = (gated * layer["gain"]).astype(BF)
    high, low = two_parts(squares)
    lanes = lax.broadcasted_iota(jnp.int32, (gated.shape[0], LANES), 1)
    marks = jnp.where(lanes == 0, high, jnp.where(lanes == 1, low, jnp.zeros((), BF)))
    partial = jnp.concatenate([dot_plain(gained, layer["mamba"]).astype(BF), marks], axis=1)
    total = collect(partial)
    mamba = total[:, :MODEL_WIDTH]
    square = total[:, MODEL_WIDTH : MODEL_WIDTH + 1] + total[:, MODEL_WIDTH + 1 : MODEL_WIDTH + 2]
    ssm_scale = lax.rsqrt(square / INNER + EPSILON)
    hidden = x + ssm_scale * mamba + attention
    kept = (
        unit,
        scale,
        own_unit,
        own,
        recv,
        gate_raw,
        attended,
        stat,
        starts,
        mixed,
        gated,
        gained,
        mamba,
        ssm_scale,
    )
    return hidden, kept


def forward_wide(hidden, layer):
    unit, scale = normalize(hidden)
    own_unit = spread(unit.astype(BF))
    both = dot_plain(own_unit, layer["wide"])
    gate_val = both[:, : 2 * FF_CORE]
    up_val = both[:, 2 * FF_CORE :]
    swish = (jax.nn.silu(gate_val) * up_val).astype(BF)
    return dot_plain(swish, layer["down"]), (unit, scale, own_unit, gate_val, up_val, swish)


def backward_wide(grad_out, grad_out_own, kept, layer):
    unit, scale, own_unit, gate_val, up_val, swish = kept
    grad_swish = dot_back(grad_out_own, layer["down"])
    sig = jax.nn.sigmoid(gate_val)
    grad_gate = grad_swish * up_val * (sig * (1.0 + gate_val * (1.0 - sig)))
    grad_up = grad_swish * (gate_val * sig)
    grad_both = jnp.concatenate([grad_gate, grad_up], axis=1).astype(BF)
    grad_unit = collect(dot_back(grad_both, layer["wide"]))
    grad_hidden = grad_out + normalize_back(unit, scale, grad_unit)
    return grad_hidden, dot_rows(own_unit, grad_both), dot_rows(swish, grad_out_own)


def backward_mixer(grad_hidden, kept, layer, core):
    (
        unit,
        scale,
        own_unit,
        own,
        recv,
        gate_raw,
        attended,
        stat,
        starts,
        mixed,
        gated,
        gained,
        mamba,
        ssm_scale,
    ) = kept
    grad_low = grad_hidden.astype(BF)
    inner = jnp.sum(grad_low.astype(F32) * mamba, axis=-1, keepdims=True)
    pull_back = ssm_scale * ssm_scale * ssm_scale * inner / INNER
    rows = grad_low.shape[0]
    sent = jnp.concatenate(
        [grad_low, *two_parts(ssm_scale), *two_parts(pull_back), jnp.zeros((rows, 124), BF)],
        axis=1,
    )
    met = spread(sent)
    grad_own = met[:, :MODEL_WIDTH]
    extra = met[:, MODEL_WIDTH : MODEL_WIDTH + 4].astype(F32)
    scale_own = extra[:, 0:1] + extra[:, 1:2]
    pull_own = extra[:, 2:3] + extra[:, 3:4]
    grad_mixer = dot_back(grad_own, layer["mamba"])
    grad_attended = dot_back(grad_own, layer["out"]).astype(BF)
    grad_gated = scale_own * layer["gain"] * grad_mixer - gated * pull_own
    sig = jax.nn.sigmoid(gate_raw)
    grad_mixed = (grad_gated * gate_raw * sig).astype(BF)
    grad_gate_raw = grad_gated * mixed * (sig * (1.0 + gate_raw * (1.0 - sig)))
    grad_recv = swap_cores(grad_mixed[:, LANES:])
    grad_query, key_mine, key_theirs = attend_back(core, own, recv, stat, grad_attended)
    mine, theirs, conv_grad, cols_grad = mixer_back(
        core, own, recv, layer, starts, grad_mixed[:, :LANES], grad_recv
    )
    other = swap_cores(jnp.concatenate([theirs, key_theirs], axis=1)).astype(F32)
    mixer_low = (gained.astype(F32) * scale_own).astype(BF)
    grad_mamba = dot_rows(mixer_low, grad_own)
    grad_out = dot_rows(attended, grad_own)
    grad_gain = jnp.sum(grad_mixer * gated * scale_own, axis=0)
    grad_project = jnp.concatenate(
        [
            grad_gate_raw,
            mine[:, :LANES],
            grad_query,
            other[:, :LANES],
            mine[:, LANES:] + other[:, LANES:CONVED],
            key_mine + other[:, CONVED:],
        ],
        axis=1,
    ).astype(BF)
    grad_unit = collect(dot_back(grad_project, layer["in"]))
    grad_x = grad_hidden + normalize_back(unit, scale, grad_unit)
    grad_in = dot_rows(own_unit, grad_project)
    return grad_x, grad_in, grad_mamba, grad_out, grad_gain, conv_grad, cols_grad


def cut_in(w_in, query_weight, key_weight, value_weight, first_spare, second_spare):
    rows = w_in.shape[0]

    def even(w):
        return w.reshape(rows, SHARDS, -1).transpose(1, 0, 2)

    def by_core(w):
        return jnp.tile(w.reshape(rows, CORES, -1).transpose(1, 0, 2), (CHIPS, 1, 1))

    def by_key_head(w):
        groups = CHIPS // KEY_VALUE_HEADS
        cut = w.reshape(rows, KEY_VALUE_HEADS, CORES, -1).transpose(1, 2, 0, 3)
        cut = jnp.broadcast_to(cut[:, None], (KEY_VALUE_HEADS, groups) + cut.shape[1:])
        return cut.reshape((SHARDS,) + cut.shape[3:])

    maps = 2 * INNER + 2 * NS
    steps = jnp.broadcast_to(w_in[None, :, maps:], (SHARDS, rows, NH))
    return jnp.concatenate(
        [
            even(w_in[:, :INNER]),
            first_spare,
            even(w_in[:, INNER : 2 * INNER]),
            steps,
            jnp.zeros((SHARDS, rows, LANES - NARROW - NH), BF),
            by_core(w_in[:, 2 * INNER : maps]),
            even(query_weight),
            by_key_head(key_weight),
            by_key_head(value_weight),
            second_spare,
        ],
        axis=2,
    )


def cut_wide(w_gate, w_up):
    rows = w_gate.shape[0]
    both = [w.reshape(rows, SHARDS, FF_CORE).transpose(1, 0, 2) for w in (w_gate, w_up)]
    return jnp.concatenate(both, axis=2)


def body(
    inputs,
    cotangent,
    norm_in,
    w_in,
    conv_w,
    conv_b,
    dt_bias,
    a_log,
    skip_gain,
    norm_ssm,
    w_out,
    query_weight,
    key_weight,
    value_weight,
    output_weight,
    norm_mid,
    w_gate,
    w_up,
    w_down,
):
    place = lax.axis_index("shard")
    core = place % CORES
    core_word = core.reshape(1).astype(jnp.int32)
    section = lax.axis_index("section")
    reps = lax.axis_size("rep")
    local = inputs.shape[2]
    spare = LANES - NARROW

    gain_in = norm_in[0].astype(F32)[:, None]
    gain_mid = norm_mid[0].astype(F32)[:, None]

    def scaled(w, gain):
        return (w[0].astype(F32) * gain).astype(BF)

    conv_all = jnp.concatenate([conv_w[0], conv_b], axis=0)
    conv_count = conv_all.size
    conv_cols = jnp.concatenate(
        [conv_all.reshape(-1), jnp.zeros((spare * local - conv_count,), BF)]
    ).reshape(1, local, spare)
    cut = cut_in(
        scaled(w_in, gain_in),
        scaled(query_weight, gain_in),
        scaled(key_weight, gain_in),
        scaled(value_weight, gain_in),
        jnp.broadcast_to(conv_cols, (SHARDS, local, spare)),
        jnp.zeros((SHARDS, local, LANES - 3 * HALF_HEAD), BF),
    )
    everywhere = ("section", "shard")
    met = lax.all_to_all(jnp.concatenate([cut, cut], axis=0), everywhere, 0, 0, tiled=True)
    met = met.reshape(2, SHARDS, local, IN_COLS)
    conv_met = met[:, :, :, NARROW:LANES].reshape(2, SHARDS, spare * local)[:, :, :conv_count]
    conv_met = conv_met.reshape(2, SHARDS, CONV + 1, -1).transpose(0, 2, 1, 3)
    conv_met = conv_met.reshape(2, CONV + 1, INNER + 2 * NS).astype(F32)
    own_cols = met.reshape(2, SHARDS * local, IN_COLS)
    other_cols = swap_cores(own_cols)
    cut = cut_wide(scaled(w_gate, gain_mid), scaled(w_up, gain_mid))
    wide_cols = lax.all_to_all(jnp.concatenate([cut, cut], axis=0), everywhere, 0, 0, tiled=True)
    wide_cols = wide_cols.reshape(2, SHARDS * local, WIDE_COLS)
    other_wide = swap_cores(wide_cols)

    def both_layers(own):
        other = swap_sections(own)
        return jnp.where(section == 0, jnp.stack([own, other]), jnp.stack([other, own]))

    row_weights = both_layers(jnp.concatenate([w_out[0], output_weight[0], w_down[0]], axis=0))
    other_rows = swap_cores(row_weights)
    out_row, down_row = NARROW, NARROW + HALF_HEAD
    per_head = jnp.concatenate([dt_bias[0], a_log[0], skip_gain[0], norm_ssm[0].astype(F32)])
    per_head = both_layers(per_head)
    own_gain = per_head[:, 3 * NH :]
    other_gain = swap_cores(own_gain)
    lane = lax.broadcasted_iota(jnp.int32, (NH, LANES), 1)
    head_of = jnp.where(lane < NARROW, (lane + place * NARROW) // HD, -1)
    member = (head_of == lax.broadcasted_iota(jnp.int32, (NH, LANES), 0)).astype(F32)
    sel = jnp.concatenate(
        [jnp.zeros((NARROW, LANES), F32), member, jnp.zeros((LANES - NARROW - NH, LANES), F32)]
    ).astype(BF)
    in_first = (head_of[0:1] == head_of[0:1, 0:1]).astype(F32)
    in_second = (head_of[0:1] == head_of[0:1, NARROW - 1 : NARROW]).astype(F32)

    def to_columns(values):
        return jnp.sum(values[:, None] * member, axis=0, keepdims=True)

    def padded(g):
        return jnp.concatenate([g, jnp.zeros((spare,), F32)])

    no_rows = jnp.zeros((spare, MODEL_WIDTH), BF)
    layers = []
    for layer in range(2):
        mine, theirs = own_cols[layer], other_cols[layer]
        block = [slice(k * LANES, (k + 1) * LANES) for k in range(4)]

        def paired(at):
            low = 3 * LANES + at * HALF_HEAD
            cols = slice(low, low + HALF_HEAD)
            return by_place(core, mine[:, cols], theirs[:, cols], 1)

        head_values = per_head[layer]
        cols = jnp.concatenate(
            [
                to_columns(head_values[:NH]),
                to_columns(jnp.exp(head_values[NH : 2 * NH])),
                to_columns(head_values[2 * NH : 3 * NH]),
                in_first,
                in_second,
                jnp.zeros((3, LANES), F32),
            ]
        )
        conv_own = jnp.concatenate(
            [
                lax.dynamic_slice_in_dim(conv_met[layer], place * NARROW, NARROW, axis=1),
                jnp.zeros((CONV + 1, spare), F32),
                conv_met[layer, :, INNER:],
            ],
            axis=1,
        )
        rows, others = row_weights[layer], other_rows[layer]
        layers.append(
            {
                "in": jnp.concatenate(
                    [
                        mine[:, block[0]],
                        theirs[:, block[0]],
                        mine[:, block[1]],
                        paired(0),
                        jnp.zeros((SHARDS * local, LANES - ATTN_HEAD_SIZE), BF),
                        theirs[:, block[1]],
                        by_place(core, mine[:, block[2]], theirs[:, block[2]], 1),
                        paired(1),
                        paired(2),
                    ],
                    axis=1,
                ),
                "wide": jnp.concatenate(
                    [
                        wide_cols[layer, :, :FF_CORE],
                        other_wide[layer, :, :FF_CORE],
                        wide_cols[layer, :, FF_CORE:],
                        other_wide[layer, :, FF_CORE:],
                    ],
                    axis=1,
                ),
                "mamba": jnp.concatenate([rows[:out_row], no_rows, others[:out_row], no_rows]),
                "out": by_place(core, rows[out_row:down_row], others[out_row:down_row], 0),
                "down": jnp.concatenate([rows[down_row:], others[down_row:]]),
                "conv": jnp.concatenate([conv_own, jnp.zeros((7 - CONV, CONVED), F32)]),
                "cols": cols,
                "sel": sel,
                "gain": jnp.concatenate([padded(own_gain[layer]), padded(other_gain[layer])])[None],
            }
        )

    own_input = lax.dynamic_index_in_dim(inputs[:, 0], section, 0, False).astype(F32)
    own_target = lax.dynamic_index_in_dim(cotangent[:, 0], section, 0, False)
    x = own_input
    outs = []
    kept_mixer, kept_wide = [], []
    for layer in range(2):
        hidden, kept = forward_mixer(x, layers[layer], core_word)
        kept_mixer.append(kept)
        partial, kept = forward_wide(hidden, layers[layer])
        kept_wide.append(kept)
        outs.append((hidden + collect(partial)).astype(BF))
        x = outs[layer].astype(F32)

    grad = own_target.astype(F32)
    grads = [None, None]
    input_grads = [None, None]
    for layer in (1, 0):
        grad_own = spread(grad.astype(BF))
        grad_hidden, grad_wide, grad_down = backward_wide(
            grad, grad_own, kept_wide[layer], layers[layer]
        )
        grad_x, *rest = backward_mixer(grad_hidden, kept_mixer[layer], layers[layer], core_word)
        input_grads[layer] = grad_x
        grad = grad_x.astype(BF).astype(F32)
        grads[layer] = (grad_wide, grad_down, *rest)

    def exchanged(first, second):
        own = jnp.where(section == 0, first, second)
        other = swap_sections(jnp.where(section == 0, second, first).astype(BF))
        other = other.astype(own.dtype)
        return jnp.where(section == 0, jnp.stack([own, other]), jnp.stack([other, own]))

    section_out = exchanged(*outs)[None, :, None]
    input_grad = exchanged(*input_grads)[None, :, None]

    row_grads = []
    for layer in range(2):
        _, grad_down, _, grad_mamba, grad_out, _, _, _ = grads[layer]
        out_first, out_second = grad_out[:HALF_HEAD], grad_out[HALF_HEAD:]
        mine = jnp.concatenate(
            [
                grad_mamba[:NARROW],
                jnp.where(core == 0, out_first, out_second),
                grad_down[:FF_CORE],
            ]
        )
        theirs = jnp.concatenate(
            [
                grad_mamba[LANES : LANES + NARROW],
                jnp.where(core == 0, out_second, out_first),
                grad_down[FF_CORE:],
            ]
        )
        row_grads.append((mine + swap_cores(theirs.astype(BF)).astype(F32)).astype(BF))
    met = lax.all_to_all(jnp.concatenate(row_grads), ("section", "rep"), 0, 0, tiled=True)
    row_total = jnp.sum(met.reshape(2 * reps, -1, MODEL_WIDTH).astype(F32), axis=0).astype(BF)
    copies = jnp.broadcast_to(row_total[None], (reps,) + row_total.shape)
    row_total = lax.all_to_all(copies, "rep", 0, 0, tiled=True)
    row_total = row_total.reshape(-1, MODEL_WIDTH).astype(F32)

    part = local // reps
    all_cols = IN_COLS + WIDE_COLS
    sent = []
    for layer in range(2):
        grad_wide, _, grad_in, _, _, grad_gain, conv_grad, cols_grad = grads[layer]
        blocks = [grad_in[:, k * LANES : (k + 1) * LANES].astype(BF) for k in range(8)]
        wide = [grad_wide[:, k * LANES : (k + 1) * LANES].astype(BF) for k in range(4)]
        heads = [
            jnp.concatenate(
                [
                    blocks[3][:, low : low + HALF_HEAD],
                    blocks[7][:, low : low + HALF_HEAD],
                    blocks[7][:, low + ATTN_HEAD_SIZE : low + ATTN_HEAD_SIZE + HALF_HEAD],
                    jnp.zeros((blocks[3].shape[0], LANES - 3 * HALF_HEAD), BF),
                ],
                axis=1,
            )
            for low in (0, HALF_HEAD)
        ]
        mine = jnp.concatenate(
            [
                blocks[0],
                blocks[2],
                jnp.where(core == 0, blocks[5], blocks[6]),
                jnp.where(core == 0, heads[0], heads[1]),
                wide[0],
                wide[2],
            ],
            axis=1,
        )
        theirs = jnp.concatenate(
            [
                blocks[1],
                blocks[4],
                jnp.where(core == 0, blocks[6], blocks[5]),
                jnp.where(core == 0, heads[1], heads[0]),
                wide[1],
                wide[3],
            ],
            axis=1,
        )
        mine = (mine.astype(F32) + swap_cores(theirs).astype(F32)).astype(BF)
        mine = mine.reshape(SHARDS, reps, part, all_cols).transpose(1, 0, 2, 3)
        conv_grad = conv_grad[: CONV + 1]
        conv_grad = jnp.concatenate(
            [
                lax.dynamic_update_slice_in_dim(
                    jnp.zeros((CONV + 1, INNER), F32), conv_grad[:, :NARROW], place * NARROW, axis=1
                ),
                conv_grad[:, LANES:],
            ],
            axis=1,
        )
        conv_grad = conv_grad.reshape(CONV + 1, SHARDS, -1).transpose(1, 0, 2).reshape(SHARDS, -1)
        gain_halves = by_place(core, grad_gain[:NARROW], grad_gain[LANES : LANES + NARROW], 0)
        gain_grad = lax.dynamic_update_slice_in_dim(
            jnp.zeros((INNER,), F32), gain_halves, (place // CORES) * CORES * NARROW, axis=0
        ).reshape(SHARDS, -1)
        head_grad = jnp.sum(cols_grad[:3, None, :] * member[None], axis=2).reshape(-1)
        head_high, head_low = two_parts(head_grad)
        extra = jnp.concatenate(
            [
                conv_grad.astype(BF),
                gain_grad.astype(BF),
                jnp.broadcast_to(head_high[None], (SHARDS, 3 * NH)),
                jnp.broadcast_to(head_low[None], (SHARDS, 3 * NH)),
            ],
            axis=1,
        )
        room = part * spare
        extra_count = extra.shape[1]
        extra = jnp.concatenate([extra, jnp.zeros((SHARDS, 2 * room - extra_count), BF)], axis=1)
        extra = extra.reshape(1, SHARDS, 2, part, spare)
        extra = jnp.broadcast_to(extra, (reps,) + extra.shape[1:])
        sent.append(
            jnp.concatenate(
                [
                    mine[..., :NARROW],
                    extra[:, :, 0],
                    mine[..., LANES : 3 * LANES + 3 * HALF_HEAD],
                    extra[:, :, 1],
                    mine[..., IN_COLS:],
                ],
                axis=3,
            )
        )
    sent = jnp.stack(sent).reshape(2 * reps * SHARDS, part, all_cols)
    met = lax.all_to_all(sent, ("section", "rep", "shard"), 0, 0, tiled=True)
    total = jnp.sum(met.reshape(2 * reps, SHARDS, part, all_cols).astype(F32), axis=0)
    tail_at = 3 * LANES + 3 * HALF_HEAD
    extra = jnp.concatenate(
        [
            jnp.sum(total[:, :, NARROW:LANES], axis=0).reshape(room),
            jnp.sum(total[:, :, tail_at:IN_COLS], axis=0).reshape(room),
        ]
    )
    conv_total = extra[:conv_count].reshape(CONV + 1, -1)
    gain_total = extra[conv_count : conv_count + NARROW]
    head_total = extra[conv_count + NARROW : extra_count]
    head_total = (head_total[: 3 * NH] + head_total[3 * NH :]).reshape(3, NH)

    def even(g):
        return g.transpose(1, 0, 2).reshape(part, -1)

    def by_key_head(g):
        groups = CHIPS // KEY_VALUE_HEADS
        g = jnp.sum(g.reshape(KEY_VALUE_HEADS, groups, CORES, part, -1), axis=1)
        return even(g.reshape(KEY_VALUE_HEADS * CORES, part, -1))

    maps = total[:, :, 2 * LANES : 3 * LANES].reshape(CHIPS, CORES, part, LANES)
    heads = [
        total[:, :, 3 * LANES + k * HALF_HEAD : 3 * LANES + (k + 1) * HALF_HEAD] for k in range(3)
    ]
    column_grads = jnp.concatenate(
        [
            even(total[:, :, :NARROW]),
            even(total[:, :, LANES : LANES + NARROW]),
            even(jnp.sum(maps, axis=0)),
            jnp.sum(total[:, :, LANES + NARROW : LANES + NARROW + NH], axis=0),
            even(heads[0]),
            by_key_head(heads[1]),
            by_key_head(heads[2]),
            even(total[:, :, IN_COLS : IN_COLS + FF_CORE]),
            even(total[:, :, IN_COLS + FF_CORE :]),
        ],
        axis=1,
    ).astype(BF)
    copies = jnp.broadcast_to(column_grads[None], (reps,) + column_grads.shape)
    column_grads = lax.all_to_all(copies, "rep", 0, 0, tiled=True)
    column_grads = column_grads.reshape(local, -1).astype(F32)
    raw = (w_in, query_weight, key_weight, value_weight, w_gate, w_up)
    plain, at = [], 0
    for w in raw:
        plain.append(column_grads[:, at : at + w.shape[2]])
        at += w.shape[2]
    dots = [jnp.sum(g * w[0].astype(F32), axis=1) for g, w in zip(plain, raw)]
    grad_norm_in = dots[0] + dots[1] + dots[2] + dots[3]
    grad_norm_mid = dots[4] + dots[5]
    by_rows = [g * gain for g, gain in zip(plain, (gain_in,) * 4 + (gain_mid,) * 2)]
    return (
        section_out,
        input_grad,
        grad_norm_in[None],
        by_rows[0][None],
        conv_total[:CONV][None],
        conv_total[CONV][None],
        head_total[0][None],
        head_total[1][None],
        head_total[2][None],
        gain_total[None],
        row_total[:out_row][None],
        by_rows[1][None],
        by_rows[2][None],
        by_rows[3][None],
        row_total[out_row:down_row][None],
        grad_norm_mid[None],
        by_rows[4][None],
        by_rows[5][None],
        row_total[down_row:][None],
    )


def solution(mesh):
    return jax.shard_map(
        body,
        mesh=mesh,
        in_specs=(
            P(None, "rep", "shard", None),
            P(None, "rep", "shard", None),
            P("section", "shard"),
            P("section", "shard", None),
            P("section", None, "shard"),
            P("section", "shard"),
            P("section", None),
            P("section", None),
            P("section", None),
            P("section", "shard"),
            P("section", "shard", None),
            P("section", "shard", None),
            P("section", "shard", None),
            P("section", "shard", None),
            P("section", "shard", None),
            P("section", "shard"),
            P("section", "shard", None),
            P("section", "shard", None),
            P("section", "shard", None),
        ),
        out_specs=(
            P("section", None, "rep", "shard", None),
            P("section", None, "rep", "shard", None),
            P("section", "shard"),
            P("section", "shard", None),
            P("section", None, "shard"),
            P("section", "shard"),
            P("section", None),
            P("section", None),
            P("section", None),
            P("section", "shard"),
            P("section", "shard", None),
            P("section", "shard", None),
            P("section", "shard", None),
            P("section", "shard", None),
            P("section", "shard", None),
            P("section", "shard"),
            P("section", "shard", None),
            P("section", "shard", None),
            P("section", "shard", None),
        ),
        check_vma=False,
    )
```

time: 2060 us -> 718 us (0.35)
  blocking collectives: 592 us -> 17.6 us
  waiting for transfers between devices: 581 us -> 241 us
  matrix products: 335 us -> 67 us
  other arithmetic: 259 us -> 80.3 us
  local copies, waits for them, and re-layouts: 223 us -> 125 us
  starting transfers between devices: 24.1 us -> 121 us
  Pallas kernels: 0 us -> 49.6 us
    reduce_scatter x9 -> x0, waiting for transfers between devices: 376 us -> none  [the longest x1 84.3 us: body(): lax.psum_scatter(dot_rows(normed_all, grad_project_all).astype(jnp.bfloat...]
    all_gather x15 -> x0, blocking collectives: 322 us -> none  [the longest x3 101 us: prefix_2(): lax.all_gather(a.astype(kind), axis)]
    dot_general x132 -> x22, matrix products: 291 us -> 46.7 us  [the longest x10 23.6 us: dot_back(): lax.dot_general(former, latter, (((1,), (1,)), ((), ())), preferred_eleme...]
    all_to_all x0 -> x23, waiting for transfers between devices: none -> 170 us  [the longest x9 97.3 us: collect(): lax.all_to_all(partial.astype(BF), 'shard', 0, 0, axis_index_groups=same_...]
    psum x2 -> x0, blocking collectives: 160 us -> none  [the longest x1 142 us: body(): lax.psum((grad_dt_shift, grad_log_rate, grad_skip_gain), ('rep', 'shard'))]
    unnamed x2 -> x0, blocking collectives: 110 us -> none
    all_to_all x0 -> x23, starting transfers between devices: none -> 105 us  [the longest x9 41.4 us: collect(): lax.all_to_all(partial.astype(BF), 'shard', 0, 0, axis_index_groups=same_...]
    unnamed x37 -> x0, waiting for transfers between devices: 92.7 us -> none
  transfers between devices with their start and end apart: 40 -> 43, of which waited for: 15 -> 22; matrix products, arithmetic and copies ran while one was open for 29% -> 29% of each run, Pallas kernels for 0% -> 4%
where the time goes in v1:
time: 718 us; the launch traced here: 706 us
  waiting for transfers between devices  241 us (34%)
  local copies, waits for them, and re-layouts  125 us (17%)
  starting transfers between devices  121 us (17%)
  other arithmetic  80.3 us (11%)
  matrix products  67 us (9%)
  Pallas kernels  49.6 us (7%)
  blocking collectives  17.6 us (2%)
    all_to_all x9, waiting for transfers between devices, collect(): lax.all_to_all(partial.astype(BF), 'shard', 0, 0, axis_index_groups=same_...  97.3 us
    ppermute x4, waiting for transfers between devices, swap_sections(): return lax.ppermute(x, 'section', [(0, 1), (1, 0)])  67.7 us
    all_to_all x8, waiting for transfers between devices, spread(): lax.all_to_all(copies, 'shard', 0, 0, axis_index_groups=same_core(), tile...  48.5 us
    all_to_all x9, starting transfers between devices, collect(): lax.all_to_all(partial.astype(BF), 'shard', 0, 0, axis_index_groups=same_...  41.4 us
    all_to_all x8, starting transfers between devices, spread(): lax.all_to_all(copies, 'shard', 0, 0, axis_index_groups=same_core(), tile...  33.1 us
    pallas_call x2, Pallas kernels, mixer_back(): pl.pallas_call(mixer_back_kernel, out_shape=(jax.ShapeDtypeStruct((rows,...  28.4 us
    dot_general x10, matrix products, dot_back(): lax.dot_general(former, latter, (((1,), (1,)), ((), ())), preferred_eleme...  23.6 us
    dot_general x12, matrix products, dot_plain(): return jnp.dot(former, latter, preferred_element_type=F32)  23.1 us
  transfers between devices with their start and end apart: 43, of which 22 were waited for; matrix products, arithmetic and copies ran while one was open for 29% of the time, Pallas kernels for 4%

profile of v1, /device:TPU:0, one launch (start us, length us, event | category | flops | bytes accessed | tf_op | source)
XLA Modules:
  0.0 705.7 jit_solution(16212651366459475034)
XLA Ops:
  32.2 29.2 %collective-permute-done.5 = bf16[256,1024]{1,0:T(8,128)(2,1)} collective-permute-done((bf16[256,1024]{1,0:T(8,128)(2,1)}, bf16[256,1024]{1,0:T(8,128)(2,1)}, u32[]{:S(2)}, u32[]{:S(2)}) %collective-permute-start.5) | collective-permute-done | bytes 524320 | tf_op jit(solution)/shard_map/ppermute | solution.py:67
  96.8 6.0 shard_map.330
  117.6 14.0 %all-to-all-done.3 = bf16[8,64,1024]{2,1,0:T(8,128)(2,1)S(1)} async-done(((bf16[8,64,1024]{2,1,0:T(8,128)(2,1)}), bf16[8,64,1024]{2,1,0:T(8,128)(2,1)S(1)}, u32[]{:S(2)}, u32[]{:S(2)}) %all-to-all-start.3) | async-done | bytes 1048608 | tf_op jit(solution)/shard_map/all_to_all | solution.py:82
  138.4 14.8 %all-to-all-done.2 = bf16[8,64,1152]{2,1,0:T(8,128)(2,1)S(1)} async-done(((bf16[8,64,1152]{2,1,0:T(8,128)(2,1)}), bf16[8,64,1152]{2,1,0:T(8,128)(2,1)S(1)}, u32[]{:S(2)}, u32[]{:S(2)}) %all-to-all-start.2) | async-done | bytes 1179680 | tf_op jit(solution)/shard_map/all_to_all | solution.py:82
  168.7 7.6 %all-to-all-done.4 = bf16[8,64,1024]{2,1,0:T(8,128)(2,1)} async-done(((bf16[8,64,1024]{2,1,0:T(8,128)(2,1)}), bf16[8,64,1024]{2,1,0:T(8,128)(2,1)}, u32[]{:S(2)}, u32[]{:S(2)}) %all-to-all-start.4) | async-done | bytes 1048608 | tf_op jit(solution)/shard_map/all_to_all | solution.py:77
  179.5 17.6 %all_to_all.196 = bf16[8,64,1024]{2,1,0:T(8,128)(2,1)S(1)} all-to-all(bf16[8,64,1024]{2,1,0:T(8,128)(2,1)S(1)} %bitcast.382), channel_id=1, replica_groups={{0,2,4,6,8,10,12,14},{1,3,5,7,9,11,13,15},{16,18,20,22,24,26,28,30},{17..., dimensions={0} | all-to-all | bytes 2097152 | tf_op jit(solution)/shard_map/all_to_all | solution.py:82
  222.5 6.0 shard_map.332
  242.3 12.4 %all-to-all-done.9 = bf16[8,64,1024]{2,1,0:T(8,128)(2,1)} async-done(((bf16[8,64,1024]{2,1,0:T(8,128)(2,1)}), bf16[8,64,1024]{2,1,0:T(8,128)(2,1)}, u32[]{:S(2)}, u32[]{:S(2)}) %all-to-all-start.9) | async-done | bytes 1048608 | tf_op jit(solution)/shard_map/all_to_all | solution.py:82
  261.0 15.8 %all-to-all-done.8 = bf16[8,64,1152]{2,1,0:T(8,128)(2,1)} async-done(((bf16[8,64,1152]{2,1,0:T(8,128)(2,1)}), bf16[8,64,1152]{2,1,0:T(8,128)(2,1)}, u32[]{:S(2)}, u32[]{:S(2)}) %all-to-all-start.8) | async-done | bytes 1179680 | tf_op jit(solution)/shard_map/all_to_all | solution.py:82
  286.4 14.2 %all-to-all-done.10 = bf16[8,64,1024]{2,1,0:T(8,128)(2,1)} async-done(((bf16[8,64,1024]{2,1,0:T(8,128)(2,1)}), bf16[8,64,1024]{2,1,0:T(8,128)(2,1)}, u32[]{:S(2)}, u32[]{:S(2)}) %all-to-all-start.10) | async-done | bytes 1048608 | tf_op jit(solution)/shard_map/all_to_all | solution.py:77
  310.2 11.3 %all-to-all-done.12 = bf16[8,64,1024]{2,1,0:T(8,128)(2,1)} async-done(((bf16[8,64,1024]{2,1,0:T(8,128)(2,1)}), bf16[8,64,1024]{2,1,0:T(8,128)(2,1)}, u32[]{:S(2)}, u32[]{:S(2)}) %all-to-all-start.12) | async-done | bytes 1048608 | tf_op jit(solution)/shard_map/all_to_all | solution.py:77
  331.1 13.3 %all-to-all-done.13 = bf16[8,64,1024]{2,1,0:T(8,128)(2,1)} async-done(((bf16[8,64,1024]{2,1,0:T(8,128)(2,1)}), bf16[8,64,1024]{2,1,0:T(8,128)(2,1)}, u32[]{:S(2)}, u32[]{:S(2)}) %all-to-all-start.13) | async-done | bytes 1048608 | tf_op jit(solution)/shard_map/all_to_all | solution.py:82
  391.0 14.2 %shard_map.334 = (f32[512,384]{1,0:T(8,128)S(1)}, bf16[512,384]{1,0:T(8,128)(2,1)S(1)}, f32[8,384]{1,0:T(8,128)S(1)}, f32[8,128]{1,0:T(8,128)S(1)}) custom-call(s32[1]{0:T(128)} %bitcast.1.core_ref, bf16[512,768]{1,0:T(8,128)(2,1)S(1)} %convolution_convert_fusion.14.own_ref, bf16[512,512]{1,0:T(8,128)(2,1)S(1)} %copy-done.3, ...), custom_call_target="tpu_custom_call" | custom-call | flops 16000000000 | bytes 4000000 | tf_op jit(solution)/shard_map/pallas_call | solution.py:378
  428.9 10.7 %all-to-all-done.15 = bf16[8,64,1024]{2,1,0:T(8,128)(2,1)S(1)} async-done(((bf16[8,64,1024]{2,1,0:T(8,128)(2,1)}), bf16[8,64,1024]{2,1,0:T(8,128)(2,1)S(1)}, u32[]{:S(2)}, u32[]{:S(2)}) %all-to-all-start.15) | async-done | bytes 1048608 | tf_op jit(solution)/shard_map/all_to_all | solution.py:82
  453.3 8.2 %all-to-all-done.16 = bf16[8,64,1024]{2,1,0:T(8,128)(2,1)S(1)} async-done(((bf16[8,64,1024]{2,1,0:T(8,128)(2,1)}), bf16[8,64,1024]{2,1,0:T(8,128)(2,1)S(1)}, u32[]{:S(2)}, u32[]{:S(2)}) %all-to-all-start.16) | async-done | bytes 1048608 | tf_op jit(solution)/shard_map/all_to_all | solution.py:77
  475.8 7.9 %all-to-all-done.17 = bf16[8,64,1024]{2,1,0:T(8,128)(2,1)S(1)} async-done(((bf16[8,64,1024]{2,1,0:T(8,128)(2,1)}), bf16[8,64,1024]{2,1,0:T(8,128)(2,1)S(1)}, u32[]{:S(2)}, u32[]{:S(2)}) %all-to-all-start.17) | async-done | bytes 1048608 | tf_op jit(solution)/shard_map/all_to_all | solution.py:82
  507.0 5.8 all-to-all-start.11
  527.6 14.2 %shard_map.336 = (f32[512,384]{1,0:T(8,128)S(1)}, bf16[512,384]{1,0:T(8,128)(2,1)S(1)}, f32[8,384]{1,0:T(8,128)S(1)}, f32[8,128]{1,0:T(8,128)S(1)}) custom-call(s32[1]{0:T(128)} %bitcast.1.core_ref, bf16[512,768]{1,0:T(8,128)(2,1)S(1)} %convolution_convert_fusion.15.own_ref, bf16[512,512]{1,0:T(8,128)(2,1)S(1)} %copy-done.1, ...), custom_call_target="tpu_custom_call" | custom-call | flops 16000000000 | bytes 4000000 | tf_op jit(solution)/shard_map/pallas_call | solution.py:378
  555.4 6.6 all-to-all-start.22
  569.7 10.1 %all-to-all-done.22 = bf16[8,64,1024]{2,1,0:T(8,128)(2,1)S(1)} async-done(((bf16[8,64,1024]{2,1,0:T(8,128)(2,1)}), bf16[8,64,1024]{2,1,0:T(8,128)(2,1)S(1)}, u32[]{:S(2)}, u32[]{:S(2)}) %all-to-all-start.22) | async-done | bytes 1048608 | tf_op jit(solution)/shard_map/all_to_all | solution.py:864
  592.3 8.5 %all-to-all-done.19 = bf16[8,64,1024]{2,1,0:T(8,128)(2,1)S(1)} async-done(((bf16[8,64,1024]{2,1,0:T(8,128)(2,1)}), bf16[8,64,1024]{2,1,0:T(8,128)(2,1)S(1)}, u32[]{:S(2)}, u32[]{:S(2)}) %all-to-all-start.19) | async-done | bytes 1048608 | tf_op jit(solution)/shard_map/all_to_all | solution.py:82
  619.6 6.3 all-to-all-start.20
  632.0 36.7 %collective-permute-done.10 = bf16[64,1024]{1,0:T(8,128)(2,1)S(1)} collective-permute-done((bf16[64,1024]{1,0:T(8,128)(2,1)S(1)}, bf16[64,1024]{1,0:T(8,128)(2,1)S(1)}, u32[]{:S(2)}, u32[]{:S(2)}) %collective-permute-start.10) | collective-permute-done | bytes 131104 | tf_op jit(solution)/shard_map/ppermute | solution.py:67
  685.7 12.7 %all-to-all-done.21 = bf16[4,16,8216]{2,1,0:T(8,128)(2,1)S(1)} async-done(((bf16[4,16,8216]{2,1,0:T(8,128)(2,1)}), bf16[4,16,8216]{2,1,0:T(8,128)(2,1)S(1)}, u32[]{:S(2)}, u32[]{:S(2)}) %all-to-all-start.21) | async-done | bytes 1051680 | tf_op jit(solution)/shard_map/all_to_all | solution.py:998
  (878 shorter events, 397.1 us)
Async XLA Ops:
  2.2 29.8 %collective-permute-start.2 = (f32[168]{0:T(256)S(1)}, f32[168]{0:T(256)S(1)}, u32[]{:S(2)}, u32[]{:S(2)}) collective-permute-start(f32[168]{0:T(256)S(1)} %pad_maximum_fusion.48), channel_id=1, source_target_pairs={{0,64},{64,0},{1,65},{65,1},{2,66},{66,2},{3,67},{67,3},{4,68},{68... | collective-permute-start | bytes 2024 | tf_op jit(solution)/shard_map/ppermute | solution.py:67
  15.6 48.5 %all-to-all-start.1 = ((bf16[32,64,512]{2,1,0:T(8,128)(2,1)}), bf16[32,64,512]{2,1,0:T(8,128)(2,1)S(1)}, u32[]{:S(2)}, u32[]{:S(2)}) async-start(bf16[32,64,512]{2,1,0:T(8,128)(2,1)} %pad_maximum_fusion.1), calls=%async_computation.1 | async-start | bytes 4194304 | tf_op jit(solution)/shard_map/all_to_all | solution.py:706
  22.2 39.1 %collective-permute-start.5 = (bf16[256,1024]{1,0:T(8,128)(2,1)}, bf16[256,1024]{1,0:T(8,128)(2,1)}, u32[]{:S(2)}, u32[]{:S(2)}) collective-permute-start(bf16[256,1024]{1,0:T(8,128)(2,1)} %get-tuple-element.399), channel_id=1, source_target_pairs={{0,64},{64,0},{1,65},{65,1},{2,66},{66,2},{3,67},{67,3},{4,68},{68... | collective-permute-start | bytes 1572872 | tf_op jit(solution)/shard_map/ppermute | solution.py:67
  32.1 37.9 %collective-permute-start.4 = (f32[2,96]{1,0:T(2,128)S(1)}, f32[2,96]{1,0:T(2,128)S(1)}, u32[]{:S(2)}, u32[]{:S(2)}) collective-permute-start(f32[2,96]{1,0:T(2,128)S(1)} %slice.1028), channel_id=1, source_target_pairs={{0,1},{1,0},{2,3},{3,2},{4,5},{5,4},{6,7},{7,6},{8,9},{9,8},{10,11... | collective-permute-start | bytes 2312 | tf_op jit(solution)/shard_map/ppermute | solution.py:63
  65.3 22.0 %all-to-all-start = ((bf16[8,64,1024]{2,1,0:T(8,128)(2,1)}), bf16[8,64,1024]{2,1,0:T(8,128)(2,1)}, u32[]{:S(2)}, u32[]{:S(2)}) async-start(bf16[8,64,1024]{2,1,0:T(8,128)(2,1)} %broadcast_in_dim.141), calls=%async_computation | async-start | bytes 2097152 | tf_op jit(solution)/shard_map/all_to_all | solution.py:77
  87.2 22.7 %all-to-all-start.5 = ((bf16[32,64,256]{2,1,0:T(8,128)(2,1)}), bf16[32,64,256]{2,1,0:T(8,128)(2,1)}, u32[]{:S(2)}, u32[]{:S(2)}) async-start(bf16[32,64,256]{2,1,0:T(8,128)(2,1)} %copy.516), calls=%async_computation.5 | async-start | bytes 2097152 | tf_op jit(solution)/shard_map/all_to_all | solution.py:714
  109.9 21.6 %all-to-all-start.3 = ((bf16[8,64,1024]{2,1,0:T(8,128)(2,1)}), bf16[8,64,1024]{2,1,0:T(8,128)(2,1)S(1)}, u32[]{:S(2)}, u32[]{:S(2)}) async-start(bf16[8,64,1024]{2,1,0:T(8,128)(2,1)} %bitcast.385), calls=%async_computation.3 | async-start | bytes 2097152 | tf_op jit(solution)/shard_map/all_to_all | solution.py:82
  132.6 20.6 %all-to-all-start.2 = ((bf16[8,64,1152]{2,1,0:T(8,128)(2,1)}), bf16[8,64,1152]{2,1,0:T(8,128)(2,1)S(1)}, u32[]{:S(2)}, u32[]{:S(2)}) async-start(bf16[8,64,1152]{2,1,0:T(8,128)(2,1)} %bitcast.49), calls=%async_computation.2 | async-start | bytes 2359296 | tf_op jit(solution)/shard_map/all_to_all | solution.py:82
  136.1 30.4 %collective-permute-start.7 = (bf16[2,1024,256]{2,1,0:T(8,128)(2,1)}, bf16[2,1024,256]{2,1,0:T(8,128)(2,1)}, u32[]{:S(2)}, u32[]{:S(2)}) collective-permute-start(bf16[2,1024,256]{2,1,0:T(8,128)(2,1)} %bitcast.58), channel_id=1, source_target_pairs={{0,1},{1,0},{2,3},{3,2},{4,5},{5,4},{6,7},{7,6},{8,9},{9,8},{10,11... | collective-permute-start | bytes 3145736 | tf_op jit(solution)/shard_map/ppermute | solution.py:63
  232.6 22.0 %all-to-all-start.9 = ((bf16[8,64,1024]{2,1,0:T(8,128)(2,1)}), bf16[8,64,1024]{2,1,0:T(8,128)(2,1)}, u32[]{:S(2)}, u32[]{:S(2)}) async-start(bf16[8,64,1024]{2,1,0:T(8,128)(2,1)} %bitcast.386), calls=%async_computation.9 | async-start | bytes 2097152 | tf_op jit(solution)/shard_map/all_to_all | solution.py:82
  254.6 22.2 %all-to-all-start.8 = ((bf16[8,64,1152]{2,1,0:T(8,128)(2,1)}), bf16[8,64,1152]{2,1,0:T(8,128)(2,1)}, u32[]{:S(2)}, u32[]{:S(2)}) async-start(bf16[8,64,1152]{2,1,0:T(8,128)(2,1)} %bitcast.380), calls=%async_computation.8 | async-start | bytes 2359296 | tf_op jit(solution)/shard_map/all_to_all | solution.py:82
  281.5 19.2 %all-to-all-start.10 = ((bf16[8,64,1024]{2,1,0:T(8,128)(2,1)}), bf16[8,64,1024]{2,1,0:T(8,128)(2,1)}, u32[]{:S(2)}, u32[]{:S(2)}) async-start(bf16[8,64,1024]{2,1,0:T(8,128)(2,1)} %broadcast_in_dim.296), calls=%async_computation.10 | async-start | bytes 2097152 | tf_op jit(solution)/shard_map/all_to_all | solution.py:77
  352.2 23.1 %all-to-all-start.14 = ((bf16[8,64,1152]{2,1,0:T(8,128)(2,1)}), bf16[8,64,1152]{2,1,0:T(8,128)(2,1)}, u32[]{:S(2)}, u32[]{:S(2)}) async-start(bf16[8,64,1152]{2,1,0:T(8,128)(2,1)} %broadcast_in_dim.299), calls=%async_computation.14 | async-start | bytes 2359296 | tf_op jit(solution)/shard_map/all_to_all | solution.py:77
  417.6 22.0 %all-to-all-start.15 = ((bf16[8,64,1024]{2,1,0:T(8,128)(2,1)}), bf16[8,64,1024]{2,1,0:T(8,128)(2,1)S(1)}, u32[]{:S(2)}, u32[]{:S(2)}) async-start(bf16[8,64,1024]{2,1,0:T(8,128)(2,1)} %bitcast.399), calls=%async_computation.15 | async-start | bytes 2097152 | tf_op jit(solution)/shard_map/all_to_all | solution.py:82
  472.9 19.3 %collective-permute-start.17 = (bf16[1024,768]{0,1:T(8,128)(2,1)}, bf16[1024,768]{0,1:T(8,128)(2,1)}, u32[]{:S(2)}, u32[]{:S(2)}) collective-permute-start(bf16[1024,768]{0,1:T(8,128)(2,1)} %get-tuple-element.346), channel_id=1, source_target_pairs={{0,1},{1,0},{2,3},{3,2},{4,5},{5,4},{6,7},{7,6},{8,9},{9,8},{10,11... | collective-permute-start | bytes 4718600 | tf_op jit(solution)/shard_map/ppermute | solution.py:63
  486.0 21.0 %all-to-all-start.18 = ((bf16[8,64,1152]{2,1,0:T(8,128)(2,1)}), bf16[8,64,1152]{2,1,0:T(8,128)(2,1)S(1)}, u32[]{:S(2)}, u32[]{:S(2)}) async-start(bf16[8,64,1152]{2,1,0:T(8,128)(2,1)} %broadcast_in_dim.302), calls=%async_computation.18 | async-start | bytes 2359296 | tf_op jit(solution)/shard_map/all_to_all | solution.py:77
  507.0 48.3 %all-to-all-start.11 = ((bf16[8,64,1024]{2,1,0:T(8,128)(2,1)}), bf16[8,64,1024]{2,1,0:T(8,128)(2,1)}, u32[]{:S(2)}, u32[]{:S(2)}) async-start(bf16[8,64,1024]{2,1,0:T(8,128)(2,1)} %bitcast.381), calls=%async_computation.11 | async-start | bytes 2097152 | tf_op jit(solution)/shard_map/all_to_all | solution.py:82
  523.3 21.3 %collective-permute-start.18 = (bf16[256,1024]{1,0:T(8,128)(2,1)}, bf16[256,1024]{1,0:T(8,128)(2,1)}, u32[]{:S(2)}, u32[]{:S(2)}) collective-permute-start(bf16[256,1024]{1,0:T(8,128)(2,1)} %pad_maximum_fusion.18), channel_id=1, source_target_pairs={{0,1},{1,0},{2,3},{3,2},{4,5},{5,4},{6,7},{7,6},{8,9},{9,8},{10,11... | collective-permute-start | bytes 1572872 | tf_op jit(solution)/shard_map/ppermute | solution.py:63
  555.4 24.5 %all-to-all-start.22 = ((bf16[8,64,1024]{2,1,0:T(8,128)(2,1)}), bf16[8,64,1024]{2,1,0:T(8,128)(2,1)S(1)}, u32[]{:S(2)}, u32[]{:S(2)}) async-start(bf16[8,64,1024]{2,1,0:T(8,128)(2,1)} %bitcast.151), calls=%async_computation.22 | async-start | bytes 2097152 | tf_op jit(solution)/shard_map/all_to_all | solution.py:864
  565.6 40.2 %collective-permute-start.16 = (bf16[1024,768]{0,1:T(8,128)(2,1)}, bf16[1024,768]{0,1:T(8,128)(2,1)}, u32[]{:S(2)}, u32[]{:S(2)}) collective-permute-start(bf16[1024,768]{0,1:T(8,128)(2,1)} %get-tuple-element.342), channel_id=1, source_target_pairs={{0,1},{1,0},{2,3},{3,2},{4,5},{5,4},{6,7},{7,6},{8,9},{9,8},{10,11... | collective-permute-start | bytes 4718600 | tf_op jit(solution)/shard_map/ppermute | solution.py:63
  579.8 20.9 %all-to-all-start.19 = ((bf16[8,64,1024]{2,1,0:T(8,128)(2,1)}), bf16[8,64,1024]{2,1,0:T(8,128)(2,1)S(1)}, u32[]{:S(2)}, u32[]{:S(2)}) async-start(bf16[8,64,1024]{2,1,0:T(8,128)(2,1)} %bitcast.397), calls=%async_computation.19 | async-start | bytes 2097152 | tf_op jit(solution)/shard_map/all_to_all | solution.py:82
  619.6 56.9 %all-to-all-start.20 = ((bf16[128,16,768]{2,1,0:T(8,128)(2,1)}), bf16[128,16,768]{2,1,0:T(8,128)(2,1)S(1)}, u32[]{:S(2)}, u32[]{:S(2)}) async-start(bf16[128,16,768]{2,1,0:T(8,128)(2,1)} %bitcast.123), calls=%async_computation.20 | async-start | bytes 6291456 | tf_op jit(solution)/shard_map/all_to_all | solution.py:957
  627.6 41.0 %collective-permute-start.10 = (bf16[64,1024]{1,0:T(8,128)(2,1)S(1)}, bf16[64,1024]{1,0:T(8,128)(2,1)S(1)}, u32[]{:S(2)}, u32[]{:S(2)}) collective-permute-start(bf16[64,1024]{1,0:T(8,128)(2,1)S(1)} %get-tuple-element.397), channel_id=1, source_target_pairs={{0,64},{64,0},{1,65},{65,1},{2,66},{66,2},{3,67},{67,3},{4,68},{68... | collective-permute-start | bytes 393224 | tf_op jit(solution)/shard_map/ppermute | solution.py:67
  631.2 40.0 %collective-permute-start.15 = (bf16[64,1024]{1,0:T(8,128)(2,1)S(1)}, bf16[64,1024]{1,0:T(8,128)(2,1)S(1)}, u32[]{:S(2)}, u32[]{:S(2)}) collective-permute-start(bf16[64,1024]{1,0:T(8,128)(2,1)S(1)} %select_convert_fusion), channel_id=1, source_target_pairs={{0,64},{64,0},{1,65},{65,1},{2,66},{66,2},{3,67},{67,3},{4,68},{68... | collective-permute-start | bytes 393224 | tf_op jit(solution)/shard_map/ppermute | solution.py:67
  (222 other events, 1817.9 us)

commit v2 on v1

v2 whole, which is shorter than its diff:
```python
import functools

import jax
import jax.numpy as jnp
from jax import lax
from jax.experimental import pallas as pl
from jax.experimental.pallas import tpu as pltpu
from jax.sharding import PartitionSpec as P

MODEL_WIDTH = 1024
NH = 24
HD = 64
NS = 128
QUERY_HEADS = 8
KEY_VALUE_HEADS = 2
ATTN_HEAD_SIZE = 64
FF = 2048
CONV = 4
MB = 2

EPSILON = 1e-05

SHARDS = 16
CORES = 2
CHIPS = SHARDS // CORES
INNER = NH * HD
NARROW = INNER // SHARDS
LANES = 128
HALF_HEAD = ATTN_HEAD_SIZE // 2
IN_COLS = 4 * LANES
WIDE_COLS = 2 * LANES
CONVED = 3 * LANES
CHUNK = 128
BLOCK = 64
FF_CORE = FF // SHARDS
RATIO = ATTN_HEAD_SIZE ** (-0.5)

BF = jnp.bfloat16
F32 = jnp.float32


def dot_plain(former, latter):
    return jnp.dot(former, latter, preferred_element_type=F32)


def dot_rows(former, latter):
    return lax.dot_general(former, latter, (((0,), (0,)), ((), ())), preferred_element_type=F32)


def dot_back(former, latter):
    return lax.dot_general(former, latter, (((1,), (1,)), ((), ())), preferred_element_type=F32)


def exact(former, latter, dims):
    return lax.dot_general(
        former,
        latter,
        ((dims[:1], dims[1:]), ((), ())),
        precision=lax.Precision.HIGHEST,
        preferred_element_type=F32,
    )


def swap_cores(x):
    return lax.ppermute(x, "shard", [(i, i ^ 1) for i in range(SHARDS)])


def swap_sections(x):
    return lax.ppermute(x, "section", [(0, 1), (1, 0)])


def same_core():
    return [list(range(core, SHARDS, CORES)) for core in range(CORES)]


def joined(x, *met):
    zero = sum((m[(0,) * m.ndim] * 0).astype(F32) for m in met)
    return x + zero.astype(x.dtype)


def spread(rows):
    count, width = rows.shape
    copies = jnp.broadcast_to(rows[None], (CHIPS, count, width)).reshape(CHIPS * count, width)
    return lax.all_to_all(copies, "shard", 0, 0, axis_index_groups=same_core(), tiled=True)


def collect(partial, *beside):
    rows = partial.shape[0] // CHIPS
    met = lax.all_to_all(
        partial.astype(BF), "shard", 0, 0, axis_index_groups=same_core(), tiled=True
    )
    total = jnp.sum(met.reshape(CHIPS, rows, partial.shape[1]).astype(F32), axis=0)
    return joined(total, *beside) if beside else total


def chip_sums(x, *beside):
    ones = jnp.ones((8, x.shape[1]), F32)
    sums = exact(ones, x, (1, 1))
    copies = jnp.broadcast_to(sums[None], (CHIPS,) + sums.shape).reshape(8 * CHIPS, -1)
    met = lax.all_to_all(copies, "shard", 0, 0, axis_index_groups=same_core(), tiled=True)
    share = joined(jnp.full((8 * CHIPS, LANES), 0.125, F32), *beside)
    return exact(met, share, (0, 0))[:, :1]


def by_place(core, own, other, axis):
    return jnp.where(
        core == 0,
        jnp.concatenate([own, other], axis=axis),
        jnp.concatenate([other, own], axis=axis),
    )


def normalize(x):
    scale = lax.rsqrt(jnp.mean(x * x, axis=-1, keepdims=True) + EPSILON)
    return x * scale, scale


def normalize_back(unit, scale, grad):
    return scale * (grad - unit * jnp.mean(grad * unit, axis=-1, keepdims=True))


def whole_vmem(count):
    return [pl.BlockSpec(memory_space=pltpu.VMEM)] * count


def scalar_first(count):
    return [pl.BlockSpec(memory_space=pltpu.SMEM)] + whole_vmem(count)


def params():
    return pltpu.CompilerParams(vmem_limit_bytes=48 * 2**20)


def small_cost():
    return pl.CostEstimate(flops=10**6, bytes_accessed=10**4, transcendentals=0)


def softplus(v):
    return jnp.maximum(v, 0.0) + jnp.log1p(jnp.exp(-jnp.abs(v)))


def row_parts(refs, at):
    states, first, second = refs
    parts = [ref[at, low : low + LANES] for ref, low in (states, first, second)]
    return jnp.concatenate(parts, axis=1).astype(F32)


def sources(near_ref, maps_ref, far_ref, recv_maps_ref, recv_far_ref):
    own = ((near_ref, LANES), (maps_ref, 0), (far_ref, 2 * LANES))
    recv = ((recv_far_ref, LANES), (recv_far_ref, 2 * LANES), (recv_maps_ref, 0))
    return own, recv


def chunk_rows(core, own_refs, recv_refs, k):
    at = pl.ds(pl.multiple_of(k * BLOCK, BLOCK), BLOCK)
    own = row_parts(own_refs, at)
    recv = row_parts(recv_refs, at)
    return jnp.where(core == 0, own, recv), jnp.where(core == 0, recv, own)


def chunk_parts(core, ext, conv_ref, cols_ref, sel_ref):
    conv = conv_ref[CONV : CONV + 1, :]
    for j in range(CONV):
        start = 8 - (CONV - 1) + j
        conv = conv + conv_ref[j : j + 1, :] * ext[start : start + CHUNK, :]
    sig = 1.0 / (1.0 + jnp.exp(-conv))
    activated = conv * sig
    states_in = activated[:, 0:LANES]
    first, second = activated[:, LANES : 2 * LANES], activated[:, 2 * LANES :]
    input_map = jnp.where(core == 0, first, second)
    output_map = jnp.where(core == 0, second, first)
    raw = dot_plain(ext[8 : 8 + CHUNK, 0:LANES].astype(BF), sel_ref[...]) + cols_ref[0:1, :]
    step = softplus(raw)
    log_decay = -step * cols_ref[1:2, :]
    rows = lax.broadcasted_iota(jnp.int32, (CHUNK, CHUNK), 0)
    cols = lax.broadcasted_iota(jnp.int32, (CHUNK, CHUNK), 1)
    causal = cols <= rows
    lower = jnp.where(causal, 1.0, 0.0)
    cumulative = exact(lower, log_decay, (1, 0))
    turned = exact(log_decay, lower, (0, 1))
    weighted = states_in * step
    coupling = dot_back(output_map.astype(BF), input_map.astype(BF))
    within = []
    for lane in (0, NARROW - 1):
        gap = cumulative[:, lane : lane + 1] - turned[lane : lane + 1, :]
        within.append(jnp.where(causal, jnp.exp(jnp.where(causal, gap, 0.0)), 0.0))
    last = cumulative[CHUNK - 1 : CHUNK, :]
    tail = jnp.exp(last - cumulative)
    decay = jnp.exp(turned[:, CHUNK - 1 : CHUNK])
    return (
        conv,
        sig,
        states_in,
        input_map.astype(BF),
        output_map.astype(BF),
        raw,
        step,
        log_decay,
        lower,
        cumulative,
        weighted,
        coupling,
        within,
        last,
        tail,
        decay,
    )


def mixer_kernel(
    core_ref,
    near_ref,
    maps_ref,
    far_ref,
    recv_maps_ref,
    recv_far_ref,
    conv_ref,
    cols_ref,
    sel_ref,
    mine_ref,
    theirs_ref,
    starts_ref,
    ext,
):
    core = core_ref[0]
    own_refs, recv_refs = sources(near_ref, maps_ref, far_ref, recv_maps_ref, recv_far_ref)
    ext[0:8, :] = jnp.zeros((8, CONVED), F32)

    def chunk(k, state):
        first, second = chunk_rows(core, own_refs, recv_refs, k)
        ext[8 : 8 + BLOCK, :] = first
        ext[8 + BLOCK : 8 + CHUNK, :] = second
        (
            conv,
            sig,
            states_in,
            input_map,
            output_map,
            raw,
            step,
            log_decay,
            lower,
            cumulative,
            weighted,
            coupling,
            within,
            last,
            tail,
            decay,
        ) = chunk_parts(core, ext, conv_ref, cols_ref, sel_ref)
        starts_ref[k] = state
        mixed = dot_back(output_map, state.astype(BF)) * jnp.exp(cumulative)
        mixed = mixed + cols_ref[2:3, :] * states_in
        for head in range(2):
            mixed = mixed + dot_plain(
                (within[head] * coupling).astype(BF),
                (weighted * cols_ref[3 + head : 4 + head, :]).astype(BF),
            )
        state = decay * state + dot_rows((weighted * tail).astype(BF), input_map)
        at = pl.ds(pl.multiple_of(k * BLOCK, BLOCK), BLOCK)
        low, high = mixed[:BLOCK, :], mixed[BLOCK:, :]
        mine_ref[at, :] = jnp.where(core == 0, low, high).astype(BF)
        theirs_ref[at, :] = jnp.where(core == 0, high, low).astype(BF)
        ext[0:8, :] = ext[CHUNK : CHUNK + 8, :]
        return state

    lax.fori_loop(0, CHIPS, chunk, jnp.zeros((LANES, NS), F32), unroll=4)


def anywhere(count):
    return [pl.BlockSpec(memory_space=pl.ANY)] * count


def mixer(core, own, layer):
    rows = own[0].shape[0]
    return pl.pallas_call(
        mixer_kernel,
        out_shape=(
            jax.ShapeDtypeStruct((rows, LANES), BF),
            jax.ShapeDtypeStruct((rows, LANES), BF),
            jax.ShapeDtypeStruct((CHIPS, LANES, NS), F32),
        ),
        in_specs=scalar_first(8),
        out_specs=tuple(whole_vmem(3)),
        scratch_shapes=[pltpu.VMEM((CHUNK + 8, CONVED), F32)],
        compiler_params=params(),
        cost_estimate=small_cost(),
    )(core, *own, layer["conv"], layer["cols"], layer["sel"])


def mixer_back_kernel(
    core_ref,
    near_ref,
    maps_ref,
    far_ref,
    recv_maps_ref,
    recv_far_ref,
    conv_ref,
    cols_ref,
    sel_ref,
    starts_ref,
    grad_own_ref,
    grad_recv_ref,
    *refs,
):
    mine_ref, theirs_ref, conv_grad_ref, cols_grad_ref, ext, later = refs[-6:]
    core = core_ref[0]
    own_refs, recv_refs = sources(near_ref, maps_ref, far_ref, recv_maps_ref, recv_far_ref)
    later[...] = jnp.zeros((CHUNK + 8, CONVED), F32)
    conv_grad_ref[...] = jnp.zeros((8, CONVED), F32)
    cols_grad_ref[...] = jnp.zeros((8, LANES), F32)
    ones = jnp.ones((CHUNK, LANES), BF)
    lanes = lax.broadcasted_iota(jnp.int32, (CHUNK, LANES), 1)

    def chunk(turn, grad_state):
        k = CHIPS - 1 - turn
        first, second = chunk_rows(core, own_refs, recv_refs, k)
        ext[8 : 8 + BLOCK, :] = first
        ext[8 + BLOCK : 8 + CHUNK, :] = second
        before = jnp.maximum(k - 1, 0)
        at_end = pl.ds(pl.multiple_of(before * BLOCK + BLOCK - 16, 16), 16)
        own_end = row_parts(own_refs, at_end)
        recv_end = row_parts(recv_refs, at_end)
        end = jnp.where(core == 0, recv_end, own_end)[8:16, :]
        ext[0:8, :] = jnp.where(k > 0, end, 0.0)
        (
            conv,
            sig,
            states_in,
            input_map,
            output_map,
            raw,
            step,
            log_decay,
            lower,
            cumulative,
            weighted,
            coupling,
            within,
            last,
            tail,
            decay,
        ) = chunk_parts(core, ext, conv_ref, cols_ref, sel_ref)
        start = starts_ref[k]
        start_low = start.astype(BF)
        at = pl.ds(pl.multiple_of(k * BLOCK, BLOCK), BLOCK)
        grad_mine = grad_own_ref[at, :].astype(F32)
        grad_theirs = grad_recv_ref[at, :].astype(F32)
        grad = jnp.concatenate(
            [
                jnp.where(core == 0, grad_mine, grad_theirs),
                jnp.where(core == 0, grad_theirs, grad_mine),
            ],
            axis=0,
        )
        grad_states = cols_ref[2:3, :] * grad
        grad_skip = jnp.sum(grad * states_in, axis=0, keepdims=True)
        grown = grad * jnp.exp(cumulative)
        grown_low = grown.astype(BF)
        grad_out_map = dot_plain(grown_low, start_low)
        grad_start = dot_rows(grown_low, output_map)
        grad_cum = grown * dot_back(output_map, start_low)
        grad_coupling = jnp.zeros((CHUNK, CHUNK), F32)
        grad_weighted = jnp.zeros((CHUNK, LANES), F32)
        for head in range(2):
            member = cols_ref[3 + head : 4 + head, :]
            grad_head = (grad * member).astype(BF)
            grad_mixing = dot_back(grad_head, weighted.astype(BF))
            mixing = within[head] * coupling
            grad_weighted = grad_weighted + dot_rows(mixing.astype(BF), grad_head)
            grad_coupling = grad_coupling + grad_mixing * within[head]
            pairs = (grad_mixing * mixing).astype(BF)
            change = dot_plain(pairs, ones) - dot_rows(pairs, ones)
            grad_cum = grad_cum + jnp.where(lanes == head * (NARROW - 1), change, 0.0)
        coupling_low = grad_coupling.astype(BF)
        grad_out_map = grad_out_map + dot_plain(coupling_low, input_map)
        grad_in_map = dot_rows(coupling_low, output_map)
        state_low = grad_state.astype(BF)
        tailed = weighted * tail
        grad_in_map = grad_in_map + dot_plain(tailed.astype(BF), state_low)
        reach = dot_back(input_map, state_low)
        grad_weighted = grad_weighted + reach * tail
        moved = reach * tailed
        grad_cum = grad_cum - moved
        kept = exact(jnp.ones((8, NS), F32), grad_state * start, (1, 1))[0:1, :]
        grad_last = jnp.sum(moved, axis=0, keepdims=True) + kept * jnp.exp(last)
        grad_log = exact(lower, grad_cum, (0, 0)) + grad_last
        grad_step = grad_weighted * states_in - cols_ref[1:2, :] * grad_log
        grad_states = grad_states + grad_weighted * step
        grad_raw = grad_step / (1.0 + jnp.exp(-raw))
        cols_grad_ref[0:1, :] += jnp.sum(grad_raw, axis=0, keepdims=True)
        cols_grad_ref[1:2, :] += jnp.sum(grad_log * log_decay, axis=0, keepdims=True)
        cols_grad_ref[2:3, :] += grad_skip
        grad_dt = exact(grad_raw, sel_ref[...].astype(F32), (1, 1))
        slope = sig * (1.0 + conv * (1.0 - sig))
        grad_first = jnp.where(core == 0, grad_in_map, grad_out_map)
        grad_second = jnp.where(core == 0, grad_out_map, grad_in_map)
        grad_conv = jnp.concatenate([grad_states, grad_first, grad_second], axis=1) * slope
        later[CHUNK : CHUNK + 8, :] = later[0:8, :]
        later[0:CHUNK, :] = grad_conv
        conv_grad_ref[CONV : CONV + 1, :] += jnp.sum(grad_conv, axis=0, keepdims=True)
        grad_in = jnp.zeros((CHUNK, CONVED), F32)
        for j in range(CONV):
            low = 8 - (CONV - 1) + j
            conv_grad_ref[j : j + 1, :] += jnp.sum(
                grad_conv * ext[low : low + CHUNK, :], axis=0, keepdims=True
            )
            ahead = CONV - 1 - j
            grad_in = grad_in + conv_ref[j : j + 1, :] * later[ahead : ahead + CHUNK, :]
        grad_in = jnp.concatenate([grad_in[:, 0:LANES] + grad_dt, grad_in[:, LANES:]], axis=1)
        low, high = grad_in[:BLOCK, :], grad_in[BLOCK:, :]
        mine_ref[at, :] = jnp.where(core == 0, low, high)
        theirs_ref[at, :] = jnp.where(core == 0, high, low).astype(BF)
        return decay * grad_state + grad_start

    lax.fori_loop(0, CHIPS, chunk, jnp.zeros((LANES, NS), F32), unroll=4)


def mixer_back(core, own, layer, starts, grad_own, grad_recv):
    rows = own[0].shape[0]
    return pl.pallas_call(
        mixer_back_kernel,
        out_shape=(
            jax.ShapeDtypeStruct((rows, CONVED), F32),
            jax.ShapeDtypeStruct((rows, CONVED), BF),
            jax.ShapeDtypeStruct((8, CONVED), F32),
            jax.ShapeDtypeStruct((8, LANES), F32),
        ),
        in_specs=scalar_first(11),
        out_specs=tuple(whole_vmem(4)),
        scratch_shapes=[pltpu.VMEM((CHUNK + 8, CONVED), F32)] * 2,
        compiler_params=params(),
        cost_estimate=small_cost(),
    )(core, *own, layer["conv"], layer["cols"], layer["sel"], starts, grad_own, grad_recv)


def seen(core, part, rows, columns):
    row = lax.broadcasted_iota(jnp.int32, (rows, columns), 0) + part * rows
    col = lax.broadcasted_iota(jnp.int32, (rows, columns), 1)
    half = columns // 2
    query_at = (row // BLOCK * 2 + core) * BLOCK + row % BLOCK
    other = col // half
    key = col - other * half
    key_at = (key // BLOCK * 2 + jnp.where(other == 0, core, 1 - core)) * BLOCK + key % BLOCK
    return key_at <= query_at


def head_part(near, far, part):
    at = slice(part * HALF_HEAD, (part + 1) * HALF_HEAD)
    return jnp.concatenate([near[:, at], far[:, at]], axis=1)


def heads_of(maps_ref, far_ref, recv_maps_ref, recv_far_ref):
    near, far = maps_ref[:, LANES:], far_ref[:, 3 * LANES :]
    recv_near, recv_far = recv_far_ref[:, 3 * LANES :], recv_maps_ref[:, LANES:]
    keys, values = (
        jnp.concatenate([head_part(near, far, k), head_part(recv_near, recv_far, k)], axis=0)
        for k in (1, 2)
    )
    return head_part(near, far, 0), keys, values


def attend_kernel(
    core_ref, maps_ref, far_ref, recv_maps_ref, recv_far_ref, also_ref, out_ref, stat_ref
):
    core = core_ref[0]
    queries, keys, values = heads_of(maps_ref, far_ref, recv_maps_ref, recv_far_ref)
    for part in range(maps_ref.shape[0] // CHUNK):
        at = slice(part * CHUNK, (part + 1) * CHUNK)
        scores = dot_back(queries[at], keys) * RATIO
        scores = jnp.where(seen(core, part, *scores.shape), scores, -1e30)
        top = jnp.max(scores, axis=1, keepdims=True)
        grown = jnp.exp(scores - top)
        total = jnp.sum(grown, axis=1, keepdims=True)
        soft = grown / total
        out_ref[at, :] = dot_plain(soft.astype(BF), values).astype(BF)
        stat_ref[at, :] = jnp.broadcast_to(top + jnp.log(total), (CHUNK, LANES))


def attend(core, own, also):
    rows = own[0].shape[0]
    return pl.pallas_call(
        attend_kernel,
        out_shape=(
            jax.ShapeDtypeStruct((rows, ATTN_HEAD_SIZE), BF),
            jax.ShapeDtypeStruct((rows, LANES), F32),
        ),
        in_specs=scalar_first(4) + anywhere(1),
        out_specs=tuple(whole_vmem(2)),
        compiler_params=params(),
        cost_estimate=small_cost(),
    )(core, *own[1:], also)


def attend_back_kernel(
    core_ref,
    maps_ref,
    far_ref,
    recv_maps_ref,
    recv_far_ref,
    stat_ref,
    grad_ref,
    *refs,
):
    near_grad_ref, far_grad_ref, theirs_ref, total, query_total = refs[-5:]
    core = core_ref[0]
    queries, keys, values = heads_of(maps_ref, far_ref, recv_maps_ref, recv_far_ref)
    total[...] = jnp.zeros(total.shape, F32)
    half = maps_ref.shape[0]
    for part in range(half // CHUNK):
        at = slice(part * CHUNK, (part + 1) * CHUNK)
        query = queries[at]
        grad = grad_ref[at, :]
        scores = dot_back(query, keys) * RATIO
        visible = seen(core, part, *scores.shape)
        soft = jnp.where(visible, jnp.exp(scores - stat_ref[at, 0:1]), 0.0)
        grad_soft = dot_back(grad, values)
        row_total = jnp.sum(soft * grad_soft, axis=1, keepdims=True)
        grad_scores = (soft * (grad_soft - row_total)).astype(BF)
        query_total[at, :] = dot_plain(grad_scores, keys) * RATIO
        key_grad = dot_rows(grad_scores, query) * RATIO
        value_grad = dot_rows(soft.astype(BF), grad)
        total[...] += jnp.concatenate([key_grad, value_grad], axis=1)
    empty = jnp.zeros((half, HALF_HEAD), F32)
    mine, theirs = total[:half, :], total[half:, :]

    def cut(x, at):
        return x[:, at * HALF_HEAD : (at + 1) * HALF_HEAD]

    query = query_total[...]
    near_grad_ref[...] = jnp.concatenate([cut(query, 0), cut(mine, 0), cut(mine, 2), empty], axis=1)
    far_grad_ref[...] = jnp.concatenate([cut(query, 1), cut(mine, 1), cut(mine, 3), empty], axis=1)
    theirs_ref[:, :LANES] = jnp.concatenate(
        [empty, cut(theirs, 0), cut(theirs, 2), empty], axis=1
    ).astype(BF)
    theirs_ref[:, LANES:] = jnp.concatenate(
        [empty, cut(theirs, 1), cut(theirs, 3), empty], axis=1
    ).astype(BF)


def attend_back(core, own, stat, grad):
    rows = own[0].shape[0]
    return pl.pallas_call(
        attend_back_kernel,
        out_shape=(
            jax.ShapeDtypeStruct((rows, LANES), F32),
            jax.ShapeDtypeStruct((rows, LANES), F32),
            jax.ShapeDtypeStruct((rows, 2 * LANES), BF),
        ),
        in_specs=scalar_first(6),
        out_specs=tuple(whole_vmem(3)),
        scratch_shapes=[
            pltpu.VMEM((2 * rows, LANES), F32),
            pltpu.VMEM((rows, ATTN_HEAD_SIZE), F32),
        ],
        compiler_params=params(),
        cost_estimate=small_cost(),
    )(core, *own[1:], stat, grad)


def gather_later(rows):
    return lax.all_gather(rows, "shard", axis=0, tiled=True, axis_index_groups=same_core())


def collect_later(partial):
    return lax.psum_scatter(
        partial.astype(BF),
        "shard",
        scatter_dimension=0,
        tiled=True,
        axis_index_groups=same_core(),
    ).astype(F32)


def forward_mixer(x, unit, scale, own_unit, layer, core, also, row_weights):
    far = dot_plain(own_unit, layer["far"]).astype(BF)
    maps = dot_plain(own_unit, layer["near"][:, 2 * LANES :]).astype(BF)
    near = dot_plain(own_unit, layer["near"][:, : 2 * LANES]).astype(BF)
    own = (near, maps, far, swap_cores(maps), swap_cores(far))
    gate_raw = jnp.concatenate([near[:, :LANES], far[:, :LANES]], axis=1).astype(F32)
    mine, theirs, starts = mixer(core, own, layer)
    mixed = jnp.concatenate([mine, swap_cores(theirs)], axis=1).astype(F32)
    gated = mixed * jax.nn.silu(gate_raw)
    attended, stat = attend(core, own, own[0] if also is None else also)
    rows = row_weights(mine)
    squares = joined(gated * gated, layer["wide"])
    ssm_scale = lax.rsqrt(chip_sums(squares, attended) / INNER + EPSILON)
    mixer_low = (gated * ssm_scale * layer["gain"]).astype(BF)
    hidden = x + collect(dot_plain(mixer_low, rows["mamba"]) + dot_plain(attended, rows["out"]))
    kept = (
        unit,
        scale,
        own_unit,
        own,
        gate_raw,
        attended,
        stat,
        starts,
        mixed,
        gated,
        mixer_low,
        ssm_scale,
    )
    return hidden, kept, rows


def forward_wide(hidden, layer, rows):
    unit, scale = normalize(hidden)
    own_unit = spread(unit.astype(BF))
    near = dot_plain(own_unit, layer["wide"])
    far = dot_plain(own_unit, layer["wide_far"])
    gate_val = jnp.concatenate([near[:, :FF_CORE], far[:, :FF_CORE]], axis=1)
    up_val = jnp.concatenate([near[:, FF_CORE:], far[:, FF_CORE:]], axis=1)
    swish = (jax.nn.silu(gate_val) * up_val).astype(BF)
    return dot_plain(swish, rows["down"]), (unit, scale, own_unit, gate_val, up_val, swish)


def backward_wide(grad_out, grad_out_own, kept, layer, rows):
    unit, scale, own_unit, gate_val, up_val, swish = kept
    grad_swish = dot_back(grad_out_own, rows["down"])
    sig = jax.nn.sigmoid(gate_val)
    grad_gate = grad_swish * up_val * (sig * (1.0 + gate_val * (1.0 - sig)))
    grad_up = grad_swish * (gate_val * sig)
    grad_near = jnp.concatenate([grad_gate[:, :FF_CORE], grad_up[:, :FF_CORE]], axis=1).astype(BF)
    grad_far = jnp.concatenate([grad_gate[:, FF_CORE:], grad_up[:, FF_CORE:]], axis=1).astype(BF)
    grads = (
        dot_rows(own_unit, grad_near),
        dot_rows(own_unit, grad_far).astype(BF),
        dot_rows(swish, grad_out_own),
    )
    grad_unit = dot_back(grad_near, layer["wide"]) + dot_back(grad_far, layer["wide_far"])
    grad_unit = collect(grad_unit, *grads)
    grad_hidden = grad_out + normalize_back(unit, scale, grad_unit)
    return grad_hidden, *grads


def backward_mixer(grad_hidden, kept, layer, rows, core, reduce_rows):
    (
        unit,
        scale,
        own_unit,
        own,
        gate_raw,
        attended,
        stat,
        starts,
        mixed,
        gated,
        mixer_low,
        ssm_scale,
    ) = kept
    grad_low = grad_hidden.astype(BF)
    grad_own = spread(grad_low)
    grad_mixer = dot_back(grad_own, rows["mamba"])
    grad_attended = dot_back(grad_own, rows["out"]).astype(BF)
    grad_scaled = grad_mixer * layer["gain"]
    near_heads, far_heads, heads_theirs = attend_back(core, own, stat, grad_attended)
    if reduce_rows is not None:
        grad_mamba, grad_out = dot_rows(mixer_low, grad_own), dot_rows(attended, grad_own)
        inner = chip_sums(grad_scaled * gated, near_heads, grad_mamba, grad_out)
    else:
        inner = chip_sums(grad_scaled * gated, near_heads)
    pull_back = ssm_scale * ssm_scale * ssm_scale * inner / INNER
    grad_gated = ssm_scale * grad_scaled - gated * pull_back
    sig = jax.nn.sigmoid(gate_raw)
    grad_mixed = (grad_gated * gate_raw * sig).astype(BF)
    grad_gate_raw = grad_gated * mixed * (sig * (1.0 + gate_raw * (1.0 - sig)))
    grad_recv = swap_cores(grad_mixed[:, LANES:])
    grad_gain = jnp.sum(grad_mixer * gated * ssm_scale, axis=0)
    mine, theirs, conv_grad, cols_grad = mixer_back(
        core, own, layer, starts, grad_mixed[:, :LANES], grad_recv
    )
    other = swap_cores(jnp.concatenate([theirs, heads_theirs], axis=1)).astype(F32)
    block = [slice(k * LANES, (k + 1) * LANES) for k in range(5)]
    if reduce_rows is not None:
        row_total = reduce_rows(grad_mamba, grad_out)
        mine = joined(mine, row_total)
    grad_near = jnp.concatenate(
        [
            grad_gate_raw[:, :LANES],
            mine[:, block[0]],
            mine[:, block[1]] + other[:, block[2]],
            near_heads + other[:, block[4]],
        ],
        axis=1,
    )
    grad_far = jnp.concatenate(
        [
            grad_gate_raw[:, LANES:],
            other[:, block[0]],
            mine[:, block[2]] + other[:, block[1]],
            far_heads + other[:, block[3]],
        ],
        axis=1,
    )
    grad_near, grad_far = grad_near.astype(BF), grad_far.astype(BF)
    near, far = dot_rows(own_unit, grad_near), dot_rows(own_unit, grad_far).astype(BF)
    if reduce_rows is None:
        low = joined(mixer_low, grad_near)
        grad_mamba = dot_rows(low, grad_own)
        grad_out = dot_rows(joined(attended, grad_near), grad_own)
        beside = near, far, grad_mamba, grad_out
        row_total = grad_mamba, grad_out
    else:
        beside = near, far
    grad_unit = dot_back(grad_near, layer["near"]) + dot_back(grad_far, layer["far"])
    grad_x = grad_hidden + normalize_back(unit, scale, collect(grad_unit, *beside))
    return grad_x, near, far, row_total, grad_gain, conv_grad, cols_grad


def section_pair(section, own, other):
    return jnp.where(section == 0, jnp.stack([own, other]), jnp.stack([other, own]))


def cut_in_kernel(w_ref, query_ref, key_ref, value_ref, gain_ref, conv_ref, out_ref):
    rows = w_ref.shape[0]
    gain = gain_ref[...]
    maps = 2 * INNER

    def piece(ref, at, width):
        return (ref[:, at : at + width].astype(F32) * gain).astype(BF)

    steps = piece(w_ref, maps + 2 * NS, NH)
    filler = jnp.zeros((rows, LANES - NARROW - NH), BF)
    rest = jnp.zeros((rows, LANES - 3 * HALF_HEAD), BF)
    for device in range(SHARDS):
        chip, core = device // CORES, device % CORES
        head = (chip // (CHIPS // KEY_VALUE_HEADS) * CORES + core) * HALF_HEAD
        cut = jnp.concatenate(
            [
                piece(w_ref, device * NARROW, NARROW),
                conv_ref[...],
                piece(w_ref, INNER + device * NARROW, NARROW),
                steps,
                filler,
                piece(w_ref, maps + core * NS, NS),
                piece(query_ref, device * HALF_HEAD, HALF_HEAD),
                piece(key_ref, head, HALF_HEAD),
                piece(value_ref, head, HALF_HEAD),
                rest,
            ],
            axis=1,
        )
        out_ref[device] = cut
        out_ref[SHARDS + device] = cut


def cut_wide_kernel(gate_ref, up_ref, gain_ref, out_ref):
    gain = gain_ref[...]
    for device in range(SHARDS):
        at = slice(device * FF_CORE, (device + 1) * FF_CORE)
        for k, ref in enumerate((gate_ref, up_ref)):
            cut = (ref[:, at].astype(F32) * gain).astype(BF)
            low = slice(k * FF_CORE, (k + 1) * FF_CORE)
            out_ref[device, :, low] = cut
            out_ref[SHARDS + device, :, low] = cut


def cut_call(kernel, columns, *operands):
    return pl.pallas_call(
        kernel,
        out_shape=jax.ShapeDtypeStruct((2 * SHARDS, operands[0].shape[0], columns), BF),
        in_specs=whole_vmem(len(operands)),
        out_specs=whole_vmem(1)[0],
        compiler_params=params(),
        cost_estimate=small_cost(),
    )(*operands)


def finish_kernel(in_width, total_ref, gain_ref, mid_ref, *refs):
    raw, outs, norms_ref = refs[:6], refs[6:12], refs[12]
    sums = []
    at = 0
    for k in range(6):
        width = raw[k].shape[1]
        part = slice(at, at + width)
        grad = total_ref[:, part].astype(F32)
        sums.append(jnp.sum(grad * raw[k][...].astype(F32), axis=1, keepdims=True))
        outs[k][...] = grad * (gain_ref if k < 4 else mid_ref)[...]
        at += in_width if k == 0 else width
    lane = lax.broadcasted_iota(jnp.int32, norms_ref.shape, 1)
    norm_in = sums[0] + sums[1] + sums[2] + sums[3]
    norms_ref[...] = jnp.where(lane == 0, norm_in, sums[4] + sums[5])


def finish(in_width, total, gain_in, gain_mid, raw):
    rows = total.shape[0]
    return pl.pallas_call(
        functools.partial(finish_kernel, in_width),
        out_shape=tuple(jax.ShapeDtypeStruct(w.shape, F32) for w in raw)
        + (jax.ShapeDtypeStruct((rows, LANES), F32),),
        in_specs=whole_vmem(9),
        out_specs=tuple(whole_vmem(7)),
        compiler_params=params(),
        cost_estimate=small_cost(),
    )(total, gain_in, gain_mid, *raw)


def body(
    inputs,
    cotangent,
    norm_in,
    w_in,
    conv_w,
    conv_b,
    dt_bias,
    a_log,
    skip_gain,
    norm_ssm,
    w_out,
    query_weight,
    key_weight,
    value_weight,
    output_weight,
    norm_mid,
    w_gate,
    w_up,
    w_down,
):
    place = lax.axis_index("shard")
    core = place % CORES
    core_word = core.reshape(1).astype(jnp.int32)
    section = lax.axis_index("section")
    reps = lax.axis_size("rep")
    local = inputs.shape[2]
    spare = LANES - NARROW

    gain_in = norm_in[0].astype(F32)[:, None]
    gain_mid = norm_mid[0].astype(F32)[:, None]

    own_input = lax.dynamic_index_in_dim(inputs[:, 0], section, 0, False).astype(F32)
    own_target = lax.dynamic_index_in_dim(cotangent[:, 0], section, 0, False)
    unit, scale = normalize(own_input)
    own_unit = spread(unit.astype(BF))
    conv_all = jnp.concatenate([conv_w[0], conv_b], axis=0)
    conv_count = conv_all.size
    conv_cols = jnp.concatenate(
        [conv_all.reshape(-1), jnp.zeros((spare * local - conv_count,), BF)]
    ).reshape(local, spare)
    cut = cut_call(
        cut_in_kernel,
        IN_COLS,
        w_in[0],
        query_weight[0],
        key_weight[0],
        value_weight[0],
        gain_in,
        conv_cols,
    )
    everywhere = ("section", "shard")
    met = lax.all_to_all(cut, everywhere, 0, 0, tiled=True)
    met = met.reshape(2, SHARDS, local, IN_COLS)
    conv_met = met[:, :, :, NARROW:LANES].reshape(2, SHARDS, spare * local)[:, :, :conv_count]
    conv_met = conv_met.reshape(2, SHARDS, CONV + 1, -1).transpose(0, 2, 1, 3)
    conv_met = conv_met.reshape(2, CONV + 1, INNER + 2 * NS).astype(F32)
    own_cols = met.reshape(2, SHARDS * local, IN_COLS)
    other_cols = swap_cores(own_cols)
    cut = cut_call(cut_wide_kernel, WIDE_COLS, w_gate[0], w_up[0], gain_mid)
    wide_cols = lax.all_to_all(cut, everywhere, 0, 0, tiled=True)
    wide_cols = wide_cols.reshape(2, SHARDS * local, WIDE_COLS)
    other_wide = swap_cores(wide_cols)

    def both_layers(own):
        return section_pair(section, own, swap_sections(own))

    raw_rows = jnp.concatenate([w_out[0], output_weight[0], w_down[0]], axis=0)
    raw_rows = joined(raw_rows, met)
    sent_rows = swap_sections(raw_rows)
    row_store = {}

    def rows_at(layer):
        def make(token):
            if not row_store:
                rows = section_pair(section, raw_rows, joined(sent_rows, token))
                row_store["pair"] = rows, swap_cores(rows)
            rows, others = (x[layer] for x in row_store["pair"])
            return {
                "mamba": jnp.concatenate([rows[:out_row], no_rows, others[:out_row], no_rows]),
                "out": jnp.concatenate([rows[out_row:down_row], others[out_row:down_row]]),
                "down": jnp.concatenate([rows[down_row:], others[down_row:]]),
            }

        return make

    out_row, down_row = NARROW, NARROW + HALF_HEAD
    per_head = jnp.concatenate([dt_bias[0], a_log[0], skip_gain[0], norm_ssm[0].astype(F32)])
    per_head = both_layers(per_head)
    own_gain = per_head[:, 3 * NH :]
    other_gain = swap_cores(own_gain)
    lane = lax.broadcasted_iota(jnp.int32, (NH, LANES), 1)
    head_of = jnp.where(lane < NARROW, (lane + place * NARROW) // HD, -1)
    member = (head_of == lax.broadcasted_iota(jnp.int32, (NH, LANES), 0)).astype(F32)
    sel = jnp.concatenate(
        [jnp.zeros((NARROW, LANES), F32), member, jnp.zeros((LANES - NARROW - NH, LANES), F32)]
    ).astype(BF)
    in_first = (head_of[0:1] == head_of[0:1, 0:1]).astype(F32)
    in_second = (head_of[0:1] == head_of[0:1, NARROW - 1 : NARROW]).astype(F32)

    def to_columns(values):
        return jnp.sum(values[:, None] * member, axis=0, keepdims=True)

    def padded(g):
        return jnp.concatenate([g, jnp.zeros((spare,), F32)])

    no_rows = jnp.zeros((spare, MODEL_WIDTH), BF)
    layers = []
    for layer in range(2):
        head_values = per_head[layer]
        cols = jnp.concatenate(
            [
                to_columns(head_values[:NH]),
                to_columns(jnp.exp(head_values[NH : 2 * NH])),
                to_columns(head_values[2 * NH : 3 * NH]),
                in_first,
                in_second,
                jnp.zeros((3, LANES), F32),
            ]
        )
        conv_own = jnp.concatenate(
            [
                lax.dynamic_slice_in_dim(conv_met[layer], place * NARROW, NARROW, axis=1),
                jnp.zeros((CONV + 1, spare), F32),
                by_place(core, conv_met[layer, :, INNER : INNER + NS], conv_met[layer, :, INNER + NS :], 1),
            ],
            axis=1,
        )
        layers.append(
            {
                "near": own_cols[layer],
                "far": other_cols[layer],
                "wide": wide_cols[layer],
                "wide_far": other_wide[layer],
                "conv": jnp.concatenate([conv_own, jnp.zeros((7 - CONV, CONVED), F32)]),
                "cols": cols,
                "sel": sel,
                "gain": jnp.concatenate([padded(own_gain[layer]), padded(other_gain[layer])])[None],
            }
        )

    x = own_input
    outs = []
    target_own = None
    kept_mixer, kept_wide, row_weights = [], [], []
    for layer in range(2):
        if layer == 1:
            unit, scale = normalize(x)
            own_unit = spread(unit.astype(BF))
        hidden, kept, rows = forward_mixer(
            x, unit, scale, own_unit, layers[layer], core_word, target_own, rows_at(layer)
        )
        if layer == 0:
            target_own = gather_later(joined(own_target, hidden))
        row_weights.append(rows)
        kept_mixer.append(kept)
        partial, kept = forward_wide(hidden, layers[layer], rows)
        kept_wide.append(kept)
        total = collect(partial) if layer == 0 else collect_later(partial)
        outs.append((hidden + total).astype(BF))
        x = outs[layer].astype(F32)

    def exchanged(first, second):
        own = jnp.where(section == 0, first, second)
        other = swap_sections(jnp.where(section == 0, second, first).astype(BF))
        return section_pair(section, own, other.astype(own.dtype))

    part = local // reps

    def by_parts(columns):
        cut = columns.reshape(SHARDS, reps, part, columns.shape[1])
        return cut.transpose(1, 0, 2, 3).reshape(reps * SHARDS, part, columns.shape[1])

    def over_all(sent):
        met = lax.all_to_all(sent, ("section", "rep", "shard"), 0, 0, tiled=True)
        met = met.reshape(2 * reps, SHARDS, part, sent.shape[2])
        return jnp.sum(met.astype(F32), axis=0)

    extra_width = -(-(conv_count + NARROW + 3 * NH) // (reps * part))
    in_width = -(-(2 * INNER + 2 * NS + NH + extra_width) // LANES) * LANES

    def to_all(rows, axes, count):
        copies = jnp.broadcast_to(rows[None], (count,) + rows.shape)
        met = lax.all_to_all(copies, axes, 0, 0, tiled=True)
        return met.reshape(count * rows.shape[0], rows.shape[1])

    def even(g):
        return g.transpose(1, 0, 2).reshape(part, -1)

    def by_key_head(g):
        groups = CHIPS // KEY_VALUE_HEADS
        g = jnp.sum(g.reshape(KEY_VALUE_HEADS, groups, CORES, part, -1), axis=1)
        return even(g.reshape(KEY_VALUE_HEADS * CORES, part, -1))

    def by_weight(total):
        maps = total[:, :, 2 * LANES : 3 * LANES].reshape(CHIPS, CORES, part, LANES)
        heads = [
            total[:, :, 3 * LANES + k * HALF_HEAD : 3 * LANES + (k + 1) * HALF_HEAD]
            for k in range(3)
        ]
        columns = [
            even(total[:, :, :NARROW]),
            even(total[:, :, LANES : LANES + NARROW]),
            even(jnp.sum(maps, axis=0)),
            jnp.sum(total[:, :, LANES + NARROW : LANES + NARROW + NH], axis=0),
            jnp.sum(total[:, :, NARROW : NARROW + extra_width], axis=0),
            jnp.zeros((part, in_width - 2 * INNER - 2 * NS - NH - extra_width), F32),
            even(heads[0]),
            by_key_head(heads[1]),
            by_key_head(heads[2]),
            even(total[:, :, IN_COLS : IN_COLS + FF_CORE]),
            even(total[:, :, IN_COLS + FF_CORE :]),
        ]
        return jnp.concatenate(columns, axis=1).astype(BF)

    def pair_total(near, far):
        return (near + swap_cores(far).astype(F32)).astype(BF)

    def small_parts(grad_gain, conv_grad, cols_grad):
        conv_grad = conv_grad[: CONV + 1]
        maps_grad = by_place(core, conv_grad[:, LANES : 2 * LANES], conv_grad[:, 2 * LANES :], 1)
        conv_grad = jnp.concatenate(
            [
                lax.dynamic_update_slice_in_dim(
                    jnp.zeros((CONV + 1, INNER), F32), conv_grad[:, :NARROW], place * NARROW, axis=1
                ),
                maps_grad,
            ],
            axis=1,
        )
        conv_grad = conv_grad.reshape(CONV + 1, SHARDS, -1).transpose(1, 0, 2).reshape(SHARDS, -1)
        gain_halves = by_place(core, grad_gain[:NARROW], grad_gain[LANES : LANES + NARROW], 0)
        gain_grad = lax.dynamic_update_slice_in_dim(
            jnp.zeros((INNER,), F32), gain_halves, (place // CORES) * CORES * NARROW, axis=0
        ).reshape(SHARDS, -1)
        head_grad = jnp.sum(cols_grad[:3, None, :] * member[None], axis=2).reshape(1, -1)
        extra = jnp.concatenate(
            [conv_grad, gain_grad, jnp.broadcast_to(head_grad, (SHARDS, 3 * NH))], axis=1
        )
        width = -(-extra.shape[1] // (reps * part))
        missing = reps * part * width - extra.shape[1]
        extra = jnp.concatenate([extra, jnp.zeros((SHARDS, missing), F32)], axis=1)
        extra = extra.reshape(SHARDS, reps, part, width).transpose(1, 0, 2, 3)
        return extra.reshape(reps * SHARDS, part, width).astype(BF)

    def with_small(sent, extra):
        room = spare - extra.shape[2]
        extra = jnp.pad(extra, ((0, 0), (0, 0), (0, room)))
        return jnp.concatenate([sent[:, :, :NARROW], extra, sent[:, :, LANES:]], axis=2)

    def rows_of(grad_mamba, grad_out, grad_down):
        mine = jnp.concatenate([grad_mamba[:NARROW], grad_out[:HALF_HEAD], grad_down[:FF_CORE]])
        theirs = jnp.concatenate(
            [grad_mamba[LANES : LANES + NARROW], grad_out[HALF_HEAD:], grad_down[FF_CORE:]]
        )
        return pair_total(mine, theirs.astype(BF))

    def reduce_rows(grad_mamba, grad_out):
        first_rows = rows_of(grad_mamba, grad_out, grad_down)
        met = lax.all_to_all(
            jnp.concatenate([first_rows, last_rows]), ("section", "rep"), 0, 0, tiled=True
        )
        met = met.reshape(2 * reps, -1, MODEL_WIDTH).astype(F32)
        return joined(jnp.sum(met, axis=0), outs[1]).astype(BF)

    sent = [None, None]
    grad = own_target.astype(F32)
    input_grads = [None, None]
    for layer in (1, 0):
        grad_own = target_own if layer == 1 else spread(grad.astype(BF))
        grad_hidden, grad_wide, grad_wide_far, grad_down = backward_wide(
            grad, grad_own, kept_wide[layer], layers[layer], row_weights[layer]
        )
        grad_x, grad_near, grad_far, row_total, *small = backward_mixer(
            grad_hidden,
            kept_mixer[layer],
            layers[layer],
            row_weights[layer],
            core_word,
            reduce_rows if layer == 0 else None,
        )
        if layer == 1:
            last_rows = rows_of(*row_total, grad_down)
        input_grads[layer] = grad_x
        grad = grad_x.astype(BF).astype(F32)
        columns = [pair_total(grad_near, grad_far), pair_total(grad_wide, grad_wide_far)]
        columns = jnp.concatenate(columns, axis=1)
        sent[layer] = with_small(by_parts(columns), small_parts(*small))

    section_out = exchanged(outs[0], joined(outs[1], grad_near))[None, :, None]
    input_grad = exchanged(*input_grads)[None, :, None]
    columns = by_weight(over_all(jnp.concatenate(sent)))
    totals = to_all(jnp.concatenate([columns, row_total.reshape(part, -1)], axis=1), "rep", reps)
    columns = totals[:, : columns.shape[1]]
    row_total = totals[:, columns.shape[1] :].reshape(-1, MODEL_WIDTH).astype(F32)
    used = 2 * INNER + 2 * NS + NH
    extra = columns[:, used : used + extra_width].astype(F32).reshape(-1)
    conv_total = extra[:conv_count].reshape(CONV + 1, -1)
    gain_total = extra[conv_count : conv_count + NARROW]
    head_total = extra[conv_count + NARROW : conv_count + NARROW + 3 * NH].reshape(3, NH)
    raw = [w[0] for w in (w_in, query_weight, key_weight, value_weight, w_gate, w_up)]
    *by_rows, norms = finish(in_width, totals, gain_in, gain_mid, raw)
    grad_norm_in, grad_norm_mid = norms[:, 0], norms[:, 1]
    return (
        section_out,
        input_grad,
        grad_norm_in[None],
        by_rows[0][None],
        conv_total[:CONV][None],
        conv_total[CONV][None],
        head_total[0][None],
        head_total[1][None],
        head_total[2][None],
        gain_total[None],
        row_total[:out_row][None],
        by_rows[1][None],
        by_rows[2][None],
        by_rows[3][None],
        row_total[out_row:down_row][None],
        grad_norm_mid[None],
        by_rows[4][None],
        by_rows[5][None],
        row_total[down_row:][None],
    )


def solution(mesh):
    return jax.shard_map(
        body,
        mesh=mesh,
        in_specs=(
            P(None, "rep", "shard", None),
            P(None, "rep", "shard", None),
            P("section", "shard"),
            P("section", "shard", None),
            P("section", None, "shard"),
            P("section", "shard"),
            P("section", None),
            P("section", None),
            P("section", None),
            P("section", "shard"),
            P("section", "shard", None),
            P("section", "shard", None),
            P("section", "shard", None),
            P("section", "shard", None),
            P("section", "shard", None),
            P("section", "shard"),
            P("section", "shard", None),
            P("section", "shard", None),
            P("section", "shard", None),
        ),
        out_specs=(
            P("section", None, "rep", "shard", None),
            P("section", None, "rep", "shard", None),
            P("section", "shard"),
            P("section", "shard", None),
            P("section", None, "shard"),
            P("section", "shard"),
            P("section", None),
            P("section", None),
            P("section", None),
            P("section", "shard"),
            P("section", "shard", None),
            P("section", "shard", None),
            P("section", "shard", None),
            P("section", "shard", None),
            P("section", "shard", None),
            P("section", "shard"),
            P("section", "shard", None),
            P("section", "shard", None),
            P("section", "shard", None),
        ),
        check_vma=False,
    )
```

time: 718 us -> 679 us (0.946)
  blocking collectives: 17.6 us -> 79 us
  waiting for transfers between devices: 241 us -> 189 us
  between operations: 4.72 us -> 35.2 us
  other arithmetic: 80.3 us -> 52.5 us
  local copies, waits for them, and re-layouts: 125 us -> 98.1 us
  starting transfers between devices: 121 us -> 97.7 us
    all_to_all x9 -> x4, waiting for transfers between devices: 97.3 us -> 24.2 us  [collect(): lax.all_to_all(partial.astype(BF), 'shard', 0, 0, axis_index_groups=same_...]
    all_to_all x1 -> x3, blocking collectives: 17.6 us -> 49.4 us  [collect(): lax.all_to_all(partial.astype(BF), 'shard', 0, 0, axis_index_groups=same_...]
    all_to_all x0 -> x2, blocking collectives: none -> 29.6 us  [spread(): lax.all_to_all(copies, 'shard', 0, 0, axis_index_groups=same_core(), tile...]
    concatenate x24 -> x4, local copies, waits for them, and re-layouts: 30.5 us -> 1.49 us  [the longest x3 1.39 us: small_parts(): extra = jnp.concatenate([extra, jnp.zeros((SHARDS, missing), F32)], axis=1)]
    ppermute x4, waiting for transfers between devices: 67.7 us -> 40.4 us  [swap_sections(): return lax.ppermute(x, 'section', [(0, 1), (1, 0)])]
    all_to_all x6 -> x9, waiting for transfers between devices: 23.8 us -> 46.3 us  [the longest x1 25.9 us: body(): met = lax.all_to_all(cut, everywhere, 0, 0, tiled=True)]
    reduce_scatter x0 -> x1, waiting for transfers between devices: none -> 21.8 us  [collect_later(): lax.psum_scatter(partial.astype(BF), 'shard', scatter_dimension=0, tiled=...]
    all_to_all x9 -> x4, starting transfers between devices: 41.4 us -> 19.7 us  [collect(): lax.all_to_all(partial.astype(BF), 'shard', 0, 0, axis_index_groups=same_...]
  transfers between devices with their start and end apart: 43 -> 44, of which waited for: 22 -> 23; matrix products, arithmetic and copies ran while one was open for 29% -> 20% of each run, Pallas kernels for 4% -> 5%
where the time goes in v2:
time: 679 us; the launch traced here: 666 us
  waiting for transfers between devices  189 us (28%)
  local copies, waits for them, and re-layouts  98.1 us (14%)
  starting transfers between devices  97.7 us (14%)
  blocking collectives  79 us (12%)
  matrix products  66.2 us (10%)
  other arithmetic  52.5 us (8%)
  Pallas kernels  48.8 us (7%)
  between operations  35.2 us (5%)
    all_to_all x3, blocking collectives, collect(): lax.all_to_all(partial.astype(BF), 'shard', 0, 0, axis_index_groups=same_...  49.4 us
    all_to_all x5, waiting for transfers between devices, spread(): lax.all_to_all(copies, 'shard', 0, 0, axis_index_groups=same_core(), tile...  40.9 us
    ppermute x4, waiting for transfers between devices, swap_sections(): return lax.ppermute(x, 'section', [(0, 1), (1, 0)])  40.4 us
    all_to_all x2, blocking collectives, spread(): lax.all_to_all(copies, 'shard', 0, 0, axis_index_groups=same_core(), tile...  29.6 us
    all_to_all x1, waiting for transfers between devices, body(): met = lax.all_to_all(cut, everywhere, 0, 0, tiled=True)  25.9 us
    pallas_call x2, Pallas kernels, mixer_back(): pl.pallas_call(mixer_back_kernel, out_shape=(jax.ShapeDtypeStruct((rows,...  24.4 us
    all_to_all x4, waiting for transfers between devices, collect(): lax.all_to_all(partial.astype(BF), 'shard', 0, 0, axis_index_groups=same_...  24.2 us
    dot_general x14, matrix products, dot_back(): lax.dot_general(former, latter, (((1,), (1,)), ((), ())), preferred_eleme...  23.5 us
  transfers between devices with their start and end apart: 44, of which 23 were waited for; matrix products, arithmetic and copies ran while one was open for 20% of the time, Pallas kernels for 5%

profile of v2, /device:TPU:0, one launch (start us, length us, event | category | flops | bytes accessed | tf_op | source)
XLA Modules:
  0.0 666.2 jit_solution(13532514401048890214)
XLA Ops:
  19.4 5.6 all-to-all-start.1
  29.5 25.9 %all-to-all-done.1 = bf16[32,64,512]{2,1,0:T(8,128)(2,1)} async-done(((bf16[32,64,512]{2,1,0:T(8,128)(2,1)}), bf16[32,64,512]{2,1,0:T(8,128)(2,1)}, u32[]{:S(2)}, u32[]{:S(2)}) %all-to-all-start.1) | async-done | bytes 2097184 | tf_op jit(solution)/shard_map/all_to_all | solution.py:851
  115.7 5.1 all-to-all-done.3
  125.5 17.4 %all_to_all.191 = bf16[8,64,1024]{2,1,0:T(8,128)(2,1)S(1)} all-to-all(bf16[8,64,1024]{2,1,0:T(8,128)(2,1)S(1)} %bitcast.464), channel_id=1, replica_groups={{0,2,4,6,8,10,12,14},{1,3,5,7,9,11,13,15},{16,18,20,22,24,26,28,30},{17..., dimensions={0} | all-to-all | bytes 2097152 | tf_op jit(solution)/shard_map/all_to_all | solution.py:89
  151.7 10.1 %all-to-all-done.5 = bf16[8,64,1024]{2,1,0:T(8,128)(2,1)S(1)} async-done(((bf16[8,64,1024]{2,1,0:T(8,128)(2,1)}), bf16[8,64,1024]{2,1,0:T(8,128)(2,1)S(1)}, u32[]{:S(2)}, u32[]{:S(2)}) %all-to-all-start.5) | async-done | bytes 1048608 | tf_op jit(solution)/shard_map/all_to_all | solution.py:84
  165.4 17.6 %all_to_all.192 = bf16[8,64,1024]{2,1,0:T(8,128)(2,1)S(1)} all-to-all(bf16[8,64,1024]{2,1,0:T(8,128)(2,1)S(1)} %bitcast.460), channel_id=1, replica_groups={{0,2,4,6,8,10,12,14},{1,3,5,7,9,11,13,15},{16,18,20,22,24,26,28,30},{17..., dimensions={0} | all-to-all | bytes 2097152 | tf_op jit(solution)/shard_map/all_to_all | solution.py:89
  190.8 11.8 %all-to-all-done.7 = bf16[8,64,1024]{2,1,0:T(8,128)(2,1)S(1)} async-done(((bf16[8,64,1024]{2,1,0:T(8,128)(2,1)}), bf16[8,64,1024]{2,1,0:T(8,128)(2,1)S(1)}, u32[]{:S(2)}, u32[]{:S(2)}) %all-to-all-start.7) | async-done | bytes 1048608 | tf_op jit(solution)/shard_map/all_to_all | solution.py:84
  223.7 7.0 %all-gather.3.cloned.1.call-done = bf16[1,1,512,1024]{3,2,1,0:T(8,128)(2,1)} async-done(((bf16[1,1,64,1024]{3,2,1,0:T(8,128)(2,1)}), bf16[1,1,512,1024]{3,2,1,0:T(8,128)(2,1)}) %all-gather.3.cloned.1.call-update) | async-done | bytes 1048592 | tf_op jit(solution)/shard_map/all_gather | solution.py:562
  238.8 14.5 %all_to_all.193 = bf16[8,64,1024]{2,1,0:T(8,128)(2,1)S(1)} all-to-all(bf16[8,64,1024]{2,1,0:T(8,128)(2,1)S(1)} %bitcast.465), channel_id=1, replica_groups={{0,2,4,6,8,10,12,14},{1,3,5,7,9,11,13,15},{16,18,20,22,24,26,28,30},{17..., dimensions={0} | all-to-all | bytes 2097152 | tf_op jit(solution)/shard_map/all_to_all | solution.py:89
  253.9 14.0 %all_to_all.194 = bf16[8,64,1024]{2,1,0:T(8,128)(2,1)S(1)} all-to-all(bf16[8,64,1024]{2,1,0:T(8,128)(2,1)S(1)} %broadcast_in_dim.93), channel_id=1, replica_groups={{0,2,4,6,8,10,12,14},{1,3,5,7,9,11,13,15},{16,18,20,22,24,26,28,30},{17..., dimensions={0} | all-to-all | bytes 2097152 | tf_op jit(solution)/shard_map/all_to_all | solution.py:84
  296.2 21.8 %reduce-scatter.2.cloned.1.call-done = bf16[64,1024]{1,0:T(8,128)(2,1)} async-done(((bf16[512,1024]{1,0:T(8,128)(2,1)}), bf16[64,1024]{1,0:T(8,128)(2,1)}) %reduce-scatter.2.cloned.1.call-update) | async-done | bytes 131088 | tf_op jit(solution)/shard_map/reduce_scatter | solution.py:566
  319.8 15.7 %all_to_all.195 = bf16[8,64,1024]{2,1,0:T(8,128)(2,1)S(1)} all-to-all(bf16[8,64,1024]{2,1,0:T(8,128)(2,1)S(1)} %broadcast_in_dim.94), channel_id=1, replica_groups={{0,2,4,6,8,10,12,14},{1,3,5,7,9,11,13,15},{16,18,20,22,24,26,28,30},{17..., dimensions={0} | all-to-all | bytes 2097152 | tf_op jit(solution)/shard_map/all_to_all | solution.py:84
  358.2 12.2 %shard_map.337 = (f32[512,384]{1,0:T(8,128)S(1)}, bf16[512,384]{1,0:T(8,128)(2,1)S(1)}, f32[8,384]{1,0:T(8,128)S(1)}, f32[8,128]{1,0:T(8,128)S(1)}) custom-call(s32[1]{0:T(128)} %bitcast.1.core_ref, bf16[512,256]{1,0:T(8,128)(2,1)S(1)} %copy-done.13, bf16[512,256]{1,0:T(8,128)(2,1)S(1)} %copy-done.5, bf16[512,512]{1,0:T(8,128)(2,1)S(1)} %convolution_convert_fusion.6.far_ref, ...), custom_call_target="tpu_custom_call" | custom-call | flops 1000000 | bytes 10000 | tf_op jit(solution)/shard_map/pallas_call | solution.py:421
  376.9 6.0 all-to-all-start.14
  413.1 8.7 %all-to-all-done.15 = bf16[8,64,1024]{2,1,0:T(8,128)(2,1)S(1)} async-done(((bf16[8,64,1024]{2,1,0:T(8,128)(2,1)}), bf16[8,64,1024]{2,1,0:T(8,128)(2,1)S(1)}, u32[]{:S(2)}, u32[]{:S(2)}) %all-to-all-start.15) | async-done | bytes 1048608 | tf_op jit(solution)/shard_map/all_to_all | solution.py:84
  444.3 6.3 all-to-all-done.16
  466.4 7.2 %all-to-all-done.17 = bf16[8,64,1024]{2,1,0:T(8,128)(2,1)S(1)} async-done(((bf16[8,64,1024]{2,1,0:T(8,128)(2,1)}), bf16[8,64,1024]{2,1,0:T(8,128)(2,1)S(1)}, u32[]{:S(2)}, u32[]{:S(2)}) %all-to-all-start.17) | async-done | bytes 1048608 | tf_op jit(solution)/shard_map/all_to_all | solution.py:84
  503.8 7.0 %all-to-all-start.19 = ((bf16[8,64,1024]{2,1,0:T(8,128)(2,1)}), bf16[8,64,1024]{2,1,0:T(8,128)(2,1)}, u32[]{:S(2)}, u32[]{:S(2)}) async-start(bf16[8,64,1024]{2,1,0:T(8,128)(2,1)} %bitcast.463), calls=%async_computation.20 | async-start | bytes 2097152 | tf_op jit(solution)/shard_map/all_to_all | solution.py:1058
  511.2 12.2 %shard_map.339 = (f32[512,384]{1,0:T(8,128)S(1)}, bf16[512,384]{1,0:T(8,128)(2,1)S(1)}, f32[8,384]{1,0:T(8,128)S(1)}, f32[8,128]{1,0:T(8,128)S(1)}) custom-call(s32[1]{0:T(128)} %bitcast.1.core_ref, bf16[512,256]{1,0:T(8,128)(2,1)S(1)} %copy-done.9, bf16[512,256]{1,0:T(8,128)(2,1)S(1)} %convolution_convert_fusion.10.maps_ref, ...), custom_call_target="tpu_custom_call" | custom-call | flops 1000000 | bytes 10000 | tf_op jit(solution)/shard_map/pallas_call | solution.py:421
  545.1 5.2 all-to-all-start.20
  559.1 8.2 %all-to-all-done.20 = bf16[8,64,1024]{2,1,0:T(8,128)(2,1)S(1)} async-done(((bf16[8,64,1024]{2,1,0:T(8,128)(2,1)}), bf16[8,64,1024]{2,1,0:T(8,128)(2,1)S(1)}, u32[]{:S(2)}, u32[]{:S(2)}) %all-to-all-start.20) | async-done | bytes 1048608 | tf_op jit(solution)/shard_map/all_to_all | solution.py:89
  567.3 8.9 %all-to-all-start.21 = ((bf16[128,16,768]{2,1,0:T(8,128)(2,1)}), bf16[128,16,768]{2,1,0:T(8,128)(2,1)}, u32[]{:S(2)}, u32[]{:S(2)}) async-start(bf16[128,16,768]{2,1,0:T(8,128)(2,1)} %fusion.10), calls=%async_computation.22 | async-start | bytes 6291456 | tf_op jit(solution)/shard_map/all_to_all | solution.py:973
  583.0 35.5 %collective-permute-done.18 = bf16[64,1024]{1,0:T(8,128)(2,1)S(1)} collective-permute-done((bf16[64,1024]{1,0:T(8,128)(2,1)S(1)}, bf16[64,1024]{1,0:T(8,128)(2,1)S(1)}, u32[]{:S(2)}, u32[]{:S(2)}) %collective-permute-start.18) | collective-permute-done | bytes 131104 | tf_op jit(solution)/shard_map/ppermute | solution.py:69
  638.5 10.9 %all-to-all-done.22 = bf16[4,16,12416]{2,1,0:T(8,128)(2,1)S(1)} async-done(((bf16[4,16,12416]{2,1,0:T(8,128)(2,1)}), bf16[4,16,12416]{2,1,0:T(8,128)(2,1)S(1)}, u32[]{:S(2)}, u32[]{:S(2)}) %all-to-all-start.22) | async-done | bytes 1589280 | tf_op jit(solution)/shard_map/all_to_all | solution.py:982
  (865 shorter events, 336.3 us)
Async XLA Ops:
  8.6 20.8 %collective-permute-start.3 = (f32[168]{0:T(256)S(1)}, f32[168]{0:T(256)S(1)}, u32[]{:S(2)}, u32[]{:S(2)}) collective-permute-start(f32[168]{0:T(256)S(1)} %pad_maximum_fusion.68), channel_id=1, source_target_pairs={{0,64},{64,0},{1,65},{65,1},{2,66},{66,2},{3,67},{67,3},{4,68},{68... | collective-permute-start | bytes 2024 | tf_op jit(solution)/shard_map/ppermute | solution.py:69
  19.4 36.1 %all-to-all-start.1 = ((bf16[32,64,512]{2,1,0:T(8,128)(2,1)}), bf16[32,64,512]{2,1,0:T(8,128)(2,1)}, u32[]{:S(2)}, u32[]{:S(2)}) async-start(bf16[32,64,512]{2,1,0:T(8,128)(2,1)} %shard_map.330), calls=%async_computation.1 | async-start | bytes 4194304 | tf_op jit(solution)/shard_map/all_to_all | solution.py:851
  56.6 20.5 %all-to-all-start = ((bf16[8,64,1024]{2,1,0:T(8,128)(2,1)}), bf16[8,64,1024]{2,1,0:T(8,128)(2,1)S(1)}, u32[]{:S(2)}, u32[]{:S(2)}) async-start(bf16[8,64,1024]{2,1,0:T(8,128)(2,1)} %broadcast_in_dim.78), calls=%async_computation | async-start | bytes 2097152 | tf_op jit(solution)/shard_map/all_to_all | solution.py:84
  60.2 23.4 %collective-permute-start = (bf16[2,1024,512]{2,1,0:T(8,128)(2,1)}, bf16[2,1024,512]{2,1,0:T(8,128)(2,1)}, u32[]{:S(2)}, u32[]{:S(2)}) collective-permute-start(bf16[2,1024,512]{2,1,0:T(8,128)(2,1)} %bitcast.10), channel_id=1, source_target_pairs={{0,1},{1,0},{2,3},{3,2},{4,5},{5,4},{6,7},{7,6},{8,9},{9,8},{10,11... | collective-permute-start | bytes 6291464 | tf_op jit(solution)/shard_map/ppermute | solution.py:65
  70.6 22.6 %collective-permute-start.6 = (bf16[256,1024]{1,0:T(8,128)(2,1)}, bf16[256,1024]{1,0:T(8,128)(2,1)}, u32[]{:S(2)}, u32[]{:S(2)}) collective-permute-start(bf16[256,1024]{1,0:T(8,128)(2,1)} %maximum_add_fusion.3), channel_id=1, source_target_pairs={{0,64},{64,0},{1,65},{65,1},{2,66},{66,2},{3,67},{67,3},{4,68},{68... | collective-permute-start | bytes 1572872 | tf_op jit(solution)/shard_map/ppermute | solution.py:69
  77.1 23.1 %all-to-all-start.2 = ((bf16[32,64,256]{2,1,0:T(8,128)(2,1)}), bf16[32,64,256]{2,1,0:T(8,128)(2,1)}, u32[]{:S(2)}, u32[]{:S(2)}) async-start(bf16[32,64,256]{2,1,0:T(8,128)(2,1)} %shard_map.332), calls=%async_computation.2 | async-start | bytes 2097152 | tf_op jit(solution)/shard_map/all_to_all | solution.py:859
  95.5 25.5 %collective-permute-start.7 = (bf16[2,256,1024]{2,1,0:T(8,128)(2,1)}, bf16[2,256,1024]{2,1,0:T(8,128)(2,1)}, u32[]{:S(2)}, u32[]{:S(2)}) collective-permute-start(bf16[2,256,1024]{2,1,0:T(8,128)(2,1)} %maximum_select_fusion), channel_id=1, source_target_pairs={{0,1},{1,0},{2,3},{3,2},{4,5},{5,4},{6,7},{7,6},{8,9},{9,8},{10,11... | collective-permute-start | bytes 3145736 | tf_op jit(solution)/shard_map/ppermute | solution.py:65
  144.4 17.4 %all-to-all-start.5 = ((bf16[8,64,1024]{2,1,0:T(8,128)(2,1)}), bf16[8,64,1024]{2,1,0:T(8,128)(2,1)S(1)}, u32[]{:S(2)}, u32[]{:S(2)}) async-start(bf16[8,64,1024]{2,1,0:T(8,128)(2,1)} %broadcast_in_dim.87), calls=%async_computation.5 | async-start | bytes 2097152 | tf_op jit(solution)/shard_map/all_to_all | solution.py:84
  185.2 17.4 %all-to-all-start.7 = ((bf16[8,64,1024]{2,1,0:T(8,128)(2,1)}), bf16[8,64,1024]{2,1,0:T(8,128)(2,1)S(1)}, u32[]{:S(2)}, u32[]{:S(2)}) async-start(bf16[8,64,1024]{2,1,0:T(8,128)(2,1)} %broadcast_in_dim.88), calls=%async_computation.7 | async-start | bytes 2097152 | tf_op jit(solution)/shard_map/all_to_all | solution.py:84
  188.8 41.9 %all-gather.3.cloned.1.call-start = ((), (), s32[]{:S(2)}) async-start(), calls=%async_computation.25 | async-start | bytes 1179648 | tf_op jit(solution)/shard_map/all_gather | solution.py:562
  219.4 15.9 %all-to-all-start.8 = ((f32[8,8,512]{2,1,0:T(8,128)}), f32[8,8,512]{2,1,0:T(8,128)}, u32[]{:S(2)}, u32[]{:S(2)}) async-start(f32[8,8,512]{2,1,0:T(8,128)} %broadcast_in_dim.92), calls=%async_computation.8 | async-start | bytes 262144 | tf_op jit(solution)/shard_map/all_to_all | solution.py:100
  223.4 94.6 %reduce-scatter.2.cloned.1.call-start = ((), (), s32[]{:S(2)}) async-start(), calls=%async_computation.24 | async-start | bytes 1179648 | tf_op jit(solution)/shard_map/reduce_scatter | solution.py:566
  277.8 16.8 %all-to-all-start.11 = ((bf16[8,64,1024]{2,1,0:T(8,128)(2,1)}), bf16[8,64,1024]{2,1,0:T(8,128)(2,1)}, u32[]{:S(2)}, u32[]{:S(2)}) async-start(bf16[8,64,1024]{2,1,0:T(8,128)(2,1)} %bitcast.467), calls=%async_computation.12 | async-start | bytes 2097152 | tf_op jit(solution)/shard_map/all_to_all | solution.py:89
  376.9 23.1 %all-to-all-start.14 = ((bf16[8,64,1024]{2,1,0:T(8,128)(2,1)}), bf16[8,64,1024]{2,1,0:T(8,128)(2,1)}, u32[]{:S(2)}, u32[]{:S(2)}) async-start(bf16[8,64,1024]{2,1,0:T(8,128)(2,1)} %bitcast.480), calls=%async_computation.15 | async-start | bytes 2097152 | tf_op jit(solution)/shard_map/all_to_all | solution.py:89
  403.0 18.9 %all-to-all-start.15 = ((bf16[8,64,1024]{2,1,0:T(8,128)(2,1)}), bf16[8,64,1024]{2,1,0:T(8,128)(2,1)S(1)}, u32[]{:S(2)}, u32[]{:S(2)}) async-start(bf16[8,64,1024]{2,1,0:T(8,128)(2,1)} %broadcast_in_dim.96), calls=%async_computation.16 | async-start | bytes 2097152 | tf_op jit(solution)/shard_map/all_to_all | solution.py:84
  413.1 47.2 %collective-permute-start.16 = (bf16[256,1024]{1,0:T(8,128)(2,1)}, bf16[256,1024]{1,0:T(8,128)(2,1)}, u32[]{:S(2)}, u32[]{:S(2)}) collective-permute-start(bf16[256,1024]{1,0:T(8,128)(2,1)} %pad_maximum_fusion.18), channel_id=1, source_target_pairs={{0,1},{1,0},{2,3},{3,2},{4,5},{5,4},{6,7},{7,6},{8,9},{9,8},{10,11... | collective-permute-start | bytes 1572872 | tf_op jit(solution)/shard_map/ppermute | solution.py:65
  428.3 22.4 %all-to-all-start.16 = ((bf16[8,64,1024]{2,1,0:T(8,128)(2,1)}), bf16[8,64,1024]{2,1,0:T(8,128)(2,1)}, u32[]{:S(2)}, u32[]{:S(2)}) async-start(bf16[8,64,1024]{2,1,0:T(8,128)(2,1)} %bitcast.466), calls=%async_computation.17 | async-start | bytes 2097152 | tf_op jit(solution)/shard_map/all_to_all | solution.py:89
  435.6 26.9 %collective-permute-start.22 = (bf16[1024,512]{1,0:T(8,128)(2,1)}, bf16[1024,512]{1,0:T(8,128)(2,1)}, u32[]{:S(2)}, u32[]{:S(2)}) collective-permute-start(bf16[1024,512]{1,0:T(8,128)(2,1)} %copy-done.217), channel_id=1, source_target_pairs={{0,1},{1,0},{2,3},{3,2},{4,5},{5,4},{6,7},{7,6},{8,9},{9,8},{10,11... | collective-permute-start | bytes 3145736 | tf_op jit(solution)/shard_map/ppermute | solution.py:65
  453.9 19.7 %all-to-all-start.17 = ((bf16[8,64,1024]{2,1,0:T(8,128)(2,1)}), bf16[8,64,1024]{2,1,0:T(8,128)(2,1)S(1)}, u32[]{:S(2)}, u32[]{:S(2)}) async-start(bf16[8,64,1024]{2,1,0:T(8,128)(2,1)} %broadcast_in_dim.97), calls=%async_computation.18 | async-start | bytes 2097152 | tf_op jit(solution)/shard_map/all_to_all | solution.py:84
  503.8 26.8 %all-to-all-start.19 = ((bf16[8,64,1024]{2,1,0:T(8,128)(2,1)}), bf16[8,64,1024]{2,1,0:T(8,128)(2,1)}, u32[]{:S(2)}, u32[]{:S(2)}) async-start(bf16[8,64,1024]{2,1,0:T(8,128)(2,1)} %bitcast.463), calls=%async_computation.20 | async-start | bytes 2097152 | tf_op jit(solution)/shard_map/all_to_all | solution.py:1058
  545.1 22.2 %all-to-all-start.20 = ((bf16[8,64,1024]{2,1,0:T(8,128)(2,1)}), bf16[8,64,1024]{2,1,0:T(8,128)(2,1)S(1)}, u32[]{:S(2)}, u32[]{:S(2)}) async-start(bf16[8,64,1024]{2,1,0:T(8,128)(2,1)} %bitcast.117), calls=%async_computation.21 | async-start | bytes 2097152 | tf_op jit(solution)/shard_map/all_to_all | solution.py:89
  567.3 52.0 %all-to-all-start.21 = ((bf16[128,16,768]{2,1,0:T(8,128)(2,1)}), bf16[128,16,768]{2,1,0:T(8,128)(2,1)}, u32[]{:S(2)}, u32[]{:S(2)}) async-start(bf16[128,16,768]{2,1,0:T(8,128)(2,1)} %fusion.10), calls=%async_computation.22 | async-start | bytes 6291456 | tf_op jit(solution)/shard_map/all_to_all | solution.py:973
  578.1 40.3 %collective-permute-start.18 = (bf16[64,1024]{1,0:T(8,128)(2,1)S(1)}, bf16[64,1024]{1,0:T(8,128)(2,1)S(1)}, u32[]{:S(2)}, u32[]{:S(2)}) collective-permute-start(bf16[64,1024]{1,0:T(8,128)(2,1)S(1)} %get-tuple-element.151), channel_id=1, source_target_pairs={{0,64},{64,0},{1,65},{65,1},{2,66},{66,2},{3,67},{67,3},{4,68},{68... | collective-permute-start | bytes 393224 | tf_op jit(solution)/shard_map/ppermute | solution.py:69
  624.5 24.8 %all-to-all-start.22 = ((bf16[4,16,12416]{2,1,0:T(8,128)(2,1)}), bf16[4,16,12416]{2,1,0:T(8,128)(2,1)S(1)}, u32[]{:S(2)}, u32[]{:S(2)}) async-start(bf16[4,16,12416]{2,1,0:T(8,128)(2,1)} %broadcast_in_dim.204), calls=%async_computation.23 | async-start | bytes 3178496 | tf_op jit(solution)/shard_map/all_to_all | solution.py:982
  (244 other events, 1873.6 us)
Sparse Core Ops, SparseCore 0:
  191.3 39.3 all-gather.2
  273.7 44.2 reduce-scatter.1

commit v3 on v2

--- a/solution.py
+++ b/solution.py
@@ -634,7 +634,7 @@
     return grad_hidden, *grads
 
 
-def backward_mixer(grad_hidden, kept, layer, rows, core, reduce_rows):
+def backward_mixer(grad_hidden, kept, layer, rows, core, reduce_rows, pending):
     (
         unit,
         scale,
@@ -675,6 +675,8 @@
     if reduce_rows is not None:
         row_total = reduce_rows(grad_mamba, grad_out)
         mine = joined(mine, row_total)
+    else:
+        mine = joined(mine, pending)
     grad_near = jnp.concatenate(
         [
             grad_gate_raw[:, :LANES],
@@ -1058,8 +1060,7 @@
         met = lax.all_to_all(
             jnp.concatenate([first_rows, last_rows]), ("section", "rep"), 0, 0, tiled=True
         )
-        met = met.reshape(2 * reps, -1, MODEL_WIDTH).astype(F32)
-        return joined(jnp.sum(met, axis=0), outs[1]).astype(BF)
+        return met
 
     sent = [None, None]
     grad = own_target.astype(F32)
@@ -1076,6 +1077,7 @@
             row_weights[layer],
             core_word,
             reduce_rows if layer == 0 else None,
+            total,
         )
         if layer == 1:
             last_rows = rows_of(*row_total, grad_down)
@@ -1087,6 +1089,8 @@
 
     section_out = exchanged(outs[0], joined(outs[1], grad_near))[None, :, None]
     input_grad = exchanged(*input_grads)[None, :, None]
+    row_total = row_total.reshape(2 * reps, -1, MODEL_WIDTH).astype(F32)
+    row_total = jnp.sum(row_total, axis=0).astype(BF)
     columns = by_weight(over_all(jnp.concatenate(sent)))
     totals = to_all(jnp.concatenate([columns, row_total.reshape(part, -1)], axis=1), "rep", reps)
     columns = totals[:, : columns.shape[1]]

time: 679 us -> 661 us (0.973)
  blocking collectives: 79 us -> 63.5 us
  waiting for transfers between devices: 189 us -> 179 us
    reduce_scatter x1, waiting for transfers between devices: 21.8 us -> 0.01 us  [collect_later(): lax.psum_scatter(partial.astype(BF), 'shard', scatter_dimension=0, tiled=...]
    all_to_all x2 -> x1, blocking collectives: 29.6 us -> 14 us  [spread(): lax.all_to_all(copies, 'shard', 0, 0, axis_index_groups=same_core(), tile...]
    all_to_all x5 -> x6, waiting for transfers between devices: 40.9 us -> 55.7 us  [spread(): lax.all_to_all(copies, 'shard', 0, 0, axis_index_groups=same_core(), tile...]
    all_to_all x5 -> x6, starting transfers between devices: 17.9 us -> 22.3 us  [spread(): lax.all_to_all(copies, 'shard', 0, 0, axis_index_groups=same_core(), tile...]
    unnamed x441 -> x467, local copies, waits for them, and re-layouts: 20.9 us -> 22.5 us
  transfers between devices with their start and end apart: 44 -> 45, of which waited for: 23 -> 22; matrix products, arithmetic and copies ran while one was open for 20% -> 21% of each run, Pallas kernels for 5% -> 7%
where the time goes in v3:
time: 661 us; the launch traced here: 648 us
  waiting for transfers between devices  179 us (27%)
  starting transfers between devices  104 us (16%)
  local copies, waits for them, and re-layouts  99.5 us (15%)
  matrix products  67 us (10%)
  blocking collectives  63.5 us (10%)
  other arithmetic  51.7 us (8%)
  Pallas kernels  48.8 us (7%)
  between operations  35.4 us (5%)
    all_to_all x6, waiting for transfers between devices, spread(): lax.all_to_all(copies, 'shard', 0, 0, axis_index_groups=same_core(), tile...  55.7 us
    all_to_all x3, blocking collectives, collect(): lax.all_to_all(partial.astype(BF), 'shard', 0, 0, axis_index_groups=same_...  49.5 us
    ppermute x4, waiting for transfers between devices, swap_sections(): return lax.ppermute(x, 'section', [(0, 1), (1, 0)])  38.9 us
    all_to_all x1, waiting for transfers between devices, body(): met = lax.all_to_all(cut, everywhere, 0, 0, tiled=True)  25.9 us
    dot_general x14, matrix products, dot_back(): lax.dot_general(former, latter, (((1,), (1,)), ((), ())), preferred_eleme...  24.4 us
    pallas_call x2, Pallas kernels, mixer_back(): pl.pallas_call(mixer_back_kernel, out_shape=(jax.ShapeDtypeStruct((rows,...  24.4 us
    all_to_all x4, waiting for transfers between devices, collect(): lax.all_to_all(partial.astype(BF), 'shard', 0, 0, axis_index_groups=same_...  23 us
    unnamed x467, local copies, waits for them, and re-layouts  22.5 us
  transfers between devices with their start and end apart: 45, of which 22 were waited for; matrix products, arithmetic and copies ran while one was open for 21% of the time, Pallas kernels for 7%

profile of v3, /device:TPU:0, one launch (start us, length us, event | category | flops | bytes accessed | tf_op | source)
XLA Modules:
  0.0 648.4 jit_solution(3200167865349872263)
XLA Ops:
  19.4 5.6 all-to-all-start.1
  29.6 25.9 %all-to-all-done.1 = bf16[32,64,512]{2,1,0:T(8,128)(2,1)} async-done(((bf16[32,64,512]{2,1,0:T(8,128)(2,1)}), bf16[32,64,512]{2,1,0:T(8,128)(2,1)}, u32[]{:S(2)}, u32[]{:S(2)}) %all-to-all-start.1) | async-done | bytes 2097184 | tf_op jit(solution)/shard_map/all_to_all | solution.py:853
  77.1 5.0 all-to-all-start.2
  115.7 5.1 all-to-all-done.3
  125.4 17.4 %all_to_all.194 = bf16[8,64,1024]{2,1,0:T(8,128)(2,1)S(1)} all-to-all(bf16[8,64,1024]{2,1,0:T(8,128)(2,1)S(1)} %bitcast.462), channel_id=1, replica_groups={{0,2,4,6,8,10,12,14},{1,3,5,7,9,11,13,15},{16,18,20,22,24,26,28,30},{17..., dimensions={0} | all-to-all | bytes 2097152 | tf_op jit(solution)/shard_map/all_to_all | solution.py:89
  151.7 10.1 %all-to-all-done.5 = bf16[8,64,1024]{2,1,0:T(8,128)(2,1)S(1)} async-done(((bf16[8,64,1024]{2,1,0:T(8,128)(2,1)}), bf16[8,64,1024]{2,1,0:T(8,128)(2,1)S(1)}, u32[]{:S(2)}, u32[]{:S(2)}) %all-to-all-start.5) | async-done | bytes 1048608 | tf_op jit(solution)/shard_map/all_to_all | solution.py:84
  165.4 17.6 %all_to_all.195 = bf16[8,64,1024]{2,1,0:T(8,128)(2,1)S(1)} all-to-all(bf16[8,64,1024]{2,1,0:T(8,128)(2,1)S(1)} %bitcast.458), channel_id=1, replica_groups={{0,2,4,6,8,10,12,14},{1,3,5,7,9,11,13,15},{16,18,20,22,24,26,28,30},{17..., dimensions={0} | all-to-all | bytes 2097152 | tf_op jit(solution)/shard_map/all_to_all | solution.py:89
  190.8 11.8 %all-to-all-done.7 = bf16[8,64,1024]{2,1,0:T(8,128)(2,1)S(1)} async-done(((bf16[8,64,1024]{2,1,0:T(8,128)(2,1)}), bf16[8,64,1024]{2,1,0:T(8,128)(2,1)S(1)}, u32[]{:S(2)}, u32[]{:S(2)}) %all-to-all-start.7) | async-done | bytes 1048608 | tf_op jit(solution)/shard_map/all_to_all | solution.py:84
  223.6 7.6 %all-gather.3.cloned.1.call-done = bf16[1,1,512,1024]{3,2,1,0:T(8,128)(2,1)} async-done(((bf16[1,1,64,1024]{3,2,1,0:T(8,128)(2,1)}), bf16[1,1,512,1024]{3,2,1,0:T(8,128)(2,1)}) %all-gather.3.cloned.1.call-update) | async-done | bytes 1048592 | tf_op jit(solution)/shard_map/all_gather | solution.py:562
  239.3 14.6 %all_to_all.196 = bf16[8,64,1024]{2,1,0:T(8,128)(2,1)S(1)} all-to-all(bf16[8,64,1024]{2,1,0:T(8,128)(2,1)S(1)} %bitcast.463), channel_id=1, replica_groups={{0,2,4,6,8,10,12,14},{1,3,5,7,9,11,13,15},{16,18,20,22,24,26,28,30},{17..., dimensions={0} | all-to-all | bytes 2097152 | tf_op jit(solution)/shard_map/all_to_all | solution.py:89
  254.5 14.0 %all_to_all.197 = bf16[8,64,1024]{2,1,0:T(8,128)(2,1)S(1)} all-to-all(bf16[8,64,1024]{2,1,0:T(8,128)(2,1)S(1)} %broadcast_in_dim.93), channel_id=1, replica_groups={{0,2,4,6,8,10,12,14},{1,3,5,7,9,11,13,15},{16,18,20,22,24,26,28,30},{17..., dimensions={0} | all-to-all | bytes 2097152 | tf_op jit(solution)/shard_map/all_to_all | solution.py:84
  300.1 12.2 %all-to-all-done.12 = bf16[8,64,1024]{2,1,0:T(8,128)(2,1)} async-done(((bf16[8,64,1024]{2,1,0:T(8,128)(2,1)}), bf16[8,64,1024]{2,1,0:T(8,128)(2,1)}, u32[]{:S(2)}, u32[]{:S(2)}) %all-to-all-start.12) | async-done | bytes 1048608 | tf_op jit(solution)/shard_map/all_to_all | solution.py:84
  335.4 12.2 %shard_map.337 = (f32[512,384]{1,0:T(8,128)S(1)}, bf16[512,384]{1,0:T(8,128)(2,1)S(1)}, f32[8,384]{1,0:T(8,128)S(1)}, f32[8,128]{1,0:T(8,128)S(1)}) custom-call(s32[1]{0:T(128)} %bitcast.1.core_ref, bf16[512,256]{1,0:T(8,128)(2,1)S(1)} %copy-done.13, bf16[512,256]{1,0:T(8,128)(2,1)S(1)} %copy-done.5, bf16[512,512]{1,0:T(8,128)(2,1)S(1)} %convolution_convert_fusion.6.far_ref, ...), custom_call_target="tpu_custom_call" | custom-call | flops 1000000 | bytes 10000 | tf_op jit(solution)/shard_map/pallas_call | solution.py:421
  358.5 6.0 all-to-all-start.14
  392.2 11.3 %all-to-all-done.15 = bf16[8,64,1024]{2,1,0:T(8,128)(2,1)S(1)} async-done(((bf16[8,64,1024]{2,1,0:T(8,128)(2,1)}), bf16[8,64,1024]{2,1,0:T(8,128)(2,1)S(1)}, u32[]{:S(2)}, u32[]{:S(2)}) %all-to-all-start.15) | async-done | bytes 1048608 | tf_op jit(solution)/shard_map/all_to_all | solution.py:84
  426.0 6.3 all-to-all-done.16
  448.0 7.2 %all-to-all-done.17 = bf16[8,64,1024]{2,1,0:T(8,128)(2,1)S(1)} async-done(((bf16[8,64,1024]{2,1,0:T(8,128)(2,1)}), bf16[8,64,1024]{2,1,0:T(8,128)(2,1)S(1)}, u32[]{:S(2)}, u32[]{:S(2)}) %all-to-all-start.17) | async-done | bytes 1048608 | tf_op jit(solution)/shard_map/all_to_all | solution.py:84
  485.5 8.5 %all-to-all-start.19 = ((bf16[8,64,1024]{2,1,0:T(8,128)(2,1)}), bf16[8,64,1024]{2,1,0:T(8,128)(2,1)}, u32[]{:S(2)}, u32[]{:S(2)}) async-start(bf16[8,64,1024]{2,1,0:T(8,128)(2,1)} %bitcast.461), calls=%async_computation.20 | async-start | bytes 2097152 | tf_op jit(solution)/shard_map/all_to_all | solution.py:1060
  494.3 12.2 %shard_map.339 = (f32[512,384]{1,0:T(8,128)S(1)}, bf16[512,384]{1,0:T(8,128)(2,1)S(1)}, f32[8,384]{1,0:T(8,128)S(1)}, f32[8,128]{1,0:T(8,128)S(1)}) custom-call(s32[1]{0:T(128)} %bitcast.1.core_ref, bf16[512,256]{1,0:T(8,128)(2,1)S(1)} %copy-done.9, bf16[512,256]{1,0:T(8,128)(2,1)S(1)} %convolution_convert_fusion.10.maps_ref, ...), custom_call_target="tpu_custom_call" | custom-call | flops 1000000 | bytes 10000 | tf_op jit(solution)/shard_map/pallas_call | solution.py:421
  527.3 5.2 all-to-all-start.20
  541.4 8.2 %all-to-all-done.20 = bf16[8,64,1024]{2,1,0:T(8,128)(2,1)S(1)} async-done(((bf16[8,64,1024]{2,1,0:T(8,128)(2,1)}), bf16[8,64,1024]{2,1,0:T(8,128)(2,1)S(1)}, u32[]{:S(2)}, u32[]{:S(2)}) %all-to-all-start.20) | async-done | bytes 1048608 | tf_op jit(solution)/shard_map/all_to_all | solution.py:89
  549.5 9.0 %all-to-all-start.21 = ((bf16[128,16,768]{2,1,0:T(8,128)(2,1)}), bf16[128,16,768]{2,1,0:T(8,128)(2,1)}, u32[]{:S(2)}, u32[]{:S(2)}) async-start(bf16[128,16,768]{2,1,0:T(8,128)(2,1)} %fusion.10), calls=%async_computation.22 | async-start | bytes 6291456 | tf_op jit(solution)/shard_map/all_to_all | solution.py:975
  566.7 34.0 %collective-permute-done.18 = bf16[64,1024]{1,0:T(8,128)(2,1)S(1)} collective-permute-done((bf16[64,1024]{1,0:T(8,128)(2,1)S(1)}, bf16[64,1024]{1,0:T(8,128)(2,1)S(1)}, u32[]{:S(2)}, u32[]{:S(2)}) %collective-permute-start.18) | collective-permute-done | bytes 131104 | tf_op jit(solution)/shard_map/ppermute | solution.py:69
  620.7 10.9 %all-to-all-done.22 = bf16[4,16,12416]{2,1,0:T(8,128)(2,1)S(1)} async-done(((bf16[4,16,12416]{2,1,0:T(8,128)(2,1)}), bf16[4,16,12416]{2,1,0:T(8,128)(2,1)S(1)}, u32[]{:S(2)}, u32[]{:S(2)}) %all-to-all-start.22) | async-done | bytes 1589280 | tf_op jit(solution)/shard_map/all_to_all | solution.py:984
  (892 shorter events, 335.3 us)
Async XLA Ops:
  8.6 20.9 %collective-permute-start.3 = (f32[168]{0:T(256)S(1)}, f32[168]{0:T(256)S(1)}, u32[]{:S(2)}, u32[]{:S(2)}) collective-permute-start(f32[168]{0:T(256)S(1)} %pad_maximum_fusion.68), channel_id=1, source_target_pairs={{0,64},{64,0},{1,65},{65,1},{2,66},{66,2},{3,67},{67,3},{4,68},{68... | collective-permute-start | bytes 2024 | tf_op jit(solution)/shard_map/ppermute | solution.py:69
  19.4 36.1 %all-to-all-start.1 = ((bf16[32,64,512]{2,1,0:T(8,128)(2,1)}), bf16[32,64,512]{2,1,0:T(8,128)(2,1)}, u32[]{:S(2)}, u32[]{:S(2)}) async-start(bf16[32,64,512]{2,1,0:T(8,128)(2,1)} %shard_map.330), calls=%async_computation.1 | async-start | bytes 4194304 | tf_op jit(solution)/shard_map/all_to_all | solution.py:853
  56.6 20.5 %all-to-all-start = ((bf16[8,64,1024]{2,1,0:T(8,128)(2,1)}), bf16[8,64,1024]{2,1,0:T(8,128)(2,1)S(1)}, u32[]{:S(2)}, u32[]{:S(2)}) async-start(bf16[8,64,1024]{2,1,0:T(8,128)(2,1)} %broadcast_in_dim.78), calls=%async_computation | async-start | bytes 2097152 | tf_op jit(solution)/shard_map/all_to_all | solution.py:84
  60.2 23.4 %collective-permute-start = (bf16[2,1024,512]{2,1,0:T(8,128)(2,1)}, bf16[2,1024,512]{2,1,0:T(8,128)(2,1)}, u32[]{:S(2)}, u32[]{:S(2)}) collective-permute-start(bf16[2,1024,512]{2,1,0:T(8,128)(2,1)} %bitcast.10), channel_id=1, source_target_pairs={{0,1},{1,0},{2,3},{3,2},{4,5},{5,4},{6,7},{7,6},{8,9},{9,8},{10,11... | collective-permute-start | bytes 6291464 | tf_op jit(solution)/shard_map/ppermute | solution.py:65
  70.6 22.6 %collective-permute-start.6 = (bf16[256,1024]{1,0:T(8,128)(2,1)}, bf16[256,1024]{1,0:T(8,128)(2,1)}, u32[]{:S(2)}, u32[]{:S(2)}) collective-permute-start(bf16[256,1024]{1,0:T(8,128)(2,1)} %maximum_add_fusion.3), channel_id=1, source_target_pairs={{0,64},{64,0},{1,65},{65,1},{2,66},{66,2},{3,67},{67,3},{4,68},{68... | collective-permute-start | bytes 1572872 | tf_op jit(solution)/shard_map/ppermute | solution.py:69
  77.1 23.1 %all-to-all-start.2 = ((bf16[32,64,256]{2,1,0:T(8,128)(2,1)}), bf16[32,64,256]{2,1,0:T(8,128)(2,1)}, u32[]{:S(2)}, u32[]{:S(2)}) async-start(bf16[32,64,256]{2,1,0:T(8,128)(2,1)} %shard_map.332), calls=%async_computation.2 | async-start | bytes 2097152 | tf_op jit(solution)/shard_map/all_to_all | solution.py:861
  95.4 25.6 %collective-permute-start.7 = (bf16[2,256,1024]{2,1,0:T(8,128)(2,1)}, bf16[2,256,1024]{2,1,0:T(8,128)(2,1)}, u32[]{:S(2)}, u32[]{:S(2)}) collective-permute-start(bf16[2,256,1024]{2,1,0:T(8,128)(2,1)} %maximum_select_fusion), channel_id=1, source_target_pairs={{0,1},{1,0},{2,3},{3,2},{4,5},{5,4},{6,7},{7,6},{8,9},{9,8},{10,11... | collective-permute-start | bytes 3145736 | tf_op jit(solution)/shard_map/ppermute | solution.py:65
  144.4 17.4 %all-to-all-start.5 = ((bf16[8,64,1024]{2,1,0:T(8,128)(2,1)}), bf16[8,64,1024]{2,1,0:T(8,128)(2,1)S(1)}, u32[]{:S(2)}, u32[]{:S(2)}) async-start(bf16[8,64,1024]{2,1,0:T(8,128)(2,1)} %broadcast_in_dim.87), calls=%async_computation.5 | async-start | bytes 2097152 | tf_op jit(solution)/shard_map/all_to_all | solution.py:84
  185.2 17.4 %all-to-all-start.7 = ((bf16[8,64,1024]{2,1,0:T(8,128)(2,1)}), bf16[8,64,1024]{2,1,0:T(8,128)(2,1)S(1)}, u32[]{:S(2)}, u32[]{:S(2)}) async-start(bf16[8,64,1024]{2,1,0:T(8,128)(2,1)} %broadcast_in_dim.88), calls=%async_computation.7 | async-start | bytes 2097152 | tf_op jit(solution)/shard_map/all_to_all | solution.py:84
  188.8 42.5 %all-gather.3.cloned.1.call-start = ((), (), s32[]{:S(2)}) async-start(), calls=%async_computation.25 | async-start | bytes 1179648 | tf_op jit(solution)/shard_map/all_gather | solution.py:562
  219.4 16.5 %all-to-all-start.8 = ((f32[8,8,512]{2,1,0:T(8,128)}), f32[8,8,512]{2,1,0:T(8,128)}, u32[]{:S(2)}, u32[]{:S(2)}) async-start(f32[8,8,512]{2,1,0:T(8,128)} %broadcast_in_dim.92), calls=%async_computation.8 | async-start | bytes 262144 | tf_op jit(solution)/shard_map/all_to_all | solution.py:100
  294.1 18.1 %all-to-all-start.12 = ((bf16[8,64,1024]{2,1,0:T(8,128)(2,1)}), bf16[8,64,1024]{2,1,0:T(8,128)(2,1)}, u32[]{:S(2)}, u32[]{:S(2)}) async-start(bf16[8,64,1024]{2,1,0:T(8,128)(2,1)} %broadcast_in_dim.94), calls=%async_computation.13 | async-start | bytes 2097152 | tf_op jit(solution)/shard_map/all_to_all | solution.py:84
  298.5 52.9 %reduce-scatter.2.cloned.1.call-start = ((), (), s32[]{:S(2)}) async-start(), calls=%async_computation.24 | async-start | bytes 1179648 | tf_op jit(solution)/shard_map/reduce_scatter | solution.py:566
  358.5 23.1 %all-to-all-start.14 = ((bf16[8,64,1024]{2,1,0:T(8,128)(2,1)}), bf16[8,64,1024]{2,1,0:T(8,128)(2,1)}, u32[]{:S(2)}, u32[]{:S(2)}) async-start(bf16[8,64,1024]{2,1,0:T(8,128)(2,1)} %bitcast.478), calls=%async_computation.15 | async-start | bytes 2097152 | tf_op jit(solution)/shard_map/all_to_all | solution.py:89
  384.7 18.9 %all-to-all-start.15 = ((bf16[8,64,1024]{2,1,0:T(8,128)(2,1)}), bf16[8,64,1024]{2,1,0:T(8,128)(2,1)S(1)}, u32[]{:S(2)}, u32[]{:S(2)}) async-start(bf16[8,64,1024]{2,1,0:T(8,128)(2,1)} %broadcast_in_dim.96), calls=%async_computation.16 | async-start | bytes 2097152 | tf_op jit(solution)/shard_map/all_to_all | solution.py:84
  392.2 49.8 %collective-permute-start.16 = (bf16[256,1024]{1,0:T(8,128)(2,1)}, bf16[256,1024]{1,0:T(8,128)(2,1)}, u32[]{:S(2)}, u32[]{:S(2)}) collective-permute-start(bf16[256,1024]{1,0:T(8,128)(2,1)} %pad_maximum_fusion.18), channel_id=1, source_target_pairs={{0,1},{1,0},{2,3},{3,2},{4,5},{5,4},{6,7},{7,6},{8,9},{9,8},{10,11... | collective-permute-start | bytes 1572872 | tf_op jit(solution)/shard_map/ppermute | solution.py:65
  409.9 22.3 %all-to-all-start.16 = ((bf16[8,64,1024]{2,1,0:T(8,128)(2,1)}), bf16[8,64,1024]{2,1,0:T(8,128)(2,1)}, u32[]{:S(2)}, u32[]{:S(2)}) async-start(bf16[8,64,1024]{2,1,0:T(8,128)(2,1)} %bitcast.464), calls=%async_computation.17 | async-start | bytes 2097152 | tf_op jit(solution)/shard_map/all_to_all | solution.py:89
  417.3 26.8 %collective-permute-start.22 = (bf16[1024,512]{1,0:T(8,128)(2,1)}, bf16[1024,512]{1,0:T(8,128)(2,1)}, u32[]{:S(2)}, u32[]{:S(2)}) collective-permute-start(bf16[1024,512]{1,0:T(8,128)(2,1)} %copy-done.230), channel_id=1, source_target_pairs={{0,1},{1,0},{2,3},{3,2},{4,5},{5,4},{6,7},{7,6},{8,9},{9,8},{10,11... | collective-permute-start | bytes 3145736 | tf_op jit(solution)/shard_map/ppermute | solution.py:65
  435.5 19.7 %all-to-all-start.17 = ((bf16[8,64,1024]{2,1,0:T(8,128)(2,1)}), bf16[8,64,1024]{2,1,0:T(8,128)(2,1)S(1)}, u32[]{:S(2)}, u32[]{:S(2)}) async-start(bf16[8,64,1024]{2,1,0:T(8,128)(2,1)} %broadcast_in_dim.97), calls=%async_computation.18 | async-start | bytes 2097152 | tf_op jit(solution)/shard_map/all_to_all | solution.py:84
  485.5 28.0 %all-to-all-start.19 = ((bf16[8,64,1024]{2,1,0:T(8,128)(2,1)}), bf16[8,64,1024]{2,1,0:T(8,128)(2,1)}, u32[]{:S(2)}, u32[]{:S(2)}) async-start(bf16[8,64,1024]{2,1,0:T(8,128)(2,1)} %bitcast.461), calls=%async_computation.20 | async-start | bytes 2097152 | tf_op jit(solution)/shard_map/all_to_all | solution.py:1060
  527.3 22.2 %all-to-all-start.20 = ((bf16[8,64,1024]{2,1,0:T(8,128)(2,1)}), bf16[8,64,1024]{2,1,0:T(8,128)(2,1)S(1)}, u32[]{:S(2)}, u32[]{:S(2)}) async-start(bf16[8,64,1024]{2,1,0:T(8,128)(2,1)} %bitcast.118), calls=%async_computation.21 | async-start | bytes 2097152 | tf_op jit(solution)/shard_map/all_to_all | solution.py:89
  549.5 52.1 %all-to-all-start.21 = ((bf16[128,16,768]{2,1,0:T(8,128)(2,1)}), bf16[128,16,768]{2,1,0:T(8,128)(2,1)}, u32[]{:S(2)}, u32[]{:S(2)}) async-start(bf16[128,16,768]{2,1,0:T(8,128)(2,1)} %fusion.10), calls=%async_computation.22 | async-start | bytes 6291456 | tf_op jit(solution)/shard_map/all_to_all | solution.py:975
  560.5 40.2 %collective-permute-start.18 = (bf16[64,1024]{1,0:T(8,128)(2,1)S(1)}, bf16[64,1024]{1,0:T(8,128)(2,1)S(1)}, u32[]{:S(2)}, u32[]{:S(2)}) collective-permute-start(bf16[64,1024]{1,0:T(8,128)(2,1)S(1)} %get-tuple-element.135), channel_id=1, source_target_pairs={{0,64},{64,0},{1,65},{65,1},{2,66},{66,2},{3,67},{67,3},{4,68},{68... | collective-permute-start | bytes 393224 | tf_op jit(solution)/shard_map/ppermute | solution.py:69
  606.8 24.9 %all-to-all-start.22 = ((bf16[4,16,12416]{2,1,0:T(8,128)(2,1)}), bf16[4,16,12416]{2,1,0:T(8,128)(2,1)S(1)}, u32[]{:S(2)}, u32[]{:S(2)}) async-start(bf16[4,16,12416]{2,1,0:T(8,128)(2,1)} %broadcast_in_dim.204), calls=%async_computation.23 | async-start | bytes 3178496 | tf_op jit(solution)/shard_map/all_to_all | solution.py:984
  (258 other events, 1802.0 us)
Sparse Core Ops, SparseCore 0:
  191.8 39.3 all-gather.2
  301.7 43.8 reduce-scatter.1

commit v4 on v3

--- a/solution.py
+++ b/solution.py
@@ -581,12 +581,13 @@
     mine, theirs, starts = mixer(core, own, layer)
     mixed = jnp.concatenate([mine, swap_cores(theirs)], axis=1).astype(F32)
     gated = mixed * jax.nn.silu(gate_raw)
-    attended, stat = attend(core, own, own[0] if also is None else also)
+    attended, stat = attend(core, own, own[0])
     rows = row_weights(mine)
     squares = joined(gated * gated, layer["wide"])
     ssm_scale = lax.rsqrt(chip_sums(squares, attended) / INNER + EPSILON)
     mixer_low = (gated * ssm_scale * layer["gain"]).astype(BF)
-    hidden = x + collect(dot_plain(mixer_low, rows["mamba"]) + dot_plain(attended, rows["out"]))
+    partial = dot_plain(mixer_low, rows["mamba"]) + dot_plain(attended, rows["out"])
+    hidden = x + collect(partial, *also)
     kept = (
         unit,
         scale,
@@ -941,17 +942,18 @@
 
     x = own_input
     outs = []
-    target_own = None
+    also = ()
     kept_mixer, kept_wide, row_weights = [], [], []
     for layer in range(2):
         if layer == 1:
             unit, scale = normalize(x)
             own_unit = spread(unit.astype(BF))
         hidden, kept, rows = forward_mixer(
-            x, unit, scale, own_unit, layers[layer], core_word, target_own, rows_at(layer)
+            x, unit, scale, own_unit, layers[layer], core_word, also, rows_at(layer)
         )
         if layer == 0:
             target_own = gather_later(joined(own_target, hidden))
+            also = (target_own,)
         row_weights.append(rows)
         kept_mixer.append(kept)
         partial, kept = forward_wide(hidden, layers[layer], rows)

time: 661 us -> 705 us (1.067)
  waiting for transfers between devices: 179 us -> 207 us
  blocking collectives: 63.5 us -> 49.6 us
  local copies, waits for them, and re-layouts: 99.5 us -> 111 us
  matrix products: 67 us -> 74.5 us
    all_gather x1, waiting for transfers between devices: 7.62 us -> 33.9 us  [gather_later(): lax.all_gather(rows, 'shard', axis=0, tiled=True, axis_index_groups=same_...]
    all_to_all x3 -> x2, blocking collectives: 49.5 us -> 34.7 us  [collect(): lax.all_to_all(partial.astype(BF), 'shard', 0, 0, axis_index_groups=same_...]
    unnamed x467 -> x439, local copies, waits for them, and re-layouts: 22.5 us -> 28.8 us
    all_to_all x4 -> x5, starting transfers between devices: 19.7 us -> 25.3 us  [collect(): lax.all_to_all(partial.astype(BF), 'shard', 0, 0, axis_index_groups=same_...]
    slice x26 -> x27, local copies, waits for them, and re-layouts: 18.5 us -> 20.1 us  [joined(): zero = sum(((m[(0,) * m.ndim] * 0).astype(F32) for m in met))]
    all_to_all x4 -> x5, waiting for transfers between devices: 23 us -> 23.9 us  [collect(): lax.all_to_all(partial.astype(BF), 'shard', 0, 0, axis_index_groups=same_...]
  transfers between devices with their start and end apart: 45 -> 46, of which waited for: 22 -> 23; matrix products, arithmetic and copies ran while one was open for 21% -> 21% of each run, Pallas kernels for 7% -> 6%
where the time goes in v4:
time: 705 us; the launch traced here: 692 us
  waiting for transfers between devices  207 us (29%)
  local copies, waits for them, and re-layouts  111 us (16%)
  starting transfers between devices  107 us (15%)
  matrix products  74.5 us (11%)
  other arithmetic  56.9 us (8%)
  blocking collectives  49.6 us (7%)
  Pallas kernels  49.4 us (7%)
  between operations  35.9 us (5%)
    all_to_all x6, waiting for transfers between devices, spread(): lax.all_to_all(copies, 'shard', 0, 0, axis_index_groups=same_core(), tile...  53.7 us
    ppermute x4, waiting for transfers between devices, swap_sections(): return lax.ppermute(x, 'section', [(0, 1), (1, 0)])  38.9 us
    all_to_all x2, blocking collectives, collect(): lax.all_to_all(partial.astype(BF), 'shard', 0, 0, axis_index_groups=same_...  34.7 us
    all_gather x1, waiting for transfers between devices, gather_later(): lax.all_gather(rows, 'shard', axis=0, tiled=True, axis_index_groups=same_...  33.9 us
    unnamed x439, local copies, waits for them, and re-layouts  28.8 us
    all_to_all x1, waiting for transfers between devices, body(): met = lax.all_to_all(cut, everywhere, 0, 0, tiled=True)  25.9 us
    all_to_all x5, starting transfers between devices, collect(): lax.all_to_all(partial.astype(BF), 'shard', 0, 0, axis_index_groups=same_...  25.3 us
    dot_general x14, matrix products, dot_back(): lax.dot_general(former, latter, (((1,), (1,)), ((), ())), preferred_eleme...  24.6 us
  transfers between devices with their start and end apart: 46, of which 23 were waited for; matrix products, arithmetic and copies ran while one was open for 21% of the time, Pallas kernels for 6%

profile of v4, /device:TPU:0, one launch (start us, length us, event | category | flops | bytes accessed | tf_op | source)
XLA Modules:
  0.0 692.2 jit_solution(7013179781878268386)
XLA Ops:
  19.4 5.6 all-to-all-start.1
  29.5 25.9 %all-to-all-done.1 = bf16[32,64,512]{2,1,0:T(8,128)(2,1)} async-done(((bf16[32,64,512]{2,1,0:T(8,128)(2,1)}), bf16[32,64,512]{2,1,0:T(8,128)(2,1)}, u32[]{:S(2)}, u32[]{:S(2)}) %all-to-all-start.1) | async-done | bytes 2097184 | tf_op jit(solution)/shard_map/all_to_all | solution.py:854
  116.4 5.9 all-to-all-done.3
  128.9 17.2 %all_to_all.194 = bf16[8,64,1024]{2,1,0:T(8,128)(2,1)S(1)} all-to-all(bf16[8,64,1024]{2,1,0:T(8,128)(2,1)S(1)} %bitcast.461), channel_id=1, replica_groups={{0,2,4,6,8,10,12,14},{1,3,5,7,9,11,13,15},{16,18,20,22,24,26,28,30},{17..., dimensions={0} | all-to-all | bytes 2097152 | tf_op jit(solution)/shard_map/all_to_all | solution.py:89
  155.6 9.7 %all-to-all-done.5 = bf16[8,64,1024]{2,1,0:T(8,128)(2,1)S(1)} async-done(((bf16[8,64,1024]{2,1,0:T(8,128)(2,1)}), bf16[8,64,1024]{2,1,0:T(8,128)(2,1)S(1)}, u32[]{:S(2)}, u32[]{:S(2)}) %all-to-all-start.5) | async-done | bytes 1048608 | tf_op jit(solution)/shard_map/all_to_all | solution.py:84
  170.1 17.5 %all_to_all.195 = bf16[8,64,1024]{2,1,0:T(8,128)(2,1)S(1)} all-to-all(bf16[8,64,1024]{2,1,0:T(8,128)(2,1)S(1)} %bitcast.456), channel_id=1, replica_groups={{0,2,4,6,8,10,12,14},{1,3,5,7,9,11,13,15},{16,18,20,22,24,26,28,30},{17..., dimensions={0} | all-to-all | bytes 2097152 | tf_op jit(solution)/shard_map/all_to_all | solution.py:89
  193.5 13.7 %all-to-all-done.7 = bf16[8,64,1024]{2,1,0:T(8,128)(2,1)S(1)} async-done(((bf16[8,64,1024]{2,1,0:T(8,128)(2,1)}), bf16[8,64,1024]{2,1,0:T(8,128)(2,1)S(1)}, u32[]{:S(2)}, u32[]{:S(2)}) %all-to-all-start.7) | async-done | bytes 1048608 | tf_op jit(solution)/shard_map/all_to_all | solution.py:84
  244.8 5.6 all-to-all-start.9
  250.4 33.9 %all-gather.3.cloned.1.call-done = bf16[1,1,512,1024]{3,2,1,0:T(8,128)(2,1)} async-done(((bf16[1,1,64,1024]{3,2,1,0:T(8,128)(2,1)}), bf16[1,1,512,1024]{3,2,1,0:T(8,128)(2,1)}) %all-gather.3.cloned.1.call-update) | async-done | bytes 1048592 | tf_op jit(solution)/shard_map/all_gather | solution.py:562
  289.9 14.9 %all_to_all.196 = bf16[8,64,1024]{2,1,0:T(8,128)(2,1)S(1)} all-to-all(bf16[8,64,1024]{2,1,0:T(8,128)(2,1)S(1)} %broadcast_in_dim.93), channel_id=1, replica_groups={{0,2,4,6,8,10,12,14},{1,3,5,7,9,11,13,15},{16,18,20,22,24,26,28,30},{17..., dimensions={0} | all-to-all | bytes 2097152 | tf_op jit(solution)/shard_map/all_to_all | solution.py:84
  339.9 13.8 %all-to-all-done.12 = bf16[8,64,1024]{2,1,0:T(8,128)(2,1)} async-done(((bf16[8,64,1024]{2,1,0:T(8,128)(2,1)}), bf16[8,64,1024]{2,1,0:T(8,128)(2,1)}, u32[]{:S(2)}, u32[]{:S(2)}) %all-to-all-start.12) | async-done | bytes 1048608 | tf_op jit(solution)/shard_map/all_to_all | solution.py:84
  379.8 12.2 %shard_map.337 = (f32[512,384]{1,0:T(8,128)S(1)}, bf16[512,384]{1,0:T(8,128)(2,1)S(1)}, f32[8,384]{1,0:T(8,128)S(1)}, f32[8,128]{1,0:T(8,128)S(1)}) custom-call(s32[1]{0:T(128)} %bitcast.1.core_ref, bf16[512,256]{1,0:T(8,128)(2,1)S(1)} %copy-done.2, bf16[512,256]{1,0:T(8,128)(2,1)S(1)} %convolution_convert_fusion.8.maps_ref, ...), custom_call_target="tpu_custom_call" | custom-call | flops 1000000 | bytes 10000 | tf_op jit(solution)/shard_map/pallas_call | solution.py:421
  404.1 6.0 all-to-all-start.14
  421.6 5.5 all-to-all-done.14
  442.0 6.5 all-to-all-done.15
  470.2 8.3 %all-to-all-done.16 = bf16[8,64,1024]{2,1,0:T(8,128)(2,1)} async-done(((bf16[8,64,1024]{2,1,0:T(8,128)(2,1)}), bf16[8,64,1024]{2,1,0:T(8,128)(2,1)}, u32[]{:S(2)}, u32[]{:S(2)}) %all-to-all-start.16) | async-done | bytes 1048608 | tf_op jit(solution)/shard_map/all_to_all | solution.py:89
  495.1 6.3 all-to-all-done.17
  533.0 7.2 %all-to-all-start.19 = ((bf16[8,64,1024]{2,1,0:T(8,128)(2,1)}), bf16[8,64,1024]{2,1,0:T(8,128)(2,1)}, u32[]{:S(2)}, u32[]{:S(2)}) async-start(bf16[8,64,1024]{2,1,0:T(8,128)(2,1)} %bitcast.459), calls=%async_computation.20 | async-start | bytes 2097152 | tf_op jit(solution)/shard_map/all_to_all | solution.py:1062
  541.1 12.2 %shard_map.339 = (f32[512,384]{1,0:T(8,128)S(1)}, bf16[512,384]{1,0:T(8,128)(2,1)S(1)}, f32[8,384]{1,0:T(8,128)S(1)}, f32[8,128]{1,0:T(8,128)S(1)}) custom-call(s32[1]{0:T(128)} %bitcast.1.core_ref, bf16[512,256]{1,0:T(8,128)(2,1)S(1)} %convolution_convert_fusion.11.near_ref.also_ref, bf16[512,256]{1,0:T(8,128)(2,1)S(1)} %convolution_convert_fusion.10.maps_ref, ...), custom_call_target="tpu_custom_call" | custom-call | flops 1000000 | bytes 10000 | tf_op jit(solution)/shard_map/pallas_call | solution.py:421
  571.1 5.2 all-to-all-start.20
  585.1 8.2 %all-to-all-done.20 = bf16[8,64,1024]{2,1,0:T(8,128)(2,1)S(1)} async-done(((bf16[8,64,1024]{2,1,0:T(8,128)(2,1)}), bf16[8,64,1024]{2,1,0:T(8,128)(2,1)S(1)}, u32[]{:S(2)}, u32[]{:S(2)}) %all-to-all-start.20) | async-done | bytes 1048608 | tf_op jit(solution)/shard_map/all_to_all | solution.py:89
  593.3 9.0 %all-to-all-start.21 = ((bf16[128,16,768]{2,1,0:T(8,128)(2,1)}), bf16[128,16,768]{2,1,0:T(8,128)(2,1)}, u32[]{:S(2)}, u32[]{:S(2)}) async-start(bf16[128,16,768]{2,1,0:T(8,128)(2,1)} %fusion.10), calls=%async_computation.22 | async-start | bytes 6291456 | tf_op jit(solution)/shard_map/all_to_all | solution.py:977
  610.5 34.0 %collective-permute-done.18 = bf16[64,1024]{1,0:T(8,128)(2,1)S(1)} collective-permute-done((bf16[64,1024]{1,0:T(8,128)(2,1)S(1)}, bf16[64,1024]{1,0:T(8,128)(2,1)S(1)}, u32[]{:S(2)}, u32[]{:S(2)}) %collective-permute-start.18) | collective-permute-done | bytes 131104 | tf_op jit(solution)/shard_map/ppermute | solution.py:69
  663.5 11.9 %all-to-all-done.22 = bf16[4,16,12416]{2,1,0:T(8,128)(2,1)S(1)} async-done(((bf16[4,16,12416]{2,1,0:T(8,128)(2,1)}), bf16[4,16,12416]{2,1,0:T(8,128)(2,1)S(1)}, u32[]{:S(2)}, u32[]{:S(2)}) %all-to-all-start.22) | async-done | bytes 1589280 | tf_op jit(solution)/shard_map/all_to_all | solution.py:986
  (864 shorter events, 360.0 us)
Async XLA Ops:
  8.6 20.8 %collective-permute-start.3 = (f32[168]{0:T(256)S(1)}, f32[168]{0:T(256)S(1)}, u32[]{:S(2)}, u32[]{:S(2)}) collective-permute-start(f32[168]{0:T(256)S(1)} %pad_maximum_fusion.68), channel_id=1, source_target_pairs={{0,64},{64,0},{1,65},{65,1},{2,66},{66,2},{3,67},{67,3},{4,68},{68... | collective-permute-start | bytes 2024 | tf_op jit(solution)/shard_map/ppermute | solution.py:69
  19.4 36.1 %all-to-all-start.1 = ((bf16[32,64,512]{2,1,0:T(8,128)(2,1)}), bf16[32,64,512]{2,1,0:T(8,128)(2,1)}, u32[]{:S(2)}, u32[]{:S(2)}) async-start(bf16[32,64,512]{2,1,0:T(8,128)(2,1)} %shard_map.330), calls=%async_computation.1 | async-start | bytes 4194304 | tf_op jit(solution)/shard_map/all_to_all | solution.py:854
  56.7 20.5 %all-to-all-start = ((bf16[8,64,1024]{2,1,0:T(8,128)(2,1)}), bf16[8,64,1024]{2,1,0:T(8,128)(2,1)S(1)}, u32[]{:S(2)}, u32[]{:S(2)}) async-start(bf16[8,64,1024]{2,1,0:T(8,128)(2,1)} %broadcast_in_dim.78), calls=%async_computation | async-start | bytes 2097152 | tf_op jit(solution)/shard_map/all_to_all | solution.py:84
  60.3 22.2 %collective-permute-start = (bf16[2,1024,512]{2,1,0:T(8,128)(2,1)}, bf16[2,1024,512]{2,1,0:T(8,128)(2,1)}, u32[]{:S(2)}, u32[]{:S(2)}) collective-permute-start(bf16[2,1024,512]{2,1,0:T(8,128)(2,1)} %bitcast.10), channel_id=1, source_target_pairs={{0,1},{1,0},{2,3},{3,2},{4,5},{5,4},{6,7},{7,6},{8,9},{9,8},{10,11... | collective-permute-start | bytes 6291464 | tf_op jit(solution)/shard_map/ppermute | solution.py:65
  70.1 22.9 %collective-permute-start.6 = (bf16[256,1024]{1,0:T(8,128)(2,1)}, bf16[256,1024]{1,0:T(8,128)(2,1)}, u32[]{:S(2)}, u32[]{:S(2)}) collective-permute-start(bf16[256,1024]{1,0:T(8,128)(2,1)} %maximum_add_fusion.3), channel_id=1, source_target_pairs={{0,64},{64,0},{1,65},{65,1},{2,66},{66,2},{3,67},{67,3},{4,68},{68... | collective-permute-start | bytes 1572872 | tf_op jit(solution)/shard_map/ppermute | solution.py:69
  77.1 22.7 %all-to-all-start.2 = ((bf16[32,64,256]{2,1,0:T(8,128)(2,1)}), bf16[32,64,256]{2,1,0:T(8,128)(2,1)}, u32[]{:S(2)}, u32[]{:S(2)}) async-start(bf16[32,64,256]{2,1,0:T(8,128)(2,1)} %shard_map.332), calls=%async_computation.2 | async-start | bytes 2097152 | tf_op jit(solution)/shard_map/all_to_all | solution.py:862
  94.2 29.2 %collective-permute-start.7 = (bf16[2,256,1024]{2,1,0:T(8,128)(2,1)S(1)}, bf16[2,256,1024]{2,1,0:T(8,128)(2,1)}, u32[]{:S(2)}, u32[]{:S(2)}) collective-permute-start(bf16[2,256,1024]{2,1,0:T(8,128)(2,1)S(1)} %maximum_select_fusion), channel_id=1, source_target_pairs={{0,1},{1,0},{2,3},{3,2},{4,5},{5,4},{6,7},{7,6},{8,9},{9,8},{10,11... | collective-permute-start | bytes 3145736 | tf_op jit(solution)/shard_map/ppermute | solution.py:65
  148.2 17.1 %all-to-all-start.5 = ((bf16[8,64,1024]{2,1,0:T(8,128)(2,1)}), bf16[8,64,1024]{2,1,0:T(8,128)(2,1)S(1)}, u32[]{:S(2)}, u32[]{:S(2)}) async-start(bf16[8,64,1024]{2,1,0:T(8,128)(2,1)} %broadcast_in_dim.87), calls=%async_computation.5 | async-start | bytes 2097152 | tf_op jit(solution)/shard_map/all_to_all | solution.py:84
  189.9 17.4 %all-to-all-start.7 = ((bf16[8,64,1024]{2,1,0:T(8,128)(2,1)}), bf16[8,64,1024]{2,1,0:T(8,128)(2,1)S(1)}, u32[]{:S(2)}, u32[]{:S(2)}) async-start(bf16[8,64,1024]{2,1,0:T(8,128)(2,1)} %broadcast_in_dim.88), calls=%async_computation.7 | async-start | bytes 2097152 | tf_op jit(solution)/shard_map/all_to_all | solution.py:84
  232.9 51.4 %all-gather.3.cloned.1.call-start = ((), (), s32[]{:S(2)}) async-start(), calls=%async_computation.25 | async-start | bytes 1179648 | tf_op jit(solution)/shard_map/all_gather | solution.py:562
  244.8 41.3 %all-to-all-start.9 = ((bf16[8,64,1024]{2,1,0:T(8,128)(2,1)}), bf16[8,64,1024]{2,1,0:T(8,128)(2,1)}, u32[]{:S(2)}, u32[]{:S(2)}) async-start(bf16[8,64,1024]{2,1,0:T(8,128)(2,1)} %bitcast.460), calls=%async_computation.9 | async-start | bytes 2097152 | tf_op jit(solution)/shard_map/all_to_all | solution.py:89
  333.0 20.6 %all-to-all-start.12 = ((bf16[8,64,1024]{2,1,0:T(8,128)(2,1)}), bf16[8,64,1024]{2,1,0:T(8,128)(2,1)}, u32[]{:S(2)}, u32[]{:S(2)}) async-start(bf16[8,64,1024]{2,1,0:T(8,128)(2,1)} %broadcast_in_dim.94), calls=%async_computation.13 | async-start | bytes 2097152 | tf_op jit(solution)/shard_map/all_to_all | solution.py:84
  337.3 58.6 %reduce-scatter.2.cloned.1.call-start = ((), (), s32[]{:S(2)}) async-start(), calls=%async_computation.24 | async-start | bytes 1179648 | tf_op jit(solution)/shard_map/reduce_scatter | solution.py:566
  404.1 23.0 %all-to-all-start.14 = ((bf16[8,64,1024]{2,1,0:T(8,128)(2,1)}), bf16[8,64,1024]{2,1,0:T(8,128)(2,1)S(1)}, u32[]{:S(2)}, u32[]{:S(2)}) async-start(bf16[8,64,1024]{2,1,0:T(8,128)(2,1)} %bitcast.477), calls=%async_computation.15 | async-start | bytes 2097152 | tf_op jit(solution)/shard_map/all_to_all | solution.py:89
  429.8 18.8 %all-to-all-start.15 = ((bf16[8,64,1024]{2,1,0:T(8,128)(2,1)}), bf16[8,64,1024]{2,1,0:T(8,128)(2,1)S(1)}, u32[]{:S(2)}, u32[]{:S(2)}) async-start(bf16[8,64,1024]{2,1,0:T(8,128)(2,1)} %broadcast_in_dim.96), calls=%async_computation.16 | async-start | bytes 2097152 | tf_op jit(solution)/shard_map/all_to_all | solution.py:84
  442.0 46.2 %collective-permute-start.16 = (bf16[256,1024]{1,0:T(8,128)(2,1)}, bf16[256,1024]{1,0:T(8,128)(2,1)}, u32[]{:S(2)}, u32[]{:S(2)}) collective-permute-start(bf16[256,1024]{1,0:T(8,128)(2,1)} %pad_maximum_fusion.18), channel_id=1, source_target_pairs={{0,1},{1,0},{2,3},{3,2},{4,5},{5,4},{6,7},{7,6},{8,9},{9,8},{10,11... | collective-permute-start | bytes 1572872 | tf_op jit(solution)/shard_map/ppermute | solution.py:65
  456.1 22.4 %all-to-all-start.16 = ((bf16[8,64,1024]{2,1,0:T(8,128)(2,1)}), bf16[8,64,1024]{2,1,0:T(8,128)(2,1)}, u32[]{:S(2)}, u32[]{:S(2)}) async-start(bf16[8,64,1024]{2,1,0:T(8,128)(2,1)} %bitcast.462), calls=%async_computation.17 | async-start | bytes 2097152 | tf_op jit(solution)/shard_map/all_to_all | solution.py:89
  461.1 29.4 %collective-permute-start.22 = (bf16[1024,512]{1,0:T(8,128)(2,1)}, bf16[1024,512]{1,0:T(8,128)(2,1)}, u32[]{:S(2)}, u32[]{:S(2)}) collective-permute-start(bf16[1024,512]{1,0:T(8,128)(2,1)} %copy-done.216), channel_id=1, source_target_pairs={{0,1},{1,0},{2,3},{3,2},{4,5},{5,4},{6,7},{7,6},{8,9},{9,8},{10,11... | collective-permute-start | bytes 3145736 | tf_op jit(solution)/shard_map/ppermute | solution.py:65
  481.7 19.7 %all-to-all-start.17 = ((bf16[8,64,1024]{2,1,0:T(8,128)(2,1)}), bf16[8,64,1024]{2,1,0:T(8,128)(2,1)S(1)}, u32[]{:S(2)}, u32[]{:S(2)}) async-start(bf16[8,64,1024]{2,1,0:T(8,128)(2,1)} %broadcast_in_dim.97), calls=%async_computation.18 | async-start | bytes 2097152 | tf_op jit(solution)/shard_map/all_to_all | solution.py:84
  533.0 26.8 %all-to-all-start.19 = ((bf16[8,64,1024]{2,1,0:T(8,128)(2,1)}), bf16[8,64,1024]{2,1,0:T(8,128)(2,1)}, u32[]{:S(2)}, u32[]{:S(2)}) async-start(bf16[8,64,1024]{2,1,0:T(8,128)(2,1)} %bitcast.459), calls=%async_computation.20 | async-start | bytes 2097152 | tf_op jit(solution)/shard_map/all_to_all | solution.py:1062
  571.1 22.2 %all-to-all-start.20 = ((bf16[8,64,1024]{2,1,0:T(8,128)(2,1)}), bf16[8,64,1024]{2,1,0:T(8,128)(2,1)S(1)}, u32[]{:S(2)}, u32[]{:S(2)}) async-start(bf16[8,64,1024]{2,1,0:T(8,128)(2,1)} %bitcast.478), calls=%async_computation.21 | async-start | bytes 2097152 | tf_op jit(solution)/shard_map/all_to_all | solution.py:89
  593.3 52.1 %all-to-all-start.21 = ((bf16[128,16,768]{2,1,0:T(8,128)(2,1)}), bf16[128,16,768]{2,1,0:T(8,128)(2,1)}, u32[]{:S(2)}, u32[]{:S(2)}) async-start(bf16[128,16,768]{2,1,0:T(8,128)(2,1)} %fusion.10), calls=%async_computation.22 | async-start | bytes 6291456 | tf_op jit(solution)/shard_map/all_to_all | solution.py:977
  604.3 40.2 %collective-permute-start.18 = (bf16[64,1024]{1,0:T(8,128)(2,1)S(1)}, bf16[64,1024]{1,0:T(8,128)(2,1)S(1)}, u32[]{:S(2)}, u32[]{:S(2)}) collective-permute-start(bf16[64,1024]{1,0:T(8,128)(2,1)S(1)} %get-tuple-element.137), channel_id=1, source_target_pairs={{0,64},{64,0},{1,65},{65,1},{2,66},{66,2},{3,67},{67,3},{4,68},{68... | collective-permute-start | bytes 393224 | tf_op jit(solution)/shard_map/ppermute | solution.py:69
  650.5 24.9 %all-to-all-start.22 = ((bf16[4,16,12416]{2,1,0:T(8,128)(2,1)}), bf16[4,16,12416]{2,1,0:T(8,128)(2,1)S(1)}, u32[]{:S(2)}, u32[]{:S(2)}) async-start(bf16[4,16,12416]{2,1,0:T(8,128)(2,1)} %broadcast_in_dim.204), calls=%async_computation.23 | async-start | bytes 3178496 | tf_op jit(solution)/shard_map/all_to_all | solution.py:986
  (243 other events, 1650.6 us)
Sparse Core Ops, SparseCore 0:
  235.3 48.8 all-gather.2
  340.5 42.3 reduce-scatter.1
